TPU v7x, 512 devices: a whole 4x8x8 slice. The times are simulated.
512 devices in a mesh: grp: 16 (over y, core), wide: 32 (over z, x).
Axes of the slice: x: 4, y: 8, z: 8, core: 2. Of those that a mesh axis runs over, the one named last changes fastest.
Arguments:
- three_center: float32 [64, 1280, 256], P(None, 'wide'), may hold values from -0.6 to 0.6
- counts: int32 [32], replicated, may hold values from 1 to 40, 1024 in all
- occ_energy: float32 [64], replicated, may hold values from -2 to -0.5
- virt_energy: float32 [256], replicated, may hold values from 0.5 to 3
- match_tables: int32 [2, 16, 32], P(None, 'grp'), may hold values from 0 to 31, as said below
Outputs:
- gradient: float32 [64, 1024, 256], P('wide', 'grp')
Inputs may be any that keep to these rules, and one draw needn't show every extreme that they name: counts sum to 1024; the largest is 40. Each row match_tables[k, g, :] is a perfect matching of the 32 blocks: no block is its own partner, and the partner of the partner is the block itself.
All inputs are finite; a program needn't handle non-finite values.
Results may differ from a plain program's by a relative error of at most 0.0003.
Values sent between devices are 32-bit elements; how exact they have to be, the bound alone decides.
No kernel may reach another device: no remote copies, remote signals or barrier semaphores. Data moves between devices by JAX's collectives and lax.ppermute only.
A program may use at most 64 MiB of HBM per device.

v0:
```python
import jax
import jax.numpy as jnp
from jax import lax
from jax.sharding import PartitionSpec as P

NAUX = 1024
OCC_DEV = 2
MATCH = 2


def pair_term(own_block, partner_block, own_energy, partner_energy, virt_energy):
    highest = lax.Precision.HIGHEST
    coulomb = jnp.einsum(
        "ipa,jpb->ijab",
        own_block,
        partner_block,
        precision=highest,
        preferred_element_type=jnp.float32,
    )
    denom = (
        own_energy[:, None, None, None]
        + partner_energy[None, :, None, None]
        - virt_energy[None, None, :, None]
        - virt_energy[None, None, None, :]
    )
    amplitude = coulomb / denom
    combined = 2.0 * amplitude - jnp.swapaxes(amplitude, 2, 3)
    return jnp.einsum(
        "ijab,jpb->ipa",
        combined,
        partner_block,
        precision=highest,
        preferred_element_type=jnp.float32,
    )


def compact_rows(padded, counts, capacity, along):
    breadth = counts.shape[0]
    offsets = jnp.cumsum(counts) - counts
    aux_rows = jnp.arange(NAUX, dtype=jnp.int32)
    source = jnp.sum((offsets[None, :] <= aux_rows[:, None]).astype(jnp.int32), axis=1) - 1
    slots = jnp.arange(breadth, dtype=jnp.int32)
    starts = jnp.sum(jnp.where(slots[None, :] == source[:, None], offsets[None, :], 0), axis=1)
    gather_index = source * capacity + aux_rows - starts
    return jnp.take(padded, gather_index, axis=along)


def fetch_partner(block, partner_row, breadth):
    occupied, aux_count, virtual = block.shape
    pieces = block.reshape(occupied, breadth, aux_count // breadth, virtual)
    spread_out = lax.all_to_all(pieces, "wide", split_axis=1, concat_axis=1, tiled=True)
    routed = jnp.take(spread_out, partner_row, axis=1)
    arrived = lax.all_to_all(routed, "wide", split_axis=1, concat_axis=1, tiled=True)
    return arrived.reshape(occupied, aux_count, virtual)


def per_device(three_center, counts, occ_energy, virt_energy, match_tables):
    breadth = lax.axis_size("wide")
    groups = lax.axis_size("grp")
    position = lax.axis_index("wide")
    capacity = three_center.shape[1]
    live = (jnp.arange(capacity, dtype=jnp.int32) < counts[position]).astype(jnp.float32)
    masked = three_center * live[None, :, None]
    tables = match_tables[:, 0, :]
    own_energy = lax.dynamic_slice_in_dim(occ_energy, position * OCC_DEV, OCC_DEV)
    own_block = lax.all_to_all(masked, "wide", split_axis=0, concat_axis=1, tiled=True)
    own_block = compact_rows(own_block, counts, capacity, 1)
    gradient = pair_term(own_block, own_block, own_energy, own_energy, virt_energy) / groups
    for match_id in range(MATCH):
        partner_id = tables[match_id, position]
        partner_block = fetch_partner(own_block, tables[match_id], breadth)
        partner_energy = lax.dynamic_slice_in_dim(occ_energy, partner_id * OCC_DEV, OCC_DEV)
        gradient = gradient + pair_term(
            own_block, partner_block, own_energy, partner_energy, virt_energy
        )
    return lax.psum_scatter(gradient, "grp", scatter_dimension=1, tiled=True)


def solution(mesh):
    placed = (P(None, "wide", None), P(), P(), P(), P(None, "grp", None))
    return jax.shard_map(
        per_device, mesh=mesh, in_specs=placed, out_specs=P("wide", "grp", None), check_vma=False
    )
```

profile of v0, /device:TPU:1, one launch (start us, length us, event | category | flops | bytes accessed | tf_op | source)
XLA Modules:
  0.0 370.1 jit_solution(9019219717877178924)
XLA Ops:
  6.5 1.2 dynamic_slice.18
  7.8 0.6 compare_convert_fusion
  8.4 3.5 broadcast_multiply_fusion
  11.9 0.0 copy-start.11
  11.9 13.8 %all-to-all-start = ((f32[64,40,256]{2,1,0:T(8,128)}), f32[64,40,256]{2,1,0:T(8,128)S(1)}, u32[]{:S(2)}, u32[]{:S(2)}) async-start(f32[64,40,256]{2,1,0:T(8,128)} %broadcast_multiply_fusion), calls=%async_computation | async-start | bytes 5242880 | tf_op jit(solution)/shard_map/all_to_all | solution.py:66
  25.8 0.0 copy-done.11
  25.8 0.1 copy.74
  25.9 0.1 reduce-window.9
  25.9 0.1 reduce
  26.0 0.1 convert_reduce_fusion
  26.2 0.1 select_reduce_fusion
  26.3 0.1 reduce_sum.25
  26.3 0.1 mul.61
  26.4 59.1 %all-to-all-done = f32[64,40,256]{2,1,0:T(8,128)S(1)} async-done(((f32[64,40,256]{2,1,0:T(8,128)}), f32[64,40,256]{2,1,0:T(8,128)S(1)}, u32[]{:S(2)}, u32[]{:S(2)}) %all-to-all-start) | async-done | bytes 2621472 | tf_op jit(solution)/shard_map/all_to_all | solution.py:66
  85.5 0.2 copy.75
  85.7 8.4 %copy.76 = f32[2,1280,256]{2,0,1:T(2,128)} copy(f32[2,1280,256]{2,1,0:T(8,128)S(1)} %bitcast.126) | data formatting | bytes 5242880 | tf_op jit(solution)/shard_map/all_to_all | solution.py:66
  94.1 5.9 %gather_fusion = f32[1024,2,256]{2,1,0:T(2,128)S(1)} fusion(f32[2,1280,256]{2,0,1:T(2,128)} %copy.76, s32[1024]{0:T(1024)S(1)} %broadcast_clamp_fusion), kind=kCustom, calls=%fused_computation.2 | custom fusion | bytes 4198400 | tf_op jit(solution)/shard_map/jit(_take)/gather | solution.py:45
  100.0 1.6 copy_select_fusion
  101.6 7.0 %all-to-all-start.1 = ((f32[2,32,32,256]{3,2,0,1:T(8,128)}), f32[2,32,32,256]{3,2,0,1:T(8,128)}, u32[]{:S(2)}, u32[]{:S(2)}) async-start(f32[2,32,32,256]{3,2,0,1:T(8,128)} %copy_select_fusion), calls=%async_computation.1 | async-start | bytes 4194304 | tf_op jit(solution)/shard_map/all_to_all | solution.py:51
  108.7 0.0 copy-done.9
  108.7 47.7 %all-to-all-done.1 = f32[2,32,32,256]{3,2,0,1:T(8,128)} async-done(((f32[2,32,32,256]{3,2,0,1:T(8,128)}), f32[2,32,32,256]{3,2,0,1:T(8,128)}, u32[]{:S(2)}, u32[]{:S(2)}) %all-to-all-start.1) | async-done | bytes 2097184 | tf_op jit(solution)/shard_map/all_to_all | solution.py:51
  156.4 3.2 copy.83
  159.6 3.6 gather_fusion.1
  163.2 3.1 select_bitcast_fusion.1
  166.4 6.9 %all-to-all-start.2 = ((f32[2,32,32,256]{3,2,0,1:T(8,128)}), f32[2,32,32,256]{3,2,0,1:T(8,128)}, u32[]{:S(2)}, u32[]{:S(2)}) async-start(f32[2,32,32,256]{3,2,0,1:T(8,128)} %select_bitcast_fusion.1), calls=%async_computation.2 | async-start | bytes 4194304 | tf_op jit(solution)/shard_map/all_to_all | solution.py:53
  173.3 3.6 gather_fusion.2
  176.9 3.1 select_bitcast_fusion
  180.1 39.3 %all-to-all-done.2 = f32[2,32,32,256]{3,2,0,1:T(8,128)} async-done(((f32[2,32,32,256]{3,2,0,1:T(8,128)}), f32[2,32,32,256]{3,2,0,1:T(8,128)}, u32[]{:S(2)}, u32[]{:S(2)}) %all-to-all-start.2) | async-done | bytes 2097184 | tf_op jit(solution)/shard_map/all_to_all | solution.py:53
  219.4 7.6 %all-to-all-start.3 = ((f32[2,32,32,256]{3,2,0,1:T(8,128)}), f32[2,32,32,256]{3,2,0,1:T(8,128)}, u32[]{:S(2)}, u32[]{:S(2)}) async-start(f32[2,32,32,256]{3,2,0,1:T(8,128)} %select_bitcast_fusion), calls=%async_computation.3 | async-start | bytes 4194304 | tf_op jit(solution)/shard_map/all_to_all | solution.py:53
  227.0 0.0 reduce-scatter.2.cloned.1.call-start
  227.1 0.6 constant_dynamic-slice_fusion.1
  228.9 0.0 copy-done.8
  228.9 0.1 fusion.54
  229.0 0.1 broadcast_add_fusion.3
  229.0 0.0 copy-done.10
  229.1 0.1 broadcast_subtract_fusion.2
  229.1 3.7 bitcast_select_fusion
  232.8 0.0 copy-start
  232.8 3.9 %fusion.59 = f32[2,1024,256,1]{2,0,1,3:T(2,128)S(1)} fusion(f32[1024,2,256]{2,1,0:T(2,128)S(1)} %gather_fusion, pred[1024]{0:T(1024)(128)(4,1)S(1)} %compare_and_fusion.1), kind=kLoop, calls=%fused_computation.91 | loop fusion | flops 524288 | bytes 4195328 | tf_op jit(solution)/shard_map/jit(_take)/select_n | solution.py:45
  236.7 0.0 copy-done
  236.7 3.5 fusion.3
  240.2 1.4 copy.79
  241.6 1.9 copy.84
  243.5 0.0 copy-start.2
  243.5 1.3 copy-done.2
  244.8 0.0 copy-done.1
  244.8 4.6 %fusion.5 = f32[2,256,2,256]{3,1,2,0:T(8,128)} fusion(f32[2,1024,256,1]{2,1,3,0:T(8,128)S(1)} %bitcast.127, f32[2,1024,256]{2,0,1:T(2,128)S(1)} %copy-done.1), kind=kOutput, calls=%fused_computation.11 | convolution fusion | flops 3221225472 | bytes 5242880 | tf_op jit(solution)/shard_map/ipa,jpb->ijab/dot_general | solution.py:13
  249.4 23.5 %all-to-all-done.3 = f32[2,32,32,256]{3,2,0,1:T(8,128)} async-done(((f32[2,32,32,256]{3,2,0,1:T(8,128)}), f32[2,32,32,256]{3,2,0,1:T(8,128)}, u32[]{:S(2)}, u32[]{:S(2)}) %all-to-all-start.3) | async-done | bytes 2097184 | tf_op jit(solution)/shard_map/all_to_all | solution.py:53
  272.9 1.7 copy.90
  274.6 0.0 copy-start.4
  274.6 1.3 copy-done.4
  275.9 4.6 %fusion.8 = f32[2,256,2,256]{3,1,2,0:T(8,128)} fusion(f32[2,1024,256,1]{2,1,3,0:T(8,128)S(1)} %bitcast.129, f32[2,1024,256]{2,0,1:T(2,128)S(1)} %copy-done.1), kind=kOutput, calls=%fused_computation.14 | convolution fusion | flops 3221225472 | bytes 5242880 | tf_op jit(solution)/shard_map/ipa,jpb->ijab/dot_general | solution.py:13
  280.6 2.6 copy.93
  283.1 2.6 copy.87
  285.7 6.3 %fusion.17 = f32[1024,2,256,1]{2,0,1,3:T(8,128)S(1)} fusion(f32[2,1024,256,1]{2,1,3,0:T(8,128)} %bitcast.130, f32[2,256,2,256]{3,1,2,0:T(8,128)} %fusion.8, f32[2,256,2,256]{1,3,2,0:T(8,128)} %copy.93, f32[2,2,256]{2,0,1:T(2,128)S(1)} %get-tuple-element.14, f32[256]{0:T(256)S(1)} %copy-done.10), kind=kOutput, calls=%fused_computation.27 | convolution fusion | flops 3222798336 | bytes 6296576 | tf_op jit(solution)/shard_map/ijab,jpb->ipa/dot_general | solution.py:28
  292.1 0.0 copy-done.3
  292.1 0.0 copy-done.5
  292.1 0.0 copy-done.7
  292.1 0.0 copy-start.6
  292.1 3.8 %fusion.22 = f32[1024,2,256,1]{2,0,1,3:T(8,128)S(1)} fusion(f32[2,1024,256,1]{2,1,3,0:T(8,128)S(1)} %bitcast.128, f32[2,256,2,256]{3,1,2,0:T(8,128)S(1)} %copy-done.5, f32[2,256,2,256]{1,3,2,0:T(8,128)S(1)} %copy-done.7, f32[2,2,256]{2,0,1:T(2,128)S(1)} %get-tuple-element.13, f32[256]{0:T(256)S(1)} %copy-done.10), kind=kOutput, calls=%fused_computation.32 | convolution fusion | flops 3222798336 | bytes 6296576 | tf_op jit(solution)/shard_map/ijab,jpb->ipa/dot_general | solution.py:28
  295.9 0.0 copy-done.6
  295.9 5.3 %fusion = f32[2,1024,256]{2,1,0:T(8,128)} fusion(f32[1024,2,256,1]{2,0,1,3:T(8,128)S(1)} %fusion.17, f32[1024,2,256,1]{2,0,1,3:T(8,128)S(1)} %fusion.22, f32[2,1024,256]{2,0,1:T(2,128)S(1)} %copy-done.1, f32[2,256,2,256]{3,1,2,0:T(8,128)S(1)} %fusion.3, f32[2,256,2,256]{1,3,2,0:T(8,128)S(1)} %copy-done.6, f32[256]{0:T(256)S(1)} %copy-done.10, ...), kind=kOutput, calls=%fused_computation.4 | convolution fusion | flops 3224371200 | bytes 10490880 | tf_op jit(solution)/shard_map/ijab,jpb->ipa/dot_general | solution.py:28
  301.3 0.0 reduce-scatter.2.cloned.1.call-update
  301.3 61.9 %reduce-scatter.2.cloned.1.call-done = f32[2,64,256]{2,1,0:T(8,128)} async-done(((f32[2,1024,256]{2,1,0:T(8,128)}), f32[2,64,256]{2,1,0:T(8,128)}) %reduce-scatter.2.cloned.1.call-update) | async-done | bytes 131088 | tf_op jit(solution)/shard_map/reduce_scatter | solution.py:76
  (16 shorter events, 0.1 us)
Async XLA Ops:
  11.9 13.9 %copy-start.11 = (s32[32]{0:T(128)S(1)}, s32[32]{0:T(128)}, u32[]{:S(2)}) copy-start(s32[32]{0:T(128)} %param.8) | copy-start | bytes 388
  11.9 73.6 %all-to-all-start = ((f32[64,40,256]{2,1,0:T(8,128)}), f32[64,40,256]{2,1,0:T(8,128)S(1)}, u32[]{:S(2)}, u32[]{:S(2)}) async-start(f32[64,40,256]{2,1,0:T(8,128)} %broadcast_multiply_fusion), calls=%async_computation | async-start | bytes 5242880 | tf_op jit(solution)/shard_map/all_to_all | solution.py:66
  101.6 7.0 %copy-start.9 = (s32[2,1,32]{2,1,0:T(1,128)S(1)}, s32[2,1,32]{2,1,0:T(1,128)}, u32[]{:S(2)}) copy-start(s32[2,1,32]{2,1,0:T(1,128)} %param.11) | copy-start | bytes 772
  101.6 54.8 %all-to-all-start.1 = ((f32[2,32,32,256]{3,2,0,1:T(8,128)}), f32[2,32,32,256]{3,2,0,1:T(8,128)}, u32[]{:S(2)}, u32[]{:S(2)}) async-start(f32[2,32,32,256]{3,2,0,1:T(8,128)} %copy_select_fusion), calls=%async_computation.1 | async-start | bytes 4194304 | tf_op jit(solution)/shard_map/all_to_all | solution.py:51
  166.4 53.0 %all-to-all-start.2 = ((f32[2,32,32,256]{3,2,0,1:T(8,128)}), f32[2,32,32,256]{3,2,0,1:T(8,128)}, u32[]{:S(2)}, u32[]{:S(2)}) async-start(f32[2,32,32,256]{3,2,0,1:T(8,128)} %select_bitcast_fusion.1), calls=%async_computation.2 | async-start | bytes 4194304 | tf_op jit(solution)/shard_map/all_to_all | solution.py:53
  180.1 48.8 %copy-start.8 = (f32[64]{0:T(128)S(1)}, f32[64]{0:T(128)}, u32[]{:S(2)}) copy-start(f32[64]{0:T(128)} %param.9) | copy-start | bytes 772
  180.1 49.0 %copy-start.10 = (f32[256]{0:T(256)S(1)}, f32[256]{0:T(256)}, u32[]{:S(2)}) copy-start(f32[256]{0:T(256)} %param.10) | copy-start | bytes 3076
  219.4 53.5 %all-to-all-start.3 = ((f32[2,32,32,256]{3,2,0,1:T(8,128)}), f32[2,32,32,256]{3,2,0,1:T(8,128)}, u32[]{:S(2)}, u32[]{:S(2)}) async-start(f32[2,32,32,256]{3,2,0,1:T(8,128)} %select_bitcast_fusion), calls=%async_computation.3 | async-start | bytes 4194304 | tf_op jit(solution)/shard_map/all_to_all | solution.py:53
  227.0 136.2 %reduce-scatter.2.cloned.1.call-start = ((), (), s32[]{:S(2)}) async-start(), calls=%async_computation.5 | async-start | bytes 2228224 | tf_op jit(solution)/shard_map/reduce_scatter | solution.py:76
  232.8 3.9 %copy-start = (f32[2,1024,256]{2,0,1:T(2,128)}, f32[2,1024,256]{2,0,1:T(2,128)S(1)}, u32[]{:S(2)}) copy-start(f32[2,1024,256]{2,0,1:T(2,128)S(1)} %bitcast_select_fusion) | copy-start | bytes 6291460
  241.6 3.2 copy-start.1
  243.5 1.3 copy-start.2
  274.6 1.3 copy-start.4
  285.7 6.4 %copy-start.3 = (f32[2,32,32,256]{3,2,1,0:T(8,128)S(1)}, f32[2,32,32,256]{3,2,1,0:T(8,128)}, u32[]{:S(2)}) copy-start(f32[2,32,32,256]{3,2,1,0:T(8,128)} %copy-done.2) | copy-start | bytes 6291460
  285.7 6.4 %copy-start.5 = (f32[2,256,2,256]{3,1,2,0:T(8,128)S(1)}, f32[2,256,2,256]{3,1,2,0:T(8,128)}, u32[]{:S(2)}) copy-start(f32[2,256,2,256]{3,1,2,0:T(8,128)} %fusion.5) | copy-start | bytes 3145732
  285.7 6.4 %copy-start.7 = (f32[2,256,2,256]{1,3,2,0:T(8,128)S(1)}, f32[2,256,2,256]{1,3,2,0:T(8,128)}, u32[]{:S(2)}) copy-start(f32[2,256,2,256]{1,3,2,0:T(8,128)} %copy.87) | copy-start | bytes 3145732
  292.1 3.8 %copy-start.6 = (f32[2,256,2,256]{1,3,2,0:T(8,128)S(1)}, f32[2,256,2,256]{1,3,2,0:T(8,128)}, u32[]{:S(2)}) copy-start(f32[2,256,2,256]{1,3,2,0:T(8,128)} %copy.79) | copy-start | bytes 3145732
Sparse Core Ops, SparseCore 0:
  301.4 61.7 reduce-scatter.1
where the time goes:
time: 372 us; the launch traced here: 370 us
  waiting for transfers between devices  231 us (62%)
  local copies, waits for them, and re-layouts  39.9 us (11%)
  starting transfers between devices  35.5 us (10%)
  matrix products  28.2 us (8%)
  other arithmetic  20.1 us (5%)
  between operations  14.9 us (4%)
    all_to_all x2, waiting for transfers between devices, fetch_partner(): lax.all_to_all(routed, 'wide', split_axis=1, concat_axis=1, tiled=True)  62.7 us
    reduce_scatter x1, waiting for transfers between devices, per_device(): return lax.psum_scatter(gradient, 'grp', scatter_dimension=1, tiled=True)  61.9 us
    all_to_all x1, waiting for transfers between devices, per_device(): lax.all_to_all(masked, 'wide', split_axis=0, concat_axis=1, tiled=True)  59.1 us
    all_to_all x1, waiting for transfers between devices, fetch_partner(): lax.all_to_all(pieces, 'wide', split_axis=1, concat_axis=1, tiled=True)  47.7 us
    dot_general x3, matrix products, pair_term(): jnp.einsum('ijab,jpb->ipa', combined, partner_block, precision=highest, p...  15.5 us
    all_to_all x2, starting transfers between devices, fetch_partner(): lax.all_to_all(routed, 'wide', split_axis=1, concat_axis=1, tiled=True)  14.6 us
    all_to_all x1, starting transfers between devices, per_device(): lax.all_to_all(masked, 'wide', split_axis=0, concat_axis=1, tiled=True)  13.8 us
    dot_general x3, matrix products, pair_term(): jnp.einsum('ipa,jpb->ijab', own_block, partner_block, precision=highest,...  12.7 us
  transfers between devices with their start and end apart: 5, of which 5 were waited for; matrix products, arithmetic and copies ran while one was open for 7% of the time, Pallas kernels for 0%

commit v1 on v0

v1 whole, which is shorter than its diff:
```python
import jax
import jax.numpy as jnp
import numpy as np
from jax import lax
from jax.experimental import pallas as pl
from jax.experimental.pallas import tpu as pltpu
from jax.sharding import Mesh, PartitionSpec as P

NAUX = 1024
OCC_DEV = 2
CAP = 40
V = 256
NY, NC, NZ, NX = 8, 2, 8, 4
BLK = 64
PAD = 48
MIB = 1 << 20


def split_hi_lo(x):
    hi = x.astype(jnp.bfloat16)
    lo = (x - hi.astype(jnp.float32)).astype(jnp.bfloat16)
    return hi, lo


def dot3(ah, al, bh, bl):
    def mm(a, b):
        return lax.dot_general(a, b, (((1,), (0,)), ((), ())), preferred_element_type=jnp.float32)

    return mm(ah, bh) + mm(ah, bl) + mm(al, bh)


def put_rows(dense, off, cols, block):
    base = pl.multiple_of(off // 8 * 8, 8)
    shift = off - base
    before = lax.broadcasted_iota(jnp.int32, (8, block.shape[1]), 0) < shift
    held = dense[pl.ds(base, 8), cols]
    for k in range(CAP // 8):
        turned = pltpu.roll(block[k * 8:(k + 1) * 8, :], shift, 0)
        dense[pl.ds(base + k * 8, 8), cols] = jnp.where(before, held, turned)
        held = turned
    dense[pl.ds(base + CAP, 8), cols] = held


def own_rows_kernel(place, counts, own_ref, other_ref, hi_ref, lo_ref, dense):
    core, u = place[0], place[1]

    def put(s, off):
        g = lax.rem(s + u, 16)
        t = lax.rem(s // 16 + u // 16, 2)
        y = g // 2

        def copy(ref):
            for i in range(OCC_DEV):
                rows = ref[y, pl.ds(pl.multiple_of((t * OCC_DEV + i) * CAP, 8), CAP), :]
                put_rows(dense, off, slice(i * V, (i + 1) * V), rows)

        @pl.when(lax.rem(g, 2) == core)
        def _():
            copy(own_ref)

        @pl.when(lax.rem(g, 2) != core)
        def _():
            copy(other_ref)

        return off + counts[s]

    lax.fori_loop(0, 32, put, jnp.int32(0))

    def turn(n, carry):
        k, pair = n // 4, n % 4
        first = pl.multiple_of((4 * pair + lax.rem(core + 1 + k, 2)) * BLK, BLK)
        rows = jnp.concatenate(
            [dense[pl.ds(first, BLK), :], dense[pl.ds(first + 2 * BLK, BLK), :]], axis=0
        )
        hi, lo = split_hi_lo(rows.T)
        hi_ref[:, n * 128:(n + 1) * 128] = hi
        lo_ref[:, n * 128:(n + 1) * 128] = lo
        return carry

    for n in range(8):
        turn(n, 0)


def pair_kernel(place, counts, occ, own_hi, own_lo, own_pay, other_pay, virt, wide_ref,
                theirs_ref, mine_ref, dense, w_hi, w_lo, x_hi, x_lo):
    core, u, grp = place[0], place[1], place[2]

    def put(s, off):
        for j in range(4):
            put_rows(dense, off, slice(j * V, (j + 1) * V), wide_ref[s, j])
        return off + counts[s]

    lax.fori_loop(0, 32, put, jnp.int32(0))

    def split(n, carry):
        k, y = n // 8, lax.rem(n, 8)
        src = pl.multiple_of((2 * y + lax.rem(core + 1 + k, 2)) * BLK, BLK)
        dst = pl.multiple_of(n * BLK, BLK)
        hi, lo = split_hi_lo(dense[pl.ds(src, BLK), :])
        w_hi[pl.ds(dst, BLK), :] = hi
        w_lo[pl.ds(dst, BLK), :] = lo
        return carry

    lax.fori_loop(0, 16, split, 0)

    virt_row = jnp.broadcast_to(virt[...], (V, V))
    virt_sum = virt_row + virt_row.T
    for w in range(2):
        block = (2 * grp + w).astype(jnp.float32)
        hits = jnp.zeros((8, V), jnp.float32)
        for y in range(NY):
            for pay in (own_pay, other_pay):
                hits = hits + (pay[y, 4 * CAP:4 * CAP + 8, :] == block).astype(jnp.float32)
        times = hits[:1, :128] + hits[:1, 128:] + (u == 2 * grp + w).astype(jnp.float32)
        times = jnp.concatenate([times, times], axis=1)
        for jj in range(2):
            j = 2 * w + jj
            cols = slice(j * V, (j + 1) * V)
            coulomb = dot3(own_hi[...], own_lo[...], w_hi[:, cols], w_lo[:, cols])
            for i in range(OCC_DEV):
                c = coulomb[i * V:(i + 1) * V, :]
                scale = times / ((occ[2 * u + i] + occ[4 * grp + j]) - virt_sum)
                hi, lo = split_hi_lo((2.0 * c.T - c) * scale)
                x_hi[cols, i * V:(i + 1) * V] = hi
                x_lo[cols, i * V:(i + 1) * V] = lo

    for k, out in enumerate((theirs_ref, mine_ref)):
        for half in range(2):
            rows = slice(k * 512 + half * 256, k * 512 + half * 256 + 256)
            term = dot3(w_hi[rows, :], w_lo[rows, :], x_hi[...], x_lo[...])
            for q in range(4):
                for i in range(OCC_DEV):
                    out[half * 4 + q, i] = term[q * BLK:(q + 1) * BLK, i * V:(i + 1) * V]


def per_device(three_center, counts, occ_energy, virt_energy, match_tables):
    y, c = lax.axis_index("y"), lax.axis_index("c")
    z, x = lax.axis_index("z"), lax.axis_index("x")
    grp, pos = y * NC + c, z * NX + x
    place = jnp.stack([c, pos, grp]).astype(jnp.int32)

    wide_part = lax.dynamic_slice_in_dim(three_center, 4 * grp, 4, 0)
    wide_all = lax.all_gather(wide_part, ("z", "x"))

    axes = ("y", "c", "z", "x")
    got = []
    for t in range(2):
        to = lax.rem(grp - pos + 32, 16) + 16 * lax.rem(pos // 16 + t, 2)
        piece = lax.dynamic_slice_in_dim(three_center, OCC_DEV * to, OCC_DEV, 0)
        perm = [
            (g * 32 + s, g * 32 + (g - s) % 16 + 16 * ((s // 16 + t) % 2))
            for g in range(16) for s in range(32)
        ]
        got.append(lax.ppermute(piece, axes, perm).reshape(OCC_DEV * CAP, V))
    partners = lax.dynamic_slice_in_dim(match_tables[:, 0, :], pos, 1, 1).astype(jnp.float32)
    note = jnp.broadcast_to(jnp.repeat(partners.reshape(1, 2), 128, axis=1), (8, V))
    load = jnp.concatenate(got + [note], axis=0)
    sent = jnp.broadcast_to(load[None], (NY, 4 * CAP + 8, V))
    own_pay = lax.all_to_all(sent, "y", split_axis=0, concat_axis=0, tiled=True)
    other_pay = lax.ppermute(own_pay, "c", [(0, 1), (1, 0)])

    smem = pl.BlockSpec(memory_space=pltpu.SMEM)
    vmem = pl.BlockSpec(memory_space=pltpu.VMEM)
    own_hi, own_lo = pl.pallas_call(
        own_rows_kernel,
        out_shape=[jax.ShapeDtypeStruct((OCC_DEV * V, NAUX), jnp.bfloat16)] * 2,
        in_specs=[smem, smem, vmem, vmem],
        out_specs=[vmem, vmem],
        scratch_shapes=[pltpu.VMEM((NAUX + PAD, OCC_DEV * V), jnp.float32)],
        compiler_params=pltpu.CompilerParams(vmem_limit_bytes=24 * MIB),
        name="own_rows",
    )(place, counts, own_pay, other_pay)

    part = jax.ShapeDtypeStruct((NY, OCC_DEV, BLK, V), jnp.float32)
    theirs, mine = pl.pallas_call(
        pair_kernel,
        out_shape=[part, part],
        in_specs=[smem] * 3 + [vmem] * 6,
        out_specs=[vmem, vmem],
        scratch_shapes=[
            pltpu.VMEM((NAUX + PAD, 4 * V), jnp.float32),
            pltpu.VMEM((NAUX, 4 * V), jnp.bfloat16),
            pltpu.VMEM((NAUX, 4 * V), jnp.bfloat16),
            pltpu.VMEM((4 * V, OCC_DEV * V), jnp.bfloat16),
            pltpu.VMEM((4 * V, OCC_DEV * V), jnp.bfloat16),
        ],
        compiler_params=pltpu.CompilerParams(vmem_limit_bytes=48 * MIB),
        name="pairs",
    )(place, counts, occ_energy, own_hi, own_lo, own_pay, other_pay,
      virt_energy.reshape(1, V), wide_all)

    mine = mine + lax.ppermute(theirs, "c", [(0, 1), (1, 0)])
    pieces = lax.all_to_all(mine, "y", split_axis=0, concat_axis=0, tiled=True)
    return jnp.sum(pieces, axis=0)


def solution(mesh):
    fine = Mesh(np.asarray(mesh.devices).reshape(NY, NC, NZ, NX), ("y", "c", "z", "x"))
    wide, grp = ("z", "x"), ("y", "c")
    placed = (P(None, wide, None), P(), P(), P(), P(None, grp, None))
    return jax.shard_map(
        per_device, mesh=fine, in_specs=placed, out_specs=P(wide, grp, None), check_vma=False
    )
```

time: 372 us -> 169 us (0.45)
  waiting for transfers between devices: 231 us -> 29.5 us
  blocking collectives: 0 us -> 77.6 us
  local copies, waits for them, and re-layouts: 39.9 us -> 7.19 us
  matrix products: 28.2 us -> 0 us
  other arithmetic: 20.1 us -> 1.81 us
  Pallas kernels: 0 us -> 14.7 us
  starting transfers between devices: 35.5 us -> 23.8 us
    all_to_all x4 -> x0, waiting for transfers between devices: 170 us -> none  [the longest x2 62.7 us: fetch_partner(): lax.all_to_all(routed, 'wide', split_axis=1, concat_axis=1, tiled=True)]
    all_to_all x0 -> x2, blocking collectives: none -> 77.6 us  [the longest x1 43.4 us: per_device(): own_pay = lax.all_to_all(sent, 'y', split_axis=0, concat_axis=0, tiled=True)]
    reduce_scatter x1 -> x0, waiting for transfers between devices: 61.9 us -> none  [per_device(): return lax.psum_scatter(gradient, 'grp', scatter_dimension=1, tiled=True)]
    all_to_all x4 -> x0, starting transfers between devices: 35.5 us -> none  [the longest x2 14.6 us: fetch_partner(): lax.all_to_all(routed, 'wide', split_axis=1, concat_axis=1, tiled=True)]
    dot_general x6 -> x0, matrix products: 28.2 us -> none  [the longest x3 15.5 us: pair_term(): jnp.einsum('ijab,jpb->ipa', combined, partner_block, precision=highest, p...]
    ppermute x0 -> x4, starting transfers between devices: none -> 23.8 us  [the longest x2 14.6 us: per_device(): got.append(lax.ppermute(piece, axes, perm).reshape(OCC_DEV * CAP, V))]
    all_gather x0 -> x1, waiting for transfers between devices: none -> 23.4 us  [per_device(): wide_all = lax.all_gather(wide_part, ('z', 'x'))]
    select_n x6 -> x0, other arithmetic: 15.4 us -> none  [the longest x4 9.15 us: compact_rows(): return jnp.take(padded, gather_index, axis=along)]
  transfers between devices with their start and end apart: 5 -> 5, of which waited for: 5 -> 4; matrix products, arithmetic and copies ran while one was open for 7% -> 1% of each run, Pallas kernels for 0% -> 2%
where the time goes in v1:
time: 169 us; the launch traced here: 168 us
  blocking collectives  77.6 us (46%)
  waiting for transfers between devices  29.5 us (17%)
  starting transfers between devices  23.8 us (14%)
  Pallas kernels  14.7 us (9%)
  between operations  13.5 us (8%)
  local copies, waits for them, and re-layouts  7.19 us (4%)
  other arithmetic  1.81 us (1%)
    all_to_all x1, blocking collectives, per_device(): own_pay = lax.all_to_all(sent, 'y', split_axis=0, concat_axis=0, tiled=True)  43.4 us
    all_to_all x1, blocking collectives, per_device(): pieces = lax.all_to_all(mine, 'y', split_axis=0, concat_axis=0, tiled=True)  34.2 us
    all_gather x1, waiting for transfers between devices, per_device(): wide_all = lax.all_gather(wide_part, ('z', 'x'))  23.4 us
    ppermute x2, starting transfers between devices, per_device(): got.append(lax.ppermute(piece, axes, perm).reshape(OCC_DEV * CAP, V))  14.6 us
    pallas_call x1, Pallas kernels, per_device(): pl.pallas_call(pair_kernel, out_shape=[part, part], in_specs=[smem] * 3 +...  11.8 us
    ppermute x1, starting transfers between devices, per_device(): mine = mine + lax.ppermute(theirs, 'c', [(0, 1), (1, 0)])  4.67 us
    ppermute x1, starting transfers between devices, per_device(): other_pay = lax.ppermute(own_pay, 'c', [(0, 1), (1, 0)])  4.61 us
    unnamed x16, local copies, waits for them, and re-layouts  4.49 us
  transfers between devices with their start and end apart: 5, of which 4 were waited for; matrix products, arithmetic and copies ran while one was open for 1% of the time, Pallas kernels for 2%

profile of v1, /device:TPU:1, one launch (start us, length us, event | category | flops | bytes accessed | tf_op | source)
XLA Modules:
  0.0 168.1 jit_solution(4819557208358617818)
XLA Ops:
  6.5 0.0 all-gather.3.cloned.1.call-start
  6.5 1.6 constant_dynamic-slice_fusion
  8.1 0.0 copy-start.5
  8.1 0.0 all-gather.3.cloned.1.call-update
  8.2 0.9 constant_dynamic-slice_fusion.2
  9.2 3.9 %collective-permute-start = (f32[2,40,256]{2,1,0:T(8,128)S(1)}, f32[2,40,256]{2,1,0:T(8,128)S(1)}, u32[]{:S(2)}, u32[]{:S(2)}) collective-permute-start(f32[2,40,256]{2,1,0:T(8,128)S(1)} %get-tuple-element.13), channel_id=1, source_target_pairs={{0,0},{1,15},{2,14},{3,13},{4,12},{5,11},{6,10},{7,9},{8,8},{9,7},... | collective-permute-start | bytes 245768 | tf_op jit(solution)/shard_map/ppermute | solution.py:154
  13.1 10.6 %collective-permute-start.1 = (f32[2,40,256]{2,1,0:T(8,128)S(1)}, f32[2,40,256]{2,1,0:T(8,128)S(1)}, u32[]{:S(2)}, u32[]{:S(2)}) collective-permute-start(f32[2,40,256]{2,1,0:T(8,128)S(1)} %get-tuple-element.14), channel_id=1, source_target_pairs={{0,16},{1,31},{2,30},{3,29},{4,28},{5,27},{6,26},{7,25},{8,24},{9,... | collective-permute-start | bytes 245768 | tf_op jit(solution)/shard_map/ppermute | solution.py:154
  23.7 0.9 convert_reduce_fusion
  24.6 0.1 broadcast_bitcast_fusion
  24.7 0.0 collective-permute-done
  24.7 1.2 collective-permute-done.1
  25.8 0.1 broadcast_in_dim.19
  25.9 0.0 copy-start.6
  26.0 0.0 copy-start.7
  26.0 43.4 %all_to_all.10.own_ref.own_pay = f32[8,168,256]{2,1,0:T(8,128)S(1)} all-to-all(f32[8,168,256]{2,1,0:T(8,128)S(1)} %broadcast_in_dim.19), channel_id=1, replica_groups=mesh['y'=8,'c'=2,'z'=8,'x'=4] {'y'}, dimensions={0} | all-to-all | bytes 2752512 | tf_op jit(solution)/shard_map/all_to_all | solution.py:159
  69.4 4.6 %collective-permute-start.2 = (f32[8,168,256]{2,1,0:T(8,128)S(1)}, f32[8,168,256]{2,1,0:T(8,128)S(1)}, u32[]{:S(2)}, u32[]{:S(2)}) collective-permute-start(f32[8,168,256]{2,1,0:T(8,128)S(1)} %all_to_all.10.own_ref.own_pay), channel_id=1, source_target_pairs={{0,32},{32,0},{1,33},{33,1},{2,34},{34,2},{3,35},{35,3},{4,36},{36... | collective-permute-start | bytes 4128776 | tf_op jit(solution)/shard_map/ppermute | solution.py:160
  74.0 0.1 pad_add_fusion.place
  74.1 2.7 %collective-permute-done.2.other_ref.other_pay = f32[8,168,256]{2,1,0:T(8,128)S(1)} collective-permute-done((f32[8,168,256]{2,1,0:T(8,128)S(1)}, f32[8,168,256]{2,1,0:T(8,128)S(1)}, u32[]{:S(2)}, u32[]{:S(2)}) %collective-permute-start.2) | collective-permute-done | bytes 1376288 | tf_op jit(solution)/shard_map/ppermute | solution.py:160
  76.7 0.0 copy-done.5
  76.7 0.0 copy-start
  76.7 2.9 %own_rows.1 = (bf16[512,1024]{1,0:T(8,128)(2,1)S(1)}, bf16[512,1024]{1,0:T(8,128)(2,1)S(1)}) custom-call(s32[3]{0:T(128)S(1)} %pad_add_fusion.place, s32[32]{0:T(128)S(1)} %copy-done.5, f32[8,168,256]{2,1,0:T(8,128)S(1)} %all_to_all.10.own_ref.own_pay, f32[8,168,256]{2,1,0:T(8,128)S(1)} %collective-permute-done.2.other_ref.other_pay), custom_call_target="tpu_custom_call" | custom-call | tf_op jit(solution)/shard_map/own_rows/pallas_call | solution.py:164
  79.6 0.0 copy-start.1
  79.7 1.0 copy-done.1
  80.6 0.0 copy-start.3
  80.6 1.1 copy-done.3
  81.7 23.4 %all-gather.3.cloned.1.call-done = f32[128,40,256]{2,1,0:T(8,128)} async-done(((f32[4,40,256]{2,1,0:T(8,128)}), f32[128,40,256]{2,1,0:T(8,128)}) %all-gather.3.cloned.1.call-update) | async-done | bytes 5242896 | tf_op jit(solution)/shard_map/all_gather | solution.py:143
  105.1 0.0 copy-done
  105.1 0.0 copy-done.6
  105.1 0.0 copy-done.7
  105.1 0.0 copy-start.2
  105.1 1.2 copy-done.2
  106.3 0.0 copy-start.4
  106.3 1.2 copy-done.4
  107.5 11.8 %pairs.1 = (f32[8,2,64,256]{3,2,1,0:T(8,128)S(1)}, f32[8,2,64,256]{3,2,1,0:T(8,128)S(1)}) custom-call(s32[3]{0:T(128)S(1)} %pad_add_fusion.place, s32[32]{0:T(128)S(1)} %copy-done.5, f32[64]{0:T(128)S(1)} %copy-done.7, bf16[512,1024]{1,0:T(8,128)(2,1)S(1)} %copy-done.2, bf16[512,1024]{1,0:T(8,128)(2,1)S(1)} %copy-done.4, ...), custom_call_target="tpu_custom_call" | custom-call | tf_op jit(solution)/shard_map/pairs/pallas_call | solution.py:175
  119.3 4.7 %collective-permute-start.3 = (f32[8,2,64,256]{3,2,1,0:T(8,128)S(1)}, f32[8,2,64,256]{3,2,1,0:T(8,128)S(1)}, u32[]{:S(2)}, u32[]{:S(2)}) collective-permute-start(f32[8,2,64,256]{3,2,1,0:T(8,128)S(1)} %get-tuple-element.12), channel_id=1, source_target_pairs={{0,32},{32,0},{1,33},{33,1},{2,34},{34,2},{3,35},{35,3},{4,36},{36... | collective-permute-start | bytes 3145736 | tf_op jit(solution)/shard_map/ppermute | solution.py:192
  124.0 2.3 %collective-permute-done.3 = f32[8,2,64,256]{3,2,1,0:T(8,128)S(1)} collective-permute-done((f32[8,2,64,256]{3,2,1,0:T(8,128)S(1)}, f32[8,2,64,256]{3,2,1,0:T(8,128)S(1)}, u32[]{:S(2)}, u32[]{:S(2)}) %collective-permute-start.3) | collective-permute-done | bytes 1048608 | tf_op jit(solution)/shard_map/ppermute | solution.py:192
  126.2 0.1 add.45
  126.4 34.2 %all_to_all.11 = f32[8,2,64,256]{3,2,1,0:T(8,128)S(1)} all-to-all(f32[8,2,64,256]{3,2,1,0:T(8,128)S(1)} %add.45), channel_id=1, replica_groups=mesh['y'=8,'c'=2,'z'=8,'x'=4] {'y'}, dimensions={0} | all-to-all | bytes 2097152 | tf_op jit(solution)/shard_map/all_to_all | solution.py:193
  160.5 0.7 reduce_sum.9
  (2 shorter events, 0.0 us)
Async XLA Ops:
  6.5 98.5 %all-gather.3.cloned.1.call-start = ((), (), s32[]{:S(2)}) async-start(), calls=%async_computation.2 | async-start | bytes 5406720 | tf_op jit(solution)/shard_map/all_gather | solution.py:143
  8.1 68.6 %copy-start.5 = (s32[32]{0:T(128)S(1)}, s32[32]{0:T(128)}, u32[]{:S(2)}) copy-start(s32[32]{0:T(128)} %counts.3) | copy-start | bytes 388
  9.2 15.5 %collective-permute-start = (f32[2,40,256]{2,1,0:T(8,128)S(1)}, f32[2,40,256]{2,1,0:T(8,128)S(1)}, u32[]{:S(2)}, u32[]{:S(2)}) collective-permute-start(f32[2,40,256]{2,1,0:T(8,128)S(1)} %get-tuple-element.13), channel_id=1, source_target_pairs={{0,0},{1,15},{2,14},{3,13},{4,12},{5,11},{6,10},{7,9},{8,8},{9,7},... | collective-permute-start | bytes 245768 | tf_op jit(solution)/shard_map/ppermute | solution.py:154
  13.1 12.7 %collective-permute-start.1 = (f32[2,40,256]{2,1,0:T(8,128)S(1)}, f32[2,40,256]{2,1,0:T(8,128)S(1)}, u32[]{:S(2)}, u32[]{:S(2)}) collective-permute-start(f32[2,40,256]{2,1,0:T(8,128)S(1)} %get-tuple-element.14), channel_id=1, source_target_pairs={{0,16},{1,31},{2,30},{3,29},{4,28},{5,27},{6,26},{7,25},{8,24},{9,... | collective-permute-start | bytes 245768 | tf_op jit(solution)/shard_map/ppermute | solution.py:154
  25.9 79.1 %copy-start.6 = (f32[256]{0:T(256)S(1)}, f32[256]{0:T(256)}, u32[]{:S(2)}) copy-start(f32[256]{0:T(256)} %param.8) | copy-start | bytes 3076
  26.0 79.1 %copy-start.7 = (f32[64]{0:T(128)S(1)}, f32[64]{0:T(128)}, u32[]{:S(2)}) copy-start(f32[64]{0:T(128)} %occ.1) | copy-start | bytes 772
  69.4 7.4 %collective-permute-start.2 = (f32[8,168,256]{2,1,0:T(8,128)S(1)}, f32[8,168,256]{2,1,0:T(8,128)S(1)}, u32[]{:S(2)}, u32[]{:S(2)}) collective-permute-start(f32[8,168,256]{2,1,0:T(8,128)S(1)} %all_to_all.10.own_ref.own_pay), channel_id=1, source_target_pairs={{0,32},{32,0},{1,33},{33,1},{2,34},{34,2},{3,35},{35,3},{4,36},{36... | collective-permute-start | bytes 4128776 | tf_op jit(solution)/shard_map/ppermute | solution.py:160
  76.7 28.3 %copy-start = (f32[8,168,256]{2,1,0:T(8,128)}, f32[8,168,256]{2,1,0:T(8,128)S(1)}, u32[]{:S(2)}) copy-start(f32[8,168,256]{2,1,0:T(8,128)S(1)} %collective-permute-done.2.other_ref.other_pay) | copy-start | bytes 4128772
  79.6 1.0 copy-start.1
  80.6 1.1 copy-start.3
  105.1 1.2 copy-start.2
  106.3 1.2 copy-start.4
  119.3 6.9 %collective-permute-start.3 = (f32[8,2,64,256]{3,2,1,0:T(8,128)S(1)}, f32[8,2,64,256]{3,2,1,0:T(8,128)S(1)}, u32[]{:S(2)}, u32[]{:S(2)}) collective-permute-start(f32[8,2,64,256]{3,2,1,0:T(8,128)S(1)} %get-tuple-element.12), channel_id=1, source_target_pairs={{0,32},{32,0},{1,33},{33,1},{2,34},{34,2},{3,35},{35,3},{4,36},{36... | collective-permute-start | bytes 3145736 | tf_op jit(solution)/shard_map/ppermute | solution.py:192
Sparse Core Ops, SparseCore 0:
  10.5 94.4 all-gather.2

commit v2 on v1

v2 whole, which is shorter than its diff:
```python
import functools

import jax
import jax.numpy as jnp
import numpy as np
from jax import lax
from jax.experimental import pallas as pl
from jax.experimental.pallas import tpu as pltpu
from jax.sharding import Mesh, PartitionSpec as P

NAUX = 1024
OCC_DEV = 2
CAP = 40
V = 256
NY, NC, NZ, NX = 8, 2, 8, 4
BLK = 64
PAD = 48
MIB = 1 << 20


def split_hi_lo(x):
    hi = x.astype(jnp.bfloat16)
    lo = (x - hi.astype(jnp.float32)).astype(jnp.bfloat16)
    return hi, lo


def dot3(ah, al, bh, bl):
    def mm(a, b):
        return lax.dot_general(a, b, (((1,), (0,)), ((), ())), preferred_element_type=jnp.float32)

    return mm(ah, bh) + mm(ah, bl) + mm(al, bh)


def put_rows(dense, off, cols, block):
    base = pl.multiple_of(off // 8 * 8, 8)
    shift = off - base
    before = lax.broadcasted_iota(jnp.int32, (8, block.shape[1]), 0) < shift
    held = dense[pl.ds(base, 8), cols]
    for k in range(CAP // 8):
        turned = pltpu.roll(block[k * 8:(k + 1) * 8, :], shift, 0)
        dense[pl.ds(base + k * 8, 8), cols] = jnp.where(before, held, turned)
        held = turned
    dense[pl.ds(base + CAP, 8), cols] = held


def own_rows_kernel(place, counts, own_ref, other_ref, hi_out, lo_out, dense, hi_ref, lo_ref, sems):
    core, u = place[0], place[1]

    def put(s, off):
        g = lax.rem(s + u, 16)
        t = lax.rem(s // 16 + u // 16, 2)
        y = g // 2

        def copy(ref):
            for i in range(OCC_DEV):
                rows = ref[y, pl.ds(pl.multiple_of((t * OCC_DEV + i) * CAP, 8), CAP), :]
                put_rows(dense, off, slice(i * V, (i + 1) * V), rows)

        @pl.when(lax.rem(g, 2) == core)
        def _():
            copy(own_ref)

        @pl.when(lax.rem(g, 2) != core)
        def _():
            copy(other_ref)

        return off + counts[s]

    lax.fori_loop(0, 32, put, jnp.int32(0))

    def turn(n, carry):
        k, pair = n // 4, n % 4
        first = pl.multiple_of((4 * pair + lax.rem(core + 1 + k, 2)) * BLK, BLK)
        rows = jnp.concatenate(
            [dense[pl.ds(first, BLK), :], dense[pl.ds(first + 2 * BLK, BLK), :]], axis=0
        )
        hi, lo = split_hi_lo(rows.T)
        hi_ref[:, n * 128:(n + 1) * 128] = hi
        lo_ref[:, n * 128:(n + 1) * 128] = lo
        return carry

    for n in range(8):
        turn(n, 0)
    copies = [
        pltpu.make_async_copy(hi_ref, hi_out, sems.at[0]),
        pltpu.make_async_copy(lo_ref, lo_out, sems.at[1]),
    ]
    for copy in copies:
        copy.start()
    for copy in copies:
        copy.wait()


def block_kernel(first, place, counts, occ, own_hi_any, own_lo_any, own_pay, other_pay, virt, *refs):
    n_wide = 1 if first else 9
    wide, refs = refs[:n_wide], refs[n_wide:]
    before, refs = ((), refs) if first else (refs[:2], refs[2:])
    outs, (own_hi, own_lo, rows, dense, w_hi, w_lo, x_hi, x_lo, sems) = refs[:2], refs[2:]
    core, u, grp, z_here = place[0], place[1], place[2], place[3]

    own_copies = [
        pltpu.make_async_copy(own_hi_any, own_hi, sems.at[0]),
        pltpu.make_async_copy(own_lo_any, own_lo, sems.at[1]),
    ]
    if first:
        row_copies = [
            pltpu.make_async_copy(wide[0].at[k], rows.at[k], sems.at[2 + k]) for k in range(NZ)
        ]
    else:
        steps = (0, -1, -2, -3, 1, 2, 3)
        row_copies = [
            pltpu.make_async_copy(wide[k], rows.at[lax.rem(z_here + d + NZ, NZ)], sems.at[2 + k])
            for k, d in enumerate(steps)
        ]
        z_far = lax.rem(z_here + 4, NZ)
        row_copies += [
            pltpu.make_async_copy(wide[7 + i], rows.at[z_far, :, pl.ds(i, 1)], sems.at[9 + i])
            for i in range(2)
        ]
    for copy in row_copies + own_copies:
        copy.start()
    if not first:
        for copy in row_copies:
            copy.wait()

    off = jnp.int32(0)
    for z in range(NZ):
        if first:
            row_copies[z].wait()

        def put(k, off):
            for j in range(OCC_DEV):
                put_rows(dense, off, slice(j * V, (j + 1) * V), rows[z, k, j])
            return off + counts[z * NX + k]

        off = lax.fori_loop(0, NX, put, off)

    def split(n, carry):
        k, y = n // 8, lax.rem(n, 8)
        src = pl.multiple_of((2 * y + lax.rem(core + 1 + k, 2)) * BLK, BLK)
        dst = pl.multiple_of(n * BLK, BLK)
        hi, lo = split_hi_lo(dense[pl.ds(src, BLK), :])
        w_hi[pl.ds(dst, BLK), :] = hi
        w_lo[pl.ds(dst, BLK), :] = lo
        return carry

    lax.fori_loop(0, 16, split, 0)

    virt_row = jnp.broadcast_to(virt[...], (V, V))
    virt_sum = virt_row + virt_row.T
    w = 2 * grp + (0 if first else 1)
    hits = jnp.zeros((8, V), jnp.float32)
    for y in range(NY):
        for pay in (own_pay, other_pay):
            hits = hits + (pay[y, 4 * CAP:4 * CAP + 8, :] == w.astype(jnp.float32)).astype(jnp.float32)
    times = hits[:1, :128] + hits[:1, 128:] + (u == w).astype(jnp.float32)
    times = jnp.concatenate([times, times], axis=1)
    for copy in own_copies:
        copy.wait()
    for j in range(OCC_DEV):
        cols = slice(j * V, (j + 1) * V)
        coulomb = dot3(own_hi[...], own_lo[...], w_hi[:, cols], w_lo[:, cols])
        for i in range(OCC_DEV):
            c = coulomb[i * V:(i + 1) * V, :]
            scale = times / ((occ[2 * u + i] + occ[2 * w + j]) - virt_sum)
            hi, lo = split_hi_lo((2.0 * c.T - c) * scale)
            x_hi[cols, i * V:(i + 1) * V] = hi
            x_lo[cols, i * V:(i + 1) * V] = lo

    for k, out in enumerate(outs):
        for half in range(2):
            part = slice(k * 512 + half * 256, k * 512 + half * 256 + 256)
            term = dot3(w_hi[part, :], w_lo[part, :], x_hi[...], x_lo[...])
            for q in range(4):
                for i in range(OCC_DEV):
                    value = term[q * BLK:(q + 1) * BLK, i * V:(i + 1) * V]
                    if not first:
                        value = value + before[k][half * 4 + q, i]
                    out[half * 4 + q, i] = value


def per_device(three_center, counts, occ_energy, virt_energy, match_tables):
    y, c = lax.axis_index("y"), lax.axis_index("c")
    z, x = lax.axis_index("z"), lax.axis_index("x")
    grp, pos = y * NC + c, z * NX + x
    place = jnp.stack([c, pos, grp, z]).astype(jnp.int32)

    axes = ("y", "c", "z", "x")
    got = []
    for t in range(2):
        to = lax.rem(grp - pos + 32, 16) + 16 * lax.rem(pos // 16 + t, 2)
        piece = lax.dynamic_slice_in_dim(three_center, OCC_DEV * to, OCC_DEV, 0)
        perm = [
            (g * 32 + s, g * 32 + (g - s) % 16 + 16 * ((s // 16 + t) % 2))
            for g in range(16) for s in range(32)
        ]
        got.append(lax.ppermute(piece, axes, perm).reshape(OCC_DEV * CAP, V))

    both = lax.dynamic_slice_in_dim(three_center, 4 * grp, 4, 0).reshape(2, OCC_DEV, CAP, V)
    both = lax.all_gather(both, "x", axis=1)
    first_rows = lax.all_gather(both[0], "z")

    partners = lax.dynamic_slice_in_dim(match_tables[:, 0, :], pos, 1, 1).astype(jnp.float32)
    note = jnp.broadcast_to(jnp.repeat(partners.reshape(1, 2), 128, axis=1), (8, V))
    load = jnp.concatenate(got + [note], axis=0)
    sent = jnp.broadcast_to(load[None], (NY, 4 * CAP + 8, V))
    own_pay = lax.all_to_all(sent, "y", split_axis=0, concat_axis=0, tiled=True)

    def along_z(a, d):
        return lax.ppermute(a, "z", [(k, (k + d) % NZ) for k in range(NZ)])

    up, down = [both[1]], [both[1]]
    for step in range(3):
        up.append(along_z(up[-1], 1))
        down.append(along_z(down[-1], -1))
        if step == 1:
            own_pay, up[2], down[2] = lax.optimization_barrier((own_pay, up[2], down[2]))
    far = (along_z(up[3][:, :1], 1), along_z(down[3][:, 1:], -1))
    second_rows = (*up, *down[1:], *far)

    other_pay = lax.ppermute(own_pay, "c", [(0, 1), (1, 0)])

    smem = pl.BlockSpec(memory_space=pltpu.SMEM)
    vmem = pl.BlockSpec(memory_space=pltpu.VMEM)
    hbm = pl.BlockSpec(memory_space=pltpu.HBM)
    own_hi, own_lo = pl.pallas_call(
        own_rows_kernel,
        out_shape=[jax.ShapeDtypeStruct((OCC_DEV * V, NAUX), jnp.bfloat16)] * 2,
        in_specs=[smem, smem, vmem, vmem],
        out_specs=[hbm, hbm],
        scratch_shapes=[
            pltpu.VMEM((NAUX + PAD, OCC_DEV * V), jnp.float32),
            pltpu.VMEM((OCC_DEV * V, NAUX), jnp.bfloat16),
            pltpu.VMEM((OCC_DEV * V, NAUX), jnp.bfloat16),
            pltpu.SemaphoreType.DMA((2,)),
        ],
        compiler_params=pltpu.CompilerParams(vmem_limit_bytes=60 * MIB),
        name="own_rows",
    )(place, counts, own_pay, other_pay)

    part = jax.ShapeDtypeStruct((NY, OCC_DEV, BLK, V), jnp.float32)
    outs = ()
    for first, wide in ((True, (first_rows,)), (False, second_rows)):
        wide_dims = 2 * V
        outs = pl.pallas_call(
            functools.partial(block_kernel, first),
            out_shape=[part, part],
            in_specs=[smem] * 3 + [hbm] * 2 + [vmem] * 3 + [hbm] * len(wide) + [vmem] * len(outs),
            out_specs=[vmem, vmem],
            scratch_shapes=[
                pltpu.VMEM((OCC_DEV * V, NAUX), jnp.bfloat16),
                pltpu.VMEM((OCC_DEV * V, NAUX), jnp.bfloat16),
                pltpu.VMEM((NZ, NX, OCC_DEV, CAP, V), jnp.float32),
                pltpu.VMEM((NAUX + PAD, wide_dims), jnp.float32),
                pltpu.VMEM((NAUX, wide_dims), jnp.bfloat16),
                pltpu.VMEM((NAUX, wide_dims), jnp.bfloat16),
                pltpu.VMEM((wide_dims, OCC_DEV * V), jnp.bfloat16),
                pltpu.VMEM((wide_dims, OCC_DEV * V), jnp.bfloat16),
                pltpu.SemaphoreType.DMA((12,)),
            ],
            compiler_params=pltpu.CompilerParams(vmem_limit_bytes=60 * MIB),
            cost_estimate=pl.CostEstimate(flops=6 * 2 * 512 * 512 * 1024, bytes_accessed=8 * MIB, transcendentals=0),
            name="first_block" if first else "second_block",
        )(place, counts, occ_energy, own_hi, own_lo, own_pay, other_pay,
          virt_energy.reshape(1, V), *wide, *outs)
    theirs, mine = outs

    mine = mine + lax.ppermute(theirs, "c", [(0, 1), (1, 0)])
    pieces = lax.all_to_all(mine, "y", split_axis=0, concat_axis=0, tiled=True)
    return jnp.sum(pieces, axis=0)


def solution(mesh):
    fine = Mesh(np.asarray(mesh.devices).reshape(NY, NC, NZ, NX), ("y", "c", "z", "x"))
    wide, grp = ("z", "x"), ("y", "c")
    placed = (P(None, wide, None), P(), P(), P(), P(None, grp, None))
    return jax.shard_map(
        per_device, mesh=fine, in_specs=placed, out_specs=P(wide, grp, None), check_vma=False
    )
```

time: 169 us -> 183 us (1.083)
  starting transfers between devices: 23.8 us -> 58.3 us
  blocking collectives: 77.6 us -> 44.4 us
  Pallas kernels: 14.7 us -> 24.6 us
  waiting for transfers between devices: 29.5 us -> 32 us
  local copies, waits for them, and re-layouts: 7.19 us -> 5.13 us
    all_to_all x1 -> x0, blocking collectives: 43.4 us -> none  [per_device(): own_pay = lax.all_to_all(sent, 'y', split_axis=0, concat_axis=0, tiled=True)]
    ppermute x0 -> x8, starting transfers between devices: none -> 32.2 us  [along_z(): return lax.ppermute(a, 'z', [(k, (k + d) % NZ) for k in range(NZ)])]
    ppermute x0 -> x8, waiting for transfers between devices: none -> 24.6 us  [along_z(): return lax.ppermute(a, 'z', [(k, (k + d) % NZ) for k in range(NZ)])]
    all_gather x1, waiting for transfers between devices: 23.4 us -> 0.02 us  [per_device(): first_rows = lax.all_gather(both[0], 'z')]
    all_gather x0 -> x1, blocking collectives: none -> 11.3 us  [per_device(): both = lax.all_gather(both, 'x', axis=1)]
    pallas_call x1 -> x2, Pallas kernels: 11.8 us -> 19.1 us  [per_device(): pl.pallas_call(functools.partial(block_kernel, first), out_shape=[part, p...]
    all_to_all x0 -> x1, starting transfers between devices: none -> 3.94 us  [per_device(): own_pay = lax.all_to_all(sent, 'y', split_axis=0, concat_axis=0, tiled=True)]
    ppermute x2, waiting for transfers between devices: 1.17 us -> 4.86 us  [per_device(): got.append(lax.ppermute(piece, axes, perm).reshape(OCC_DEV * CAP, V))]
  transfers between devices with their start and end apart: 5 -> 14, of which waited for: 4 -> 5; matrix products, arithmetic and copies ran while one was open for 1% -> 2% of each run, Pallas kernels for 2% -> 8%
where the time goes in v2:
time: 183 us; the launch traced here: 181 us
  starting transfers between devices  58.3 us (32%)
  blocking collectives  44.4 us (24%)
  waiting for transfers between devices  32 us (17%)
  Pallas kernels  24.6 us (13%)
  between operations  13.7 us (7%)
  local copies, waits for them, and re-layouts  5.13 us (3%)
  other arithmetic  2.92 us (2%)
    all_to_all x1, blocking collectives, per_device(): pieces = lax.all_to_all(mine, 'y', split_axis=0, concat_axis=0, tiled=True)  33.1 us
    ppermute x8, starting transfers between devices, along_z(): return lax.ppermute(a, 'z', [(k, (k + d) % NZ) for k in range(NZ)])  32.2 us
    ppermute x8, waiting for transfers between devices, along_z(): return lax.ppermute(a, 'z', [(k, (k + d) % NZ) for k in range(NZ)])  24.6 us
    pallas_call x2, Pallas kernels, per_device(): pl.pallas_call(functools.partial(block_kernel, first), out_shape=[part, p...  19.1 us
    ppermute x2, starting transfers between devices, per_device(): got.append(lax.ppermute(piece, axes, perm).reshape(OCC_DEV * CAP, V))  15 us
    all_gather x1, blocking collectives, per_device(): both = lax.all_gather(both, 'x', axis=1)  11.3 us
    pallas_call x1, Pallas kernels, per_device(): pl.pallas_call(own_rows_kernel, out_shape=[jax.ShapeDtypeStruct((OCC_DEV...  5.49 us
    ppermute x2, waiting for transfers between devices, per_device(): got.append(lax.ppermute(piece, axes, perm).reshape(OCC_DEV * CAP, V))  4.86 us
  transfers between devices with their start and end apart: 14, of which 5 were waited for; matrix products, arithmetic and copies ran while one was open for 2% of the time, Pallas kernels for 8%

profile of v2, /device:TPU:1, one launch (start us, length us, event | category | flops | bytes accessed | tf_op | source)
XLA Modules:
  0.0 181.1 jit_solution(13025172836000571401)
XLA Ops:
  6.5 0.0 copy-start.5
  6.5 0.0 all-gather.2.cloned.1.call-start
  6.5 0.9 constant_dynamic-slice_fusion
  7.5 11.3 %all_gather.6 = f32[2,4,2,40,256]{4,3,2,1,0:T(8,128)S(1)} all-gather(f32[2,1,2,40,256]{4,3,2,1,0:T(8,128)S(1)} %bitcast.12), channel_id=1, replica_groups=mesh['y'=8,'c'=2,'z'=8,'x'=4] {'x'}, dimensions={1}, use_global_device_ids=true | all-gather | bytes 819200 | tf_op jit(solution)/shard_map/all_gather | solution.py:200
  18.8 0.8 fusion
  19.6 0.0 copy-start.2
  19.6 0.0 all-gather.2.cloned.1.call-update
  19.7 1.0 constant_dynamic-slice_fusion.2
  20.7 2.8 %collective-permute-start = (f32[2,40,256]{2,1,0:T(8,128)S(1)}, f32[2,40,256]{2,1,0:T(8,128)S(1)}, u32[]{:S(2)}, u32[]{:S(2)}) collective-permute-start(f32[2,40,256]{2,1,0:T(8,128)S(1)} %get-tuple-element.23), channel_id=1, source_target_pairs={{0,0},{1,15},{2,14},{3,13},{4,12},{5,11},{6,10},{7,9},{8,8},{9,7},... | collective-permute-start | bytes 245768 | tf_op jit(solution)/shard_map/ppermute | solution.py:197
  23.5 12.2 %collective-permute-start.1 = (f32[2,40,256]{2,1,0:T(8,128)S(1)}, f32[2,40,256]{2,1,0:T(8,128)S(1)}, u32[]{:S(2)}, u32[]{:S(2)}) collective-permute-start(f32[2,40,256]{2,1,0:T(8,128)S(1)} %get-tuple-element.24), channel_id=1, source_target_pairs={{0,16},{1,31},{2,30},{3,29},{4,28},{5,27},{6,26},{7,25},{8,24},{9,... | collective-permute-start | bytes 245768 | tf_op jit(solution)/shard_map/ppermute | solution.py:197
  35.7 0.0 copy-done.5
  35.7 0.2 convert_reduce_fusion
  35.9 0.1 broadcast_bitcast_fusion
  36.0 0.0 collective-permute-done
  36.0 4.9 %collective-permute-done.1 = f32[2,40,256]{2,1,0:T(8,128)S(1)} collective-permute-done((f32[2,40,256]{2,1,0:T(8,128)S(1)}, f32[2,40,256]{2,1,0:T(8,128)S(1)}, u32[]{:S(2)}, u32[]{:S(2)}) %collective-permute-start.1) | collective-permute-done | bytes 81952 | tf_op jit(solution)/shard_map/ppermute | solution.py:197
  40.8 1.2 broadcast_in_dim.19
  42.0 3.9 %all-to-all-start = ((f32[8,168,256]{2,1,0:T(8,128)}), f32[8,168,256]{2,1,0:T(8,128)S(1)}, u32[]{:S(2)}, u32[]{:S(2)}) async-start(f32[8,168,256]{2,1,0:T(8,128)} %broadcast_in_dim.19), calls=%async_computation | async-start | bytes 2752512 | tf_op jit(solution)/shard_map/all_to_all | solution.py:207
  46.0 3.1 %collective-permute-start.2 = (f32[4,2,40,256]{3,2,1,0:T(8,128)S(1)}, f32[4,2,40,256]{3,2,1,0:T(8,128)S(1)}, u32[]{:S(2)}, u32[]{:S(2)}) collective-permute-start(f32[4,2,40,256]{3,2,1,0:T(8,128)S(1)} %get-tuple-element.26.refs_0_), channel_id=1, source_target_pairs={{0,4},{4,8},{8,12},{12,16},{16,20},{20,24},{24,28},{28,0},{1,5},{5... | collective-permute-start | bytes 983048 | tf_op jit(solution)/shard_map/ppermute | solution.py:210
  49.1 0.0 copy-done.2
  49.1 7.5 %collective-permute-start.4 = (f32[4,2,40,256]{3,2,1,0:T(8,128)S(1)}, f32[4,2,40,256]{3,2,1,0:T(8,128)S(1)}, u32[]{:S(2)}, u32[]{:S(2)}) collective-permute-start(f32[4,2,40,256]{3,2,1,0:T(8,128)S(1)} %get-tuple-element.26.refs_0_), channel_id=1, source_target_pairs={{0,28},{4,0},{8,4},{12,8},{16,12},{20,16},{24,20},{28,24},{1,29},{... | collective-permute-start | bytes 983048 | tf_op jit(solution)/shard_map/ppermute | solution.py:210
  56.6 11.9 %collective-permute-done.2.refs_1_ = f32[4,2,40,256]{3,2,1,0:T(8,128)S(1)} collective-permute-done((f32[4,2,40,256]{3,2,1,0:T(8,128)S(1)}, f32[4,2,40,256]{3,2,1,0:T(8,128)S(1)}, u32[]{:S(2)}, u32[]{:S(2)}) %collective-permute-start.2) | collective-permute-done | bytes 327712 | tf_op jit(solution)/shard_map/ppermute | solution.py:210
  68.5 0.0 copy-start.6
  68.5 1.9 %collective-permute-start.3 = (f32[4,2,40,256]{3,2,1,0:T(8,128)S(1)}, f32[4,2,40,256]{3,2,1,0:T(8,128)}, u32[]{:S(2)}, u32[]{:S(2)}) collective-permute-start(f32[4,2,40,256]{3,2,1,0:T(8,128)S(1)} %collective-permute-done.2.refs_1_), channel_id=1, source_target_pairs={{0,4},{4,8},{8,12},{12,16},{16,20},{20,24},{24,28},{28,0},{1,5},{5... | collective-permute-start | bytes 983048 | tf_op jit(solution)/shard_map/ppermute | solution.py:210
  70.4 0.0 collective-permute-done.4.refs_4_
  70.4 0.0 copy-start.7
  70.4 4.6 %collective-permute-start.5 = (f32[4,2,40,256]{3,2,1,0:T(8,128)S(1)}, f32[4,2,40,256]{3,2,1,0:T(8,128)S(1)}, u32[]{:S(2)}, u32[]{:S(2)}) collective-permute-start(f32[4,2,40,256]{3,2,1,0:T(8,128)S(1)} %collective-permute-done.4.refs_4_), channel_id=1, source_target_pairs={{0,28},{4,0},{8,4},{12,8},{16,12},{20,16},{24,20},{28,24},{1,29},{... | collective-permute-start | bytes 983048 | tf_op jit(solution)/shard_map/ppermute | solution.py:210
  75.0 8.2 %collective-permute-done.3.refs_2_ = f32[4,2,40,256]{3,2,1,0:T(8,128)} collective-permute-done((f32[4,2,40,256]{3,2,1,0:T(8,128)S(1)}, f32[4,2,40,256]{3,2,1,0:T(8,128)}, u32[]{:S(2)}, u32[]{:S(2)}) %collective-permute-start.3) | collective-permute-done | bytes 327712 | tf_op jit(solution)/shard_map/ppermute | solution.py:210
  83.2 0.0 copy-done.6
  83.2 0.0 copy-done.7
  83.2 0.0 collective-permute-done.5.refs_5_
  83.2 0.0 copy-start.8
  83.2 0.0 all-to-all-done.own_ref.own_pay
  83.2 0.0 copy-start
  83.3 4.1 %collective-permute-start.6 = (f32[8,168,256]{2,1,0:T(8,128)S(1)}, f32[8,168,256]{2,1,0:T(8,128)S(1)}, u32[]{:S(2)}, u32[]{:S(2)}) collective-permute-start(f32[8,168,256]{2,1,0:T(8,128)S(1)} %all-to-all-done.own_ref.own_pay), channel_id=1, source_target_pairs={{0,32},{32,0},{1,33},{33,1},{2,34},{34,2},{3,35},{35,3},{4,36},{36... | collective-permute-start | bytes 4128776 | tf_op jit(solution)/shard_map/ppermute | solution.py:221
  87.4 5.9 %collective-permute-start.8 = (f32[4,2,40,256]{3,2,1,0:T(8,128)S(1)}, f32[4,2,40,256]{3,2,1,0:T(8,128)S(1)}, u32[]{:S(2)}, u32[]{:S(2)}) collective-permute-start(f32[4,2,40,256]{3,2,1,0:T(8,128)S(1)} %collective-permute-done.5.refs_5_), channel_id=1, source_target_pairs={{0,28},{4,0},{8,4},{12,8},{16,12},{20,16},{24,20},{28,24},{1,29},{... | collective-permute-start | bytes 983048 | tf_op jit(solution)/shard_map/ppermute | solution.py:210
  93.3 1.9 %collective-permute-start.7 = (f32[4,2,40,256]{3,2,1,0:T(8,128)}, f32[4,2,40,256]{3,2,1,0:T(8,128)S(1)}, u32[]{:S(2)}, u32[]{:S(2)}) collective-permute-start(f32[4,2,40,256]{3,2,1,0:T(8,128)} %collective-permute-done.3.refs_2_), channel_id=1, source_target_pairs={{0,4},{4,8},{8,12},{12,16},{16,20},{20,24},{24,28},{28,0},{1,5},{5... | collective-permute-start | bytes 983048 | tf_op jit(solution)/shard_map/ppermute | solution.py:210
  95.2 0.7 pad_add_fusion.place
  95.9 0.0 copy-done.8
  95.9 4.5 %collective-permute-done.8.refs_6_ = f32[4,2,40,256]{3,2,1,0:T(8,128)S(1)} collective-permute-done((f32[4,2,40,256]{3,2,1,0:T(8,128)S(1)}, f32[4,2,40,256]{3,2,1,0:T(8,128)S(1)}, u32[]{:S(2)}, u32[]{:S(2)}) %collective-permute-start.8) | collective-permute-done | bytes 327712 | tf_op jit(solution)/shard_map/ppermute | solution.py:210
  100.4 0.0 copy-start.3
  100.4 5.3 %collective-permute-start.10 = (f32[4,1,40,256]{3,2,1,0:T(8,128)S(1)}, f32[4,1,40,256]{3,2,1,0:T(8,128)}, u32[]{:S(2)}, u32[]{:S(2)}) collective-permute-start(f32[4,1,40,256]{3,2,1,0:T(8,128)S(1)} %slice.19), channel_id=1, source_target_pairs={{0,28},{4,0},{8,4},{12,8},{16,12},{20,16},{24,20},{28,24},{1,29},{... | collective-permute-start | bytes 491528 | tf_op jit(solution)/shard_map/ppermute | solution.py:210
  105.8 0.0 collective-permute-done.7.refs_3_
  105.8 0.0 copy-start.4
  105.8 1.9 %collective-permute-start.9 = (f32[4,1,40,256]{3,2,1,0:T(8,128)S(1)}, f32[4,1,40,256]{3,2,1,0:T(8,128)}, u32[]{:S(2)}, u32[]{:S(2)}) collective-permute-start(f32[4,1,40,256]{3,2,1,0:T(8,128)S(1)} %slice.18), channel_id=1, source_target_pairs={{0,4},{4,8},{8,12},{12,16},{16,20},{20,24},{24,28},{28,0},{1,5},{5... | collective-permute-start | bytes 491528 | tf_op jit(solution)/shard_map/ppermute | solution.py:210
  107.7 0.0 copy-done.4
  107.8 0.0 collective-permute-done.6.other_ref.other_pay
  107.8 0.0 copy-done
  107.8 0.0 copy-start.1
  107.8 1.1 copy-done.1
  108.9 5.5 %own_rows.1 = (bf16[512,1024]{1,0:T(8,128)(2,1)}, bf16[512,1024]{1,0:T(8,128)(2,1)}) custom-call(s32[4]{0:T(128)} %pad_add_fusion.place, s32[32]{0:T(128)} %counts.5, f32[8,168,256]{2,1,0:T(8,128)} %copy-done, f32[8,168,256]{2,1,0:T(8,128)} %copy-done.1), custom_call_target="tpu_custom_call" | custom-call | tf_op jit(solution)/shard_map/own_rows/pallas_call | solution.py:226
  114.4 0.0 all-gather.2.cloned.1.call-done.refs_0_
  114.4 9.0 %first_block.1 = (f32[8,2,64,256]{3,2,1,0:T(8,128)}, f32[8,2,64,256]{3,2,1,0:T(8,128)}) custom-call(s32[4]{0:T(128)} %pad_add_fusion.place, s32[32]{0:T(128)} %counts.5, f32[64]{0:T(128)} %occ.3, bf16[512,1024]{1,0:T(8,128)(2,1)} %get-tuple-element.15.own_hi_any, bf16[512,1024]{1,0:T(8,128)(2,1)} %get-tuple-element.16.own_lo_any, f32[8,168,256]{2,1,0:T(8,128)} %copy-done, ...), custom_call_target="tpu_custom_call" | custom-call | flops 3221225472 | bytes 8388608 | tf_op jit(solution)/shard_map/first_block/pallas_call | solution.py:245
  123.4 0.0 copy-done.3
  123.4 0.0 collective-permute-done.10.refs_8_
  123.5 0.0 collective-permute-done.9.refs_7_
  123.5 10.1 %second_block.1 = (f32[8,2,64,256]{3,2,1,0:T(8,128)}, f32[8,2,64,256]{3,2,1,0:T(8,128)}) custom-call(s32[4]{0:T(128)} %pad_add_fusion.place, s32[32]{0:T(128)} %counts.5, f32[64]{0:T(128)} %occ.3, bf16[512,1024]{1,0:T(8,128)(2,1)} %get-tuple-element.15.own_hi_any, bf16[512,1024]{1,0:T(8,128)(2,1)} %get-tuple-element.16.own_lo_any, f32[8,168,256]{2,1,0:T(8,128)} %copy-done, ...), custom_call_target="tpu_custom_call" | custom-call | flops 3221225472 | bytes 8388608 | tf_op jit(solution)/shard_map/second_block/pallas_call | solution.py:245
  133.6 3.0 %collective-permute-start.11 = (f32[8,2,64,256]{3,2,1,0:T(8,128)}, f32[8,2,64,256]{3,2,1,0:T(8,128)S(1)}, u32[]{:S(2)}, u32[]{:S(2)}) collective-permute-start(f32[8,2,64,256]{3,2,1,0:T(8,128)} %get-tuple-element.22), channel_id=1, source_target_pairs={{0,32},{32,0},{1,33},{33,1},{2,34},{34,2},{3,35},{35,3},{4,36},{36... | collective-permute-start | bytes 3145736 | tf_op jit(solution)/shard_map/ppermute | solution.py:268
  136.6 2.5 %collective-permute-done.11 = f32[8,2,64,256]{3,2,1,0:T(8,128)S(1)} collective-permute-done((f32[8,2,64,256]{3,2,1,0:T(8,128)}, f32[8,2,64,256]{3,2,1,0:T(8,128)S(1)}, u32[]{:S(2)}, u32[]{:S(2)}) %collective-permute-start.11) | collective-permute-done | bytes 1048608 | tf_op jit(solution)/shard_map/ppermute | solution.py:268
  139.1 1.4 add.45
  140.4 33.1 %all_to_all.10 = f32[8,2,64,256]{3,2,1,0:T(8,128)S(1)} all-to-all(f32[8,2,64,256]{3,2,1,0:T(8,128)S(1)} %add.45), channel_id=1, replica_groups=mesh['y'=8,'c'=2,'z'=8,'x'=4] {'y'}, dimensions={0} | all-to-all | bytes 2097152 | tf_op jit(solution)/shard_map/all_to_all | solution.py:269
  173.5 0.7 reduce_sum.9
  (4 shorter events, 0.0 us)
Async XLA Ops:
  6.5 29.2 %copy-start.5 = (s32[2,1,32]{2,1,0:T(1,128)S(1)}, s32[2,1,32]{2,1,0:T(1,128)}, u32[]{:S(2)}) copy-start(s32[2,1,32]{2,1,0:T(1,128)} %param.9) | copy-start | bytes 772
  6.5 107.9 %all-gather.2.cloned.1.call-start = ((), (), s32[]{:S(2)}) async-start(), calls=%async_computation.2 | async-start | bytes 2949120 | tf_op jit(solution)/shard_map/all_gather | solution.py:201
  19.6 29.5 %copy-start.2 = (f32[4,2,40,256]{3,2,1,0:T(8,128)}, f32[4,2,40,256]{3,2,1,0:T(8,128)S(1)}, u32[]{:S(2)}) copy-start(f32[4,2,40,256]{3,2,1,0:T(8,128)S(1)} %get-tuple-element.26.refs_0_) | copy-start | bytes 983044
  20.7 15.3 %collective-permute-start = (f32[2,40,256]{2,1,0:T(8,128)S(1)}, f32[2,40,256]{2,1,0:T(8,128)S(1)}, u32[]{:S(2)}, u32[]{:S(2)}) collective-permute-start(f32[2,40,256]{2,1,0:T(8,128)S(1)} %get-tuple-element.23), channel_id=1, source_target_pairs={{0,0},{1,15},{2,14},{3,13},{4,12},{5,11},{6,10},{7,9},{8,8},{9,7},... | collective-permute-start | bytes 245768 | tf_op jit(solution)/shard_map/ppermute | solution.py:197
  23.5 17.3 %collective-permute-start.1 = (f32[2,40,256]{2,1,0:T(8,128)S(1)}, f32[2,40,256]{2,1,0:T(8,128)S(1)}, u32[]{:S(2)}, u32[]{:S(2)}) collective-permute-start(f32[2,40,256]{2,1,0:T(8,128)S(1)} %get-tuple-element.24), channel_id=1, source_target_pairs={{0,16},{1,31},{2,30},{3,29},{4,28},{5,27},{6,26},{7,25},{8,24},{9,... | collective-permute-start | bytes 245768 | tf_op jit(solution)/shard_map/ppermute | solution.py:197
  42.0 41.2 %all-to-all-start = ((f32[8,168,256]{2,1,0:T(8,128)}), f32[8,168,256]{2,1,0:T(8,128)S(1)}, u32[]{:S(2)}, u32[]{:S(2)}) async-start(f32[8,168,256]{2,1,0:T(8,128)} %broadcast_in_dim.19), calls=%async_computation | async-start | bytes 2752512 | tf_op jit(solution)/shard_map/all_to_all | solution.py:207
  46.0 22.5 %collective-permute-start.2 = (f32[4,2,40,256]{3,2,1,0:T(8,128)S(1)}, f32[4,2,40,256]{3,2,1,0:T(8,128)S(1)}, u32[]{:S(2)}, u32[]{:S(2)}) collective-permute-start(f32[4,2,40,256]{3,2,1,0:T(8,128)S(1)} %get-tuple-element.26.refs_0_), channel_id=1, source_target_pairs={{0,4},{4,8},{8,12},{12,16},{16,20},{20,24},{24,28},{28,0},{1,5},{5... | collective-permute-start | bytes 983048 | tf_op jit(solution)/shard_map/ppermute | solution.py:210
  49.1 21.4 %collective-permute-start.4 = (f32[4,2,40,256]{3,2,1,0:T(8,128)S(1)}, f32[4,2,40,256]{3,2,1,0:T(8,128)S(1)}, u32[]{:S(2)}, u32[]{:S(2)}) collective-permute-start(f32[4,2,40,256]{3,2,1,0:T(8,128)S(1)} %get-tuple-element.26.refs_0_), channel_id=1, source_target_pairs={{0,28},{4,0},{8,4},{12,8},{16,12},{20,16},{24,20},{28,24},{1,29},{... | collective-permute-start | bytes 983048 | tf_op jit(solution)/shard_map/ppermute | solution.py:210
  68.5 14.7 %copy-start.6 = (f32[4,2,40,256]{3,2,1,0:T(8,128)}, f32[4,2,40,256]{3,2,1,0:T(8,128)S(1)}, u32[]{:S(2)}) copy-start(f32[4,2,40,256]{3,2,1,0:T(8,128)S(1)} %collective-permute-done.2.refs_1_) | copy-start | bytes 983044
  68.5 14.7 %collective-permute-start.3 = (f32[4,2,40,256]{3,2,1,0:T(8,128)S(1)}, f32[4,2,40,256]{3,2,1,0:T(8,128)}, u32[]{:S(2)}, u32[]{:S(2)}) collective-permute-start(f32[4,2,40,256]{3,2,1,0:T(8,128)S(1)} %collective-permute-done.2.refs_1_), channel_id=1, source_target_pairs={{0,4},{4,8},{8,12},{12,16},{16,20},{20,24},{24,28},{28,0},{1,5},{5... | collective-permute-start | bytes 983048 | tf_op jit(solution)/shard_map/ppermute | solution.py:210
  70.4 12.8 %copy-start.7 = (f32[4,2,40,256]{3,2,1,0:T(8,128)}, f32[4,2,40,256]{3,2,1,0:T(8,128)S(1)}, u32[]{:S(2)}) copy-start(f32[4,2,40,256]{3,2,1,0:T(8,128)S(1)} %collective-permute-done.4.refs_4_) | copy-start | bytes 983044
  70.4 12.8 %collective-permute-start.5 = (f32[4,2,40,256]{3,2,1,0:T(8,128)S(1)}, f32[4,2,40,256]{3,2,1,0:T(8,128)S(1)}, u32[]{:S(2)}, u32[]{:S(2)}) collective-permute-start(f32[4,2,40,256]{3,2,1,0:T(8,128)S(1)} %collective-permute-done.4.refs_4_), channel_id=1, source_target_pairs={{0,28},{4,0},{8,4},{12,8},{16,12},{20,16},{24,20},{28,24},{1,29},{... | collective-permute-start | bytes 983048 | tf_op jit(solution)/shard_map/ppermute | solution.py:210
  83.2 12.7 %copy-start.8 = (f32[4,2,40,256]{3,2,1,0:T(8,128)}, f32[4,2,40,256]{3,2,1,0:T(8,128)S(1)}, u32[]{:S(2)}) copy-start(f32[4,2,40,256]{3,2,1,0:T(8,128)S(1)} %collective-permute-done.5.refs_5_) | copy-start | bytes 983044
  83.2 24.5 %copy-start = (f32[8,168,256]{2,1,0:T(8,128)}, f32[8,168,256]{2,1,0:T(8,128)S(1)}, u32[]{:S(2)}) copy-start(f32[8,168,256]{2,1,0:T(8,128)S(1)} %all-to-all-done.own_ref.own_pay) | copy-start | bytes 4128772
  83.3 24.5 %collective-permute-start.6 = (f32[8,168,256]{2,1,0:T(8,128)S(1)}, f32[8,168,256]{2,1,0:T(8,128)S(1)}, u32[]{:S(2)}, u32[]{:S(2)}) collective-permute-start(f32[8,168,256]{2,1,0:T(8,128)S(1)} %all-to-all-done.own_ref.own_pay), channel_id=1, source_target_pairs={{0,32},{32,0},{1,33},{33,1},{2,34},{34,2},{3,35},{35,3},{4,36},{36... | collective-permute-start | bytes 4128776 | tf_op jit(solution)/shard_map/ppermute | solution.py:221
  87.4 13.1 %collective-permute-start.8 = (f32[4,2,40,256]{3,2,1,0:T(8,128)S(1)}, f32[4,2,40,256]{3,2,1,0:T(8,128)S(1)}, u32[]{:S(2)}, u32[]{:S(2)}) collective-permute-start(f32[4,2,40,256]{3,2,1,0:T(8,128)S(1)} %collective-permute-done.5.refs_5_), channel_id=1, source_target_pairs={{0,28},{4,0},{8,4},{12,8},{16,12},{20,16},{24,20},{28,24},{1,29},{... | collective-permute-start | bytes 983048 | tf_op jit(solution)/shard_map/ppermute | solution.py:210
  93.3 12.5 %collective-permute-start.7 = (f32[4,2,40,256]{3,2,1,0:T(8,128)}, f32[4,2,40,256]{3,2,1,0:T(8,128)S(1)}, u32[]{:S(2)}, u32[]{:S(2)}) collective-permute-start(f32[4,2,40,256]{3,2,1,0:T(8,128)} %collective-permute-done.3.refs_2_), channel_id=1, source_target_pairs={{0,4},{4,8},{8,12},{12,16},{16,20},{20,24},{24,28},{28,0},{1,5},{5... | collective-permute-start | bytes 983048 | tf_op jit(solution)/shard_map/ppermute | solution.py:210
  100.4 23.0 %copy-start.3 = (f32[4,2,40,256]{3,2,1,0:T(8,128)}, f32[4,2,40,256]{3,2,1,0:T(8,128)S(1)}, u32[]{:S(2)}) copy-start(f32[4,2,40,256]{3,2,1,0:T(8,128)S(1)} %collective-permute-done.8.refs_6_) | copy-start | bytes 983044
  100.4 23.0 %collective-permute-start.10 = (f32[4,1,40,256]{3,2,1,0:T(8,128)S(1)}, f32[4,1,40,256]{3,2,1,0:T(8,128)}, u32[]{:S(2)}, u32[]{:S(2)}) collective-permute-start(f32[4,1,40,256]{3,2,1,0:T(8,128)S(1)} %slice.19), channel_id=1, source_target_pairs={{0,28},{4,0},{8,4},{12,8},{16,12},{20,16},{24,20},{28,24},{1,29},{... | collective-permute-start | bytes 491528 | tf_op jit(solution)/shard_map/ppermute | solution.py:210
  105.8 2.0 %copy-start.4 = (f32[4,2,40,256]{3,2,1,0:T(8,128)}, f32[4,2,40,256]{3,2,1,0:T(8,128)S(1)}, u32[]{:S(2)}) copy-start(f32[4,2,40,256]{3,2,1,0:T(8,128)S(1)} %collective-permute-done.7.refs_3_) | copy-start | bytes 983044
  105.8 17.6 %collective-permute-start.9 = (f32[4,1,40,256]{3,2,1,0:T(8,128)S(1)}, f32[4,1,40,256]{3,2,1,0:T(8,128)}, u32[]{:S(2)}, u32[]{:S(2)}) collective-permute-start(f32[4,1,40,256]{3,2,1,0:T(8,128)S(1)} %slice.18), channel_id=1, source_target_pairs={{0,4},{4,8},{8,12},{12,16},{16,20},{20,24},{24,28},{28,0},{1,5},{5... | collective-permute-start | bytes 491528 | tf_op jit(solution)/shard_map/ppermute | solution.py:210
  107.8 1.1 copy-start.1
  133.6 5.5 %collective-permute-start.11 = (f32[8,2,64,256]{3,2,1,0:T(8,128)}, f32[8,2,64,256]{3,2,1,0:T(8,128)S(1)}, u32[]{:S(2)}, u32[]{:S(2)}) collective-permute-start(f32[8,2,64,256]{3,2,1,0:T(8,128)} %get-tuple-element.22), channel_id=1, source_target_pairs={{0,32},{32,0},{1,33},{33,1},{2,34},{34,2},{3,35},{35,3},{4,36},{36... | collective-permute-start | bytes 3145736 | tf_op jit(solution)/shard_map/ppermute | solution.py:268
Sparse Core Ops, SparseCore 0:
  19.7 59.4 all-gather.1

commit v3 on v1

v3 whole, which is shorter than its diff:
```python
import jax
import jax.numpy as jnp
import numpy as np
from jax import lax
from jax.experimental import pallas as pl
from jax.experimental.pallas import tpu as pltpu
from jax.sharding import Mesh, PartitionSpec as P

NAUX = 1024
OCC_DEV = 2
CAP = 40
V = 256
NY, NC, NZ, NX = 8, 2, 8, 4
BLK = 64
PAD = 48
MIB = 1 << 20


def split_hi_lo(x):
    hi = x.astype(jnp.bfloat16)
    lo = (x - hi.astype(jnp.float32)).astype(jnp.bfloat16)
    return hi, lo


def dot3(ah, al, bh, bl):
    def mm(a, b):
        return lax.dot_general(a, b, (((1,), (0,)), ((), ())), preferred_element_type=jnp.float32)

    return mm(ah, bh) + mm(ah, bl) + mm(al, bh)


def put_rows(dense, off, cols, block):
    base = pl.multiple_of(off // 8 * 8, 8)
    shift = off - base
    before = lax.broadcasted_iota(jnp.int32, (8, block.shape[1]), 0) < shift
    held = dense[pl.ds(base, 8), cols]
    for k in range(CAP // 8):
        turned = pltpu.roll(block[k * 8:(k + 1) * 8, :], shift, 0)
        dense[pl.ds(base + k * 8, 8), cols] = jnp.where(before, held, turned)
        held = turned
    dense[pl.ds(base + CAP, 8), cols] = held


def own_rows_kernel(place, counts, own_ref, other_ref, hi_ref, lo_ref, times_ref, dense):
    core, u, grp = place[0], place[1], place[2]
    for w in range(2):
        block = (2 * grp + w).astype(jnp.float32)
        hits = jnp.zeros((8, V), jnp.float32)
        for y in range(NY):
            for pay in (own_ref, other_ref):
                hits = hits + (pay[y, 4 * CAP:4 * CAP + 8, :] == block).astype(jnp.float32)
        times = hits[:, :128] + hits[:, 128:] + (u == 2 * grp + w).astype(jnp.float32)
        times_ref[w] = jnp.concatenate([times, times], axis=1)

    def put(s, off):
        g = lax.rem(s + u, 16)
        t = lax.rem(s // 16 + u // 16, 2)
        y = g // 2

        def copy(ref):
            for i in range(OCC_DEV):
                rows = ref[y, pl.ds(pl.multiple_of((t * OCC_DEV + i) * CAP, 8), CAP), :]
                put_rows(dense, off, slice(i * V, (i + 1) * V), rows)

        @pl.when(lax.rem(g, 2) == core)
        def _():
            copy(own_ref)

        @pl.when(lax.rem(g, 2) != core)
        def _():
            copy(other_ref)

        return off + counts[s]

    lax.fori_loop(0, 32, put, jnp.int32(0))

    def turn(n, carry):
        k, pair = n // 4, n % 4
        first = pl.multiple_of((4 * pair + lax.rem(core + 1 + k, 2)) * BLK, BLK)
        rows = jnp.concatenate(
            [dense[pl.ds(first, BLK), :], dense[pl.ds(first + 2 * BLK, BLK), :]], axis=0
        )
        hi, lo = split_hi_lo(rows.T)
        hi_ref[:, n * 128:(n + 1) * 128] = hi
        lo_ref[:, n * 128:(n + 1) * 128] = lo
        return carry

    for n in range(8):
        turn(n, 0)


def pair_kernel(place, counts, occ, own_hi_any, own_lo_any, times, virt, wide_any,
                theirs_ref, mine_ref, own_hi, own_lo, rows, dense, w_hi, w_lo, x_hi, x_lo, sems):
    core, u, grp = place[0], place[1], place[2]
    row_copies = [pltpu.make_async_copy(wide_any.at[z], rows.at[z], sems.at[z]) for z in range(NZ)]
    own_copies = [
        pltpu.make_async_copy(own_hi_any, own_hi, sems.at[NZ]),
        pltpu.make_async_copy(own_lo_any, own_lo, sems.at[NZ + 1]),
    ]
    for copy in row_copies + own_copies:
        copy.start()

    off = jnp.int32(0)
    for z in range(NZ):
        row_copies[z].wait()
        for x in range(NX):
            for j in range(4):
                put_rows(dense, off, slice(j * V, (j + 1) * V), rows[z, x, j])
            off = off + counts[z * NX + x]

    for k in range(2):
        for y in range(NY):
            src = pl.multiple_of((2 * y + lax.rem(core + 1 + k, 2)) * BLK, BLK)
            dst = slice((k * NY + y) * BLK, (k * NY + y + 1) * BLK)
            hi, lo = split_hi_lo(dense[pl.ds(src, BLK), :])
            w_hi[dst, :] = hi
            w_lo[dst, :] = lo

    virt_row = jnp.broadcast_to(virt[...], (V, V))
    virt_sum = virt_row + virt_row.T
    for copy in own_copies:
        copy.wait()
    for j in range(4):
        cols = slice(j * V, (j + 1) * V)
        coulomb = dot3(own_hi[...], own_lo[...], w_hi[:, cols], w_lo[:, cols])
        for i in range(OCC_DEV):
            c = coulomb[i * V:(i + 1) * V, :]
            scale = times[j // 2, :1, :] / ((occ[2 * u + i] + occ[4 * grp + j]) - virt_sum)
            hi, lo = split_hi_lo((2.0 * c.T - c) * scale)
            x_hi[cols, i * V:(i + 1) * V] = hi
            x_lo[cols, i * V:(i + 1) * V] = lo

    for k, out in enumerate((theirs_ref, mine_ref)):
        for half in range(2):
            rows = slice(k * 512 + half * 256, k * 512 + half * 256 + 256)
            term = dot3(w_hi[rows, :], w_lo[rows, :], x_hi[...], x_lo[...])
            for q in range(4):
                for i in range(OCC_DEV):
                    out[half * 4 + q, i] = term[q * BLK:(q + 1) * BLK, i * V:(i + 1) * V]


SMEM = pl.BlockSpec(memory_space=pltpu.SMEM)
VMEM = pl.BlockSpec(memory_space=pltpu.VMEM)
HBM = pl.BlockSpec(memory_space=pl.ANY)


def own_rows(place, counts, own_pay, other_pay):
    return pl.pallas_call(
        own_rows_kernel,
        out_shape=[jax.ShapeDtypeStruct((OCC_DEV * V, NAUX), jnp.bfloat16)] * 2
        + [jax.ShapeDtypeStruct((2, 8, V), jnp.float32)],
        in_specs=[SMEM, SMEM, VMEM, VMEM],
        out_specs=[VMEM] * 3,
        scratch_shapes=[pltpu.VMEM((NAUX + PAD, OCC_DEV * V), jnp.float32)],
        compiler_params=pltpu.CompilerParams(vmem_limit_bytes=24 * MIB),
        name="own_rows",
    )(place, counts, own_pay, other_pay)


def pairs(place, counts, occ_energy, own_hi, own_lo, times, virt, wide_all):
    part = jax.ShapeDtypeStruct((NY, OCC_DEV, BLK, V), jnp.float32)
    return pl.pallas_call(
        pair_kernel,
        out_shape=[part, part],
        in_specs=[SMEM] * 3 + [HBM, HBM, VMEM, VMEM, HBM],
        out_specs=[VMEM, VMEM],
        scratch_shapes=[
            pltpu.VMEM((OCC_DEV * V, NAUX), jnp.bfloat16),
            pltpu.VMEM((OCC_DEV * V, NAUX), jnp.bfloat16),
            pltpu.VMEM((NZ, NX, 4, CAP, V), jnp.float32),
            pltpu.VMEM((NAUX + PAD, 4 * V), jnp.float32),
            pltpu.VMEM((NAUX, 4 * V), jnp.bfloat16),
            pltpu.VMEM((NAUX, 4 * V), jnp.bfloat16),
            pltpu.VMEM((4 * V, OCC_DEV * V), jnp.bfloat16),
            pltpu.VMEM((4 * V, OCC_DEV * V), jnp.bfloat16),
            pltpu.SemaphoreType.DMA((NZ + 2,)),
        ],
        compiler_params=pltpu.CompilerParams(vmem_limit_bytes=56 * MIB),
        name="pairs",
    )(place, counts, occ_energy, own_hi, own_lo, times, virt, wide_all)


def per_device(three_center, counts, occ_energy, virt_energy, match_tables):
    y, c = lax.axis_index("y"), lax.axis_index("c")
    z, x = lax.axis_index("z"), lax.axis_index("x")
    grp, pos = y * NC + c, z * NX + x
    place = jnp.stack([c, pos, grp]).astype(jnp.int32)

    wide_part = lax.dynamic_slice_in_dim(three_center, 4 * grp, 4, 0)
    wide_all = lax.all_gather(lax.all_gather(wide_part, "x"), "z")

    axes = ("y", "c", "z", "x")
    got = []
    for t in range(2):
        to = lax.rem(grp - pos + 32, 16) + 16 * lax.rem(pos // 16 + t, 2)
        piece = lax.dynamic_slice_in_dim(three_center, OCC_DEV * to, OCC_DEV, 0)
        perm = [
            (g * 32 + s, g * 32 + (g - s) % 16 + 16 * ((s // 16 + t) % 2))
            for g in range(16) for s in range(32)
        ]
        got.append(lax.ppermute(piece, axes, perm).reshape(OCC_DEV * CAP, V))
    partners = lax.dynamic_slice_in_dim(match_tables[:, 0, :], pos, 1, 1).astype(jnp.float32)
    note = jnp.broadcast_to(jnp.repeat(partners.reshape(1, 2), 128, axis=1), (8, V))
    load = jnp.concatenate(got + [note], axis=0)
    sent = jnp.broadcast_to(load[None], (NY, 4 * CAP + 8, V))
    own_pay = lax.all_to_all(sent, "y", split_axis=0, concat_axis=0, tiled=True)
    other_pay = lax.ppermute(own_pay, "c", [(0, 1), (1, 0)])

    own_hi, own_lo, times = own_rows(place, counts, own_pay, other_pay)
    theirs, mine = pairs(place, counts, occ_energy, own_hi, own_lo, times, virt_energy.reshape(1, V), wide_all)

    mine = mine + lax.ppermute(theirs, "c", [(0, 1), (1, 0)])
    pieces = lax.all_to_all(mine, "y", split_axis=0, concat_axis=0, tiled=True)
    return jnp.sum(pieces, axis=0)


def solution(mesh):
    fine = Mesh(np.asarray(mesh.devices).reshape(NY, NC, NZ, NX), ("y", "c", "z", "x"))
    wide, grp = ("z", "x"), ("y", "c")
    placed = (P(None, wide, None), P(), P(), P(), P(None, grp, None))
    return jax.shard_map(
        per_device, mesh=fine, in_specs=placed, out_specs=P(wide, grp, None), check_vma=False
    )
```

time: 169 us -> 156 us (0.923)
  waiting for transfers between devices: 29.5 us -> 13.6 us
  blocking collectives: 77.6 us -> 81.5 us
  local copies, waits for them, and re-layouts: 7.19 us -> 4.63 us
    all_gather x1, waiting for transfers between devices: 23.4 us -> 4.26 us  [per_device(): wide_all = lax.all_gather(lax.all_gather(wide_part, 'x'), 'z')]
    all_gather x0 -> x1, blocking collectives: none -> 12.7 us  [per_device(): wide_all = lax.all_gather(lax.all_gather(wide_part, 'x'), 'z')]
    all_to_all x1, blocking collectives: 43.4 us -> 34.6 us  [per_device(): own_pay = lax.all_to_all(sent, 'y', split_axis=0, concat_axis=0, tiled=True)]
    ppermute x1, starting transfers between devices: 4.61 us -> 7.78 us  [per_device(): other_pay = lax.ppermute(own_pay, 'c', [(0, 1), (1, 0)])]
    ppermute x2, waiting for transfers between devices: 1.17 us -> 4.17 us  [per_device(): got.append(lax.ppermute(piece, axes, perm).reshape(OCC_DEV * CAP, V))]
    ppermute x1, starting transfers between devices: 4.67 us -> 2.59 us  [per_device(): mine = mine + lax.ppermute(theirs, 'c', [(0, 1), (1, 0)])]
    unnamed x16 -> x10, local copies, waits for them, and re-layouts: 4.49 us -> 2.59 us
where the time goes in v3:
time: 156 us
  blocking collectives  81.5 us (52%)
  starting transfers between devices  24.5 us (16%)
  Pallas kernels  14.8 us (9%)
  waiting for transfers between devices  13.6 us (9%)
  between operations  13.5 us (9%)
  local copies, waits for them, and re-layouts  4.63 us (3%)
  other arithmetic  3.03 us (2%)
    all_to_all x1, blocking collectives, per_device(): own_pay = lax.all_to_all(sent, 'y', split_axis=0, concat_axis=0, tiled=True)  34.6 us
    all_to_all x1, blocking collectives, per_device(): pieces = lax.all_to_all(mine, 'y', split_axis=0, concat_axis=0, tiled=True)  34.2 us
    ppermute x2, starting transfers between devices, per_device(): got.append(lax.ppermute(piece, axes, perm).reshape(OCC_DEV * CAP, V))  14.1 us
    all_gather x1, blocking collectives, per_device(): wide_all = lax.all_gather(lax.all_gather(wide_part, 'x'), 'z')  12.7 us
    pallas_call x1, Pallas kernels, pairs(): pl.pallas_call(pair_kernel, out_shape=[part, part], in_specs=[SMEM] * 3 +...  11.9 us
    ppermute x1, starting transfers between devices, per_device(): other_pay = lax.ppermute(own_pay, 'c', [(0, 1), (1, 0)])  7.78 us
    all_gather x1, waiting for transfers between devices, per_device(): wide_all = lax.all_gather(lax.all_gather(wide_part, 'x'), 'z')  4.26 us
    ppermute x2, waiting for transfers between devices, per_device(): got.append(lax.ppermute(piece, axes, perm).reshape(OCC_DEV * CAP, V))  4.17 us
  transfers between devices with their start and end apart: 5, of which 4 were waited for; matrix products, arithmetic and copies ran while one was open for 1% of the time, Pallas kernels for 2%

profile of v3, /device:TPU:1, one launch (start us, length us, event | category | flops | bytes accessed | tf_op | source)
XLA Modules:
  0.0 155.6 jit_solution(9043070277753741945)
XLA Ops:
  6.5 0.0 all-gather.4.cloned.1.call-start
  6.5 0.9 constant_dynamic-slice_fusion
  7.5 12.7 %all-gather = f32[16,40,256]{2,1,0:T(8,128)} all-gather(f32[4,40,256]{2,1,0:T(8,128)S(1)} %constant_dynamic-slice_fusion), channel_id=2, replica_groups=mesh['y'=8,'c'=2,'z'=8,'x'=4] {'x'}, dimensions={0}, use_global_device_ids=true | all-gather | bytes 819200 | tf_op jit(solution)/shard_map/all_gather | solution.py:190
  20.2 0.0 all-gather.4.cloned.1.call-update
  20.2 0.0 copy-start.4
  20.3 0.9 constant_dynamic-slice_fusion.2
  21.2 2.2 %collective-permute-start = (f32[2,40,256]{2,1,0:T(8,128)S(1)}, f32[2,40,256]{2,1,0:T(8,128)S(1)}, u32[]{:S(2)}, u32[]{:S(2)}) collective-permute-start(f32[2,40,256]{2,1,0:T(8,128)S(1)} %get-tuple-element.15), channel_id=1, source_target_pairs={{0,0},{1,15},{2,14},{3,13},{4,12},{5,11},{6,10},{7,9},{8,8},{9,7},... | collective-permute-start | bytes 245768 | tf_op jit(solution)/shard_map/ppermute | solution.py:201
  23.4 12.0 %collective-permute-start.1 = (f32[2,40,256]{2,1,0:T(8,128)S(1)}, f32[2,40,256]{2,1,0:T(8,128)S(1)}, u32[]{:S(2)}, u32[]{:S(2)}) collective-permute-start(f32[2,40,256]{2,1,0:T(8,128)S(1)} %get-tuple-element.16), channel_id=1, source_target_pairs={{0,16},{1,31},{2,30},{3,29},{4,28},{5,27},{6,26},{7,25},{8,24},{9,... | collective-permute-start | bytes 245768 | tf_op jit(solution)/shard_map/ppermute | solution.py:201
  35.4 0.9 convert_reduce_fusion
  36.2 0.1 broadcast_bitcast_fusion
  36.3 0.0 collective-permute-done
  36.3 4.2 %collective-permute-done.1 = f32[2,40,256]{2,1,0:T(8,128)S(1)} collective-permute-done((f32[2,40,256]{2,1,0:T(8,128)S(1)}, f32[2,40,256]{2,1,0:T(8,128)S(1)}, u32[]{:S(2)}, u32[]{:S(2)}) %collective-permute-start.1) | collective-permute-done | bytes 81952 | tf_op jit(solution)/shard_map/ppermute | solution.py:201
  40.5 0.1 broadcast_in_dim.19
  40.6 34.6 %all_to_all.10.own_ref = f32[8,168,256]{2,1,0:T(8,128)S(1)} all-to-all(f32[8,168,256]{2,1,0:T(8,128)S(1)} %broadcast_in_dim.19), channel_id=1, replica_groups=mesh['y'=8,'c'=2,'z'=8,'x'=4] {'y'}, dimensions={0} | all-to-all | bytes 2752512 | tf_op jit(solution)/shard_map/all_to_all | solution.py:206
  75.2 7.8 %collective-permute-start.2 = (f32[8,168,256]{2,1,0:T(8,128)S(1)}, f32[8,168,256]{2,1,0:T(8,128)S(1)}, u32[]{:S(2)}, u32[]{:S(2)}) collective-permute-start(f32[8,168,256]{2,1,0:T(8,128)S(1)} %all_to_all.10.own_ref), channel_id=1, source_target_pairs={{0,32},{32,0},{1,33},{33,1},{2,34},{34,2},{3,35},{35,3},{4,36},{36... | collective-permute-start | bytes 4128776 | tf_op jit(solution)/shard_map/ppermute | solution.py:207
  83.0 0.1 pad_add_fusion.place
  83.0 0.0 copy-start.3
  83.0 2.7 %collective-permute-done.2.other_ref = f32[8,168,256]{2,1,0:T(8,128)S(1)} collective-permute-done((f32[8,168,256]{2,1,0:T(8,128)S(1)}, f32[8,168,256]{2,1,0:T(8,128)S(1)}, u32[]{:S(2)}, u32[]{:S(2)}) %collective-permute-start.2) | collective-permute-done | bytes 1376288 | tf_op jit(solution)/shard_map/ppermute | solution.py:207
  85.7 0.0 copy-done.4
  85.7 3.0 %own_rows.1 = (bf16[512,1024]{1,0:T(8,128)(2,1)S(1)}, bf16[512,1024]{1,0:T(8,128)(2,1)S(1)}, f32[2,8,256]{2,1,0:T(8,128)S(1)}) custom-call(s32[3]{0:T(128)S(1)} %pad_add_fusion.place, s32[32]{0:T(128)S(1)} %copy-done.4, f32[8,168,256]{2,1,0:T(8,128)S(1)} %all_to_all.10.own_ref, f32[8,168,256]{2,1,0:T(8,128)S(1)} %collective-permute-done.2.other_ref), custom_call_target="tpu_custom_call" | custom-call | tf_op jit(solution)/shard_map/own_rows/pallas_call | solution.py:148
  88.7 0.0 copy-start
  88.7 1.0 copy-done
  89.7 0.0 copy-start.1
  89.7 1.0 copy-done.1
  90.7 0.0 copy-start.2
  90.7 0.6 copy-done.2
  91.3 4.3 %all-gather.4.cloned.1.call-done = f32[32,4,40,256]{3,2,1,0:T(8,128)} async-done(((f32[4,4,40,256]{3,2,1,0:T(8,128)}), f32[32,4,40,256]{3,2,1,0:T(8,128)}) %all-gather.4.cloned.1.call-update) | async-done | bytes 5242896 | tf_op jit(solution)/shard_map/all_gather | solution.py:190
  95.5 0.0 copy-done.3
  95.5 11.9 %pairs.1 = (f32[8,2,64,256]{3,2,1,0:T(8,128)}, f32[8,2,64,256]{3,2,1,0:T(8,128)}) custom-call(s32[3]{0:T(128)} %copy-done.3, s32[32]{0:T(128)} %counts.3, f32[64]{0:T(128)} %occ.1, bf16[512,1024]{1,0:T(8,128)(2,1)} %copy-done, bf16[512,1024]{1,0:T(8,128)(2,1)} %copy-done.1, f32[2,8,256]{2,1,0:T(8,128)} %copy-done.2, f32[1,256]{1,0:T(1,128)} %bitcast.14, ...), custom_call_target="tpu_custom_call" | custom-call | tf_op jit(solution)/shard_map/pairs/pallas_call | solution.py:162
  107.4 2.6 %collective-permute-start.3 = (f32[8,2,64,256]{3,2,1,0:T(8,128)}, f32[8,2,64,256]{3,2,1,0:T(8,128)S(1)}, u32[]{:S(2)}, u32[]{:S(2)}) collective-permute-start(f32[8,2,64,256]{3,2,1,0:T(8,128)} %get-tuple-element.14), channel_id=1, source_target_pairs={{0,32},{32,0},{1,33},{33,1},{2,34},{34,2},{3,35},{35,3},{4,36},{36... | collective-permute-start | bytes 3145736 | tf_op jit(solution)/shard_map/ppermute | solution.py:212
  110.0 2.5 %collective-permute-done.3 = f32[8,2,64,256]{3,2,1,0:T(8,128)S(1)} collective-permute-done((f32[8,2,64,256]{3,2,1,0:T(8,128)}, f32[8,2,64,256]{3,2,1,0:T(8,128)S(1)}, u32[]{:S(2)}, u32[]{:S(2)}) %collective-permute-start.3) | collective-permute-done | bytes 1048608 | tf_op jit(solution)/shard_map/ppermute | solution.py:212
  112.5 1.4 add.45
  113.8 34.2 %all_to_all.11 = f32[8,2,64,256]{3,2,1,0:T(8,128)S(1)} all-to-all(f32[8,2,64,256]{3,2,1,0:T(8,128)S(1)} %add.45), channel_id=1, replica_groups=mesh['y'=8,'c'=2,'z'=8,'x'=4] {'y'}, dimensions={0} | all-to-all | bytes 2097152 | tf_op jit(solution)/shard_map/all_to_all | solution.py:213
  148.0 0.7 reduce_sum.9
  (2 shorter events, 0.0 us)
Async XLA Ops:
  6.5 89.0 %all-gather.4.cloned.1.call-start = ((), (), s32[]{:S(2)}) async-start(), calls=%async_computation.2 | async-start | bytes 5898240 | tf_op jit(solution)/shard_map/all_gather | solution.py:190
  20.2 65.5 %copy-start.4 = (s32[32]{0:T(128)S(1)}, s32[32]{0:T(128)}, u32[]{:S(2)}) copy-start(s32[32]{0:T(128)} %counts.3) | copy-start | bytes 388
  21.2 15.1 %collective-permute-start = (f32[2,40,256]{2,1,0:T(8,128)S(1)}, f32[2,40,256]{2,1,0:T(8,128)S(1)}, u32[]{:S(2)}, u32[]{:S(2)}) collective-permute-start(f32[2,40,256]{2,1,0:T(8,128)S(1)} %get-tuple-element.15), channel_id=1, source_target_pairs={{0,0},{1,15},{2,14},{3,13},{4,12},{5,11},{6,10},{7,9},{8,8},{9,7},... | collective-permute-start | bytes 245768 | tf_op jit(solution)/shard_map/ppermute | solution.py:201
  23.4 17.1 %collective-permute-start.1 = (f32[2,40,256]{2,1,0:T(8,128)S(1)}, f32[2,40,256]{2,1,0:T(8,128)S(1)}, u32[]{:S(2)}, u32[]{:S(2)}) collective-permute-start(f32[2,40,256]{2,1,0:T(8,128)S(1)} %get-tuple-element.16), channel_id=1, source_target_pairs={{0,16},{1,31},{2,30},{3,29},{4,28},{5,27},{6,26},{7,25},{8,24},{9,... | collective-permute-start | bytes 245768 | tf_op jit(solution)/shard_map/ppermute | solution.py:201
  75.2 10.5 %collective-permute-start.2 = (f32[8,168,256]{2,1,0:T(8,128)S(1)}, f32[8,168,256]{2,1,0:T(8,128)S(1)}, u32[]{:S(2)}, u32[]{:S(2)}) collective-permute-start(f32[8,168,256]{2,1,0:T(8,128)S(1)} %all_to_all.10.own_ref), channel_id=1, source_target_pairs={{0,32},{32,0},{1,33},{33,1},{2,34},{34,2},{3,35},{35,3},{4,36},{36... | collective-permute-start | bytes 4128776 | tf_op jit(solution)/shard_map/ppermute | solution.py:207
  83.0 12.5 %copy-start.3 = (s32[3]{0:T(128)}, s32[3]{0:T(128)S(1)}, u32[]{:S(2)}) copy-start(s32[3]{0:T(128)S(1)} %pad_add_fusion.place) | copy-start | bytes 40
  88.7 1.0 copy-start
  89.7 1.0 copy-start.1
  90.7 0.6 copy-start.2
  107.4 5.1 %collective-permute-start.3 = (f32[8,2,64,256]{3,2,1,0:T(8,128)}, f32[8,2,64,256]{3,2,1,0:T(8,128)S(1)}, u32[]{:S(2)}, u32[]{:S(2)}) collective-permute-start(f32[8,2,64,256]{3,2,1,0:T(8,128)} %get-tuple-element.14), channel_id=1, source_target_pairs={{0,32},{32,0},{1,33},{33,1},{2,34},{34,2},{3,35},{35,3},{4,36},{36... | collective-permute-start | bytes 3145736 | tf_op jit(solution)/shard_map/ppermute | solution.py:212
Sparse Core Ops, SparseCore 0:
  20.3 75.1 all-gather.3

commit v4 on v3

--- a/solution.py
+++ b/solution.py
@@ -131,12 +131,12 @@
             x_lo[cols, i * V:(i + 1) * V] = lo
 
     for k, out in enumerate((theirs_ref, mine_ref)):
-        for half in range(2):
-            rows = slice(k * 512 + half * 256, k * 512 + half * 256 + 256)
-            term = dot3(w_hi[rows, :], w_lo[rows, :], x_hi[...], x_lo[...])
-            for q in range(4):
-                for i in range(OCC_DEV):
-                    out[half * 4 + q, i] = term[q * BLK:(q + 1) * BLK, i * V:(i + 1) * V]
+        part = slice(k * 512, (k + 1) * 512)
+        for i in range(OCC_DEV):
+            cols = slice(i * V, (i + 1) * V)
+            term = dot3(w_hi[part, :], w_lo[part, :], x_hi[:, cols], x_lo[:, cols])
+            for q in range(NY):
+                out[q, i] = term[q * BLK:(q + 1) * BLK, :]
 
 
 SMEM = pl.BlockSpec(memory_space=pltpu.SMEM)
@@ -175,7 +175,7 @@
             pltpu.VMEM((4 * V, OCC_DEV * V), jnp.bfloat16),
             pltpu.SemaphoreType.DMA((NZ + 2,)),
         ],
-        compiler_params=pltpu.CompilerParams(vmem_limit_bytes=56 * MIB),
+        compiler_params=pltpu.CompilerParams(vmem_limit_bytes=48 * MIB),
         name="pairs",
     )(place, counts, occ_energy, own_hi, own_lo, times, virt, wide_all)
 

time: 156 us -> 153 us (0.981)
  local copies, waits for them, and re-layouts: 4.63 us -> 2.05 us
  waiting for transfers between devices: 13.6 us -> 15.9 us
    unnamed x10 -> x6, local copies, waits for them, and re-layouts: 2.59 us -> 0.02 us
    all_gather x1, waiting for transfers between devices: 4.26 us -> 6.83 us  [per_device(): wide_all = lax.all_gather(lax.all_gather(wide_part, 'x'), 'z')]
where the time goes in v4:
time: 153 us
  blocking collectives  81.5 us (53%)
  starting transfers between devices  24.5 us (16%)
  waiting for transfers between devices  15.9 us (10%)
  between operations  13.5 us (9%)
  Pallas kernels  13.4 us (9%)
  local copies, waits for them, and re-layouts  2.05 us (1%)
  other arithmetic  1.81 us (1%)
    all_to_all x1, blocking collectives, per_device(): own_pay = lax.all_to_all(sent, 'y', split_axis=0, concat_axis=0, tiled=True)  34.6 us
    all_to_all x1, blocking collectives, per_device(): pieces = lax.all_to_all(mine, 'y', split_axis=0, concat_axis=0, tiled=True)  34.2 us
    ppermute x2, starting transfers between devices, per_device(): got.append(lax.ppermute(piece, axes, perm).reshape(OCC_DEV * CAP, V))  14.1 us
    all_gather x1, blocking collectives, per_device(): wide_all = lax.all_gather(lax.all_gather(wide_part, 'x'), 'z')  12.7 us
    pallas_call x1, Pallas kernels, pairs(): pl.pallas_call(pair_kernel, out_shape=[part, part], in_specs=[SMEM] * 3 +...  10.4 us
    ppermute x1, starting transfers between devices, per_device(): other_pay = lax.ppermute(own_pay, 'c', [(0, 1), (1, 0)])  7.78 us
    all_gather x1, waiting for transfers between devices, per_device(): wide_all = lax.all_gather(lax.all_gather(wide_part, 'x'), 'z')  6.83 us
    ppermute x2, waiting for transfers between devices, per_device(): got.append(lax.ppermute(piece, axes, perm).reshape(OCC_DEV * CAP, V))  4.17 us
  transfers between devices with their start and end apart: 5, of which 4 were waited for; matrix products, arithmetic and copies ran while one was open for 1% of the time, Pallas kernels for 2%

profile of v4, /device:TPU:1, one launch (start us, length us, event | category | flops | bytes accessed | tf_op | source)
XLA Modules:
  0.0 152.7 jit_solution(9704706388291085022)
XLA Ops:
  6.5 0.0 all-gather.4.cloned.1.call-start
  6.5 0.9 constant_dynamic-slice_fusion
  7.5 12.7 %all-gather = f32[16,40,256]{2,1,0:T(8,128)} all-gather(f32[4,40,256]{2,1,0:T(8,128)S(1)} %constant_dynamic-slice_fusion), channel_id=2, replica_groups=mesh['y'=8,'c'=2,'z'=8,'x'=4] {'x'}, dimensions={0}, use_global_device_ids=true | all-gather | bytes 819200 | tf_op jit(solution)/shard_map/all_gather | solution.py:190
  20.2 0.0 all-gather.4.cloned.1.call-update
  20.2 0.0 copy-start
  20.3 0.9 constant_dynamic-slice_fusion.2
  21.2 2.2 %collective-permute-start = (f32[2,40,256]{2,1,0:T(8,128)S(1)}, f32[2,40,256]{2,1,0:T(8,128)S(1)}, u32[]{:S(2)}, u32[]{:S(2)}) collective-permute-start(f32[2,40,256]{2,1,0:T(8,128)S(1)} %get-tuple-element.15), channel_id=1, source_target_pairs={{0,0},{1,15},{2,14},{3,13},{4,12},{5,11},{6,10},{7,9},{8,8},{9,7},... | collective-permute-start | bytes 245768 | tf_op jit(solution)/shard_map/ppermute | solution.py:201
  23.4 12.0 %collective-permute-start.1 = (f32[2,40,256]{2,1,0:T(8,128)S(1)}, f32[2,40,256]{2,1,0:T(8,128)S(1)}, u32[]{:S(2)}, u32[]{:S(2)}) collective-permute-start(f32[2,40,256]{2,1,0:T(8,128)S(1)} %get-tuple-element.16), channel_id=1, source_target_pairs={{0,16},{1,31},{2,30},{3,29},{4,28},{5,27},{6,26},{7,25},{8,24},{9,... | collective-permute-start | bytes 245768 | tf_op jit(solution)/shard_map/ppermute | solution.py:201
  35.4 0.9 convert_reduce_fusion
  36.2 0.1 broadcast_bitcast_fusion
  36.3 0.0 collective-permute-done
  36.3 4.2 %collective-permute-done.1 = f32[2,40,256]{2,1,0:T(8,128)S(1)} collective-permute-done((f32[2,40,256]{2,1,0:T(8,128)S(1)}, f32[2,40,256]{2,1,0:T(8,128)S(1)}, u32[]{:S(2)}, u32[]{:S(2)}) %collective-permute-start.1) | collective-permute-done | bytes 81952 | tf_op jit(solution)/shard_map/ppermute | solution.py:201
  40.5 0.1 broadcast_in_dim.19
  40.6 0.0 copy-start.1
  40.6 0.0 copy-start.2
  40.6 34.6 %all_to_all.10.own_ref = f32[8,168,256]{2,1,0:T(8,128)S(1)} all-to-all(f32[8,168,256]{2,1,0:T(8,128)S(1)} %broadcast_in_dim.19), channel_id=1, replica_groups=mesh['y'=8,'c'=2,'z'=8,'x'=4] {'y'}, dimensions={0} | all-to-all | bytes 2752512 | tf_op jit(solution)/shard_map/all_to_all | solution.py:206
  75.2 7.8 %collective-permute-start.2 = (f32[8,168,256]{2,1,0:T(8,128)S(1)}, f32[8,168,256]{2,1,0:T(8,128)S(1)}, u32[]{:S(2)}, u32[]{:S(2)}) collective-permute-start(f32[8,168,256]{2,1,0:T(8,128)S(1)} %all_to_all.10.own_ref), channel_id=1, source_target_pairs={{0,32},{32,0},{1,33},{33,1},{2,34},{34,2},{3,35},{35,3},{4,36},{36... | collective-permute-start | bytes 4128776 | tf_op jit(solution)/shard_map/ppermute | solution.py:207
  83.0 0.1 pad_add_fusion.place
  83.1 2.7 %collective-permute-done.2.other_ref = f32[8,168,256]{2,1,0:T(8,128)S(1)} collective-permute-done((f32[8,168,256]{2,1,0:T(8,128)S(1)}, f32[8,168,256]{2,1,0:T(8,128)S(1)}, u32[]{:S(2)}, u32[]{:S(2)}) %collective-permute-start.2) | collective-permute-done | bytes 1376288 | tf_op jit(solution)/shard_map/ppermute | solution.py:207
  85.7 0.0 copy-done
  85.7 3.0 %own_rows.1 = (bf16[512,1024]{1,0:T(8,128)(2,1)S(1)}, bf16[512,1024]{1,0:T(8,128)(2,1)S(1)}, f32[2,8,256]{2,1,0:T(8,128)S(1)}) custom-call(s32[3]{0:T(128)S(1)} %pad_add_fusion.place, s32[32]{0:T(128)S(1)} %copy-done, f32[8,168,256]{2,1,0:T(8,128)S(1)} %all_to_all.10.own_ref, f32[8,168,256]{2,1,0:T(8,128)S(1)} %collective-permute-done.2.other_ref), custom_call_target="tpu_custom_call" | custom-call | tf_op jit(solution)/shard_map/own_rows/pallas_call | solution.py:148
  88.7 6.8 %all-gather.4.cloned.1.call-done = f32[32,4,40,256]{3,2,1,0:T(8,128)} async-done(((f32[4,4,40,256]{3,2,1,0:T(8,128)}), f32[32,4,40,256]{3,2,1,0:T(8,128)}) %all-gather.4.cloned.1.call-update) | async-done | bytes 5242896 | tf_op jit(solution)/shard_map/all_gather | solution.py:190
  95.5 0.0 copy-done.1
  95.5 0.0 copy-done.2
  95.5 10.4 %pairs.1 = (f32[8,2,64,256]{3,2,1,0:T(8,128)S(1)}, f32[8,2,64,256]{3,2,1,0:T(8,128)S(1)}) custom-call(s32[3]{0:T(128)S(1)} %pad_add_fusion.place, s32[32]{0:T(128)S(1)} %copy-done, f32[64]{0:T(128)S(1)} %copy-done.2, bf16[512,1024]{1,0:T(8,128)(2,1)S(1)} %get-tuple-element.10.own_hi_any, bf16[512,1024]{1,0:T(8,128)(2,1)S(1)} %get-tuple-element.11.own_lo_any, ...), custom_call_target="tpu_custom_call" | custom-call | tf_op jit(solution)/shard_map/pairs/pallas_call | solution.py:162
  106.0 2.6 %collective-permute-start.3 = (f32[8,2,64,256]{3,2,1,0:T(8,128)S(1)}, f32[8,2,64,256]{3,2,1,0:T(8,128)S(1)}, u32[]{:S(2)}, u32[]{:S(2)}) collective-permute-start(f32[8,2,64,256]{3,2,1,0:T(8,128)S(1)} %get-tuple-element.14), channel_id=1, source_target_pairs={{0,32},{32,0},{1,33},{33,1},{2,34},{34,2},{3,35},{35,3},{4,36},{36... | collective-permute-start | bytes 3145736 | tf_op jit(solution)/shard_map/ppermute | solution.py:212
  108.5 2.3 %collective-permute-done.3 = f32[8,2,64,256]{3,2,1,0:T(8,128)S(1)} collective-permute-done((f32[8,2,64,256]{3,2,1,0:T(8,128)S(1)}, f32[8,2,64,256]{3,2,1,0:T(8,128)S(1)}, u32[]{:S(2)}, u32[]{:S(2)}) %collective-permute-start.3) | collective-permute-done | bytes 1048608 | tf_op jit(solution)/shard_map/ppermute | solution.py:212
  110.8 0.1 add.45
  110.9 34.2 %all_to_all.11 = f32[8,2,64,256]{3,2,1,0:T(8,128)S(1)} all-to-all(f32[8,2,64,256]{3,2,1,0:T(8,128)S(1)} %add.45), channel_id=1, replica_groups=mesh['y'=8,'c'=2,'z'=8,'x'=4] {'y'}, dimensions={0} | all-to-all | bytes 2097152 | tf_op jit(solution)/shard_map/all_to_all | solution.py:213
  145.1 0.7 reduce_sum.9
  (2 shorter events, 0.0 us)
Async XLA Ops:
  6.5 89.0 %all-gather.4.cloned.1.call-start = ((), (), s32[]{:S(2)}) async-start(), calls=%async_computation.2 | async-start | bytes 5898240 | tf_op jit(solution)/shard_map/all_gather | solution.py:190
  20.2 65.5 %copy-start = (s32[32]{0:T(128)S(1)}, s32[32]{0:T(128)}, u32[]{:S(2)}) copy-start(s32[32]{0:T(128)} %counts.3) | copy-start | bytes 388
  21.2 15.1 %collective-permute-start = (f32[2,40,256]{2,1,0:T(8,128)S(1)}, f32[2,40,256]{2,1,0:T(8,128)S(1)}, u32[]{:S(2)}, u32[]{:S(2)}) collective-permute-start(f32[2,40,256]{2,1,0:T(8,128)S(1)} %get-tuple-element.15), channel_id=1, source_target_pairs={{0,0},{1,15},{2,14},{3,13},{4,12},{5,11},{6,10},{7,9},{8,8},{9,7},... | collective-permute-start | bytes 245768 | tf_op jit(solution)/shard_map/ppermute | solution.py:201
  23.4 17.1 %collective-permute-start.1 = (f32[2,40,256]{2,1,0:T(8,128)S(1)}, f32[2,40,256]{2,1,0:T(8,128)S(1)}, u32[]{:S(2)}, u32[]{:S(2)}) collective-permute-start(f32[2,40,256]{2,1,0:T(8,128)S(1)} %get-tuple-element.16), channel_id=1, source_target_pairs={{0,16},{1,31},{2,30},{3,29},{4,28},{5,27},{6,26},{7,25},{8,24},{9,... | collective-permute-start | bytes 245768 | tf_op jit(solution)/shard_map/ppermute | solution.py:201
  40.6 54.9 %copy-start.1 = (f32[256]{0:T(256)S(1)}, f32[256]{0:T(256)}, u32[]{:S(2)}) copy-start(f32[256]{0:T(256)} %param.8) | copy-start | bytes 3076
  40.6 54.9 %copy-start.2 = (f32[64]{0:T(128)S(1)}, f32[64]{0:T(128)}, u32[]{:S(2)}) copy-start(f32[64]{0:T(128)} %occ.1) | copy-start | bytes 772
  75.2 10.5 %collective-permute-start.2 = (f32[8,168,256]{2,1,0:T(8,128)S(1)}, f32[8,168,256]{2,1,0:T(8,128)S(1)}, u32[]{:S(2)}, u32[]{:S(2)}) collective-permute-start(f32[8,168,256]{2,1,0:T(8,128)S(1)} %all_to_all.10.own_ref), channel_id=1, source_target_pairs={{0,32},{32,0},{1,33},{33,1},{2,34},{34,2},{3,35},{35,3},{4,36},{36... | collective-permute-start | bytes 4128776 | tf_op jit(solution)/shard_map/ppermute | solution.py:207
  106.0 4.9 %collective-permute-start.3 = (f32[8,2,64,256]{3,2,1,0:T(8,128)S(1)}, f32[8,2,64,256]{3,2,1,0:T(8,128)S(1)}, u32[]{:S(2)}, u32[]{:S(2)}) collective-permute-start(f32[8,2,64,256]{3,2,1,0:T(8,128)S(1)} %get-tuple-element.14), channel_id=1, source_target_pairs={{0,32},{32,0},{1,33},{33,1},{2,34},{34,2},{3,35},{35,3},{4,36},{36... | collective-permute-start | bytes 3145736 | tf_op jit(solution)/shard_map/ppermute | solution.py:212
Sparse Core Ops, SparseCore 0:
  20.3 75.1 all-gather.3

commit v5 on v4

--- a/solution.py
+++ b/solution.py
@@ -41,35 +41,22 @@
     dense[pl.ds(base + CAP, 8), cols] = held
 
 
-def own_rows_kernel(place, counts, own_ref, other_ref, hi_ref, lo_ref, times_ref, dense):
+def own_rows_kernel(place, counts, own_ref, hi_ref, lo_ref, times_ref, dense):
     core, u, grp = place[0], place[1], place[2]
     for w in range(2):
         block = (2 * grp + w).astype(jnp.float32)
         hits = jnp.zeros((8, V), jnp.float32)
-        for y in range(NY):
-            for pay in (own_ref, other_ref):
-                hits = hits + (pay[y, 4 * CAP:4 * CAP + 8, :] == block).astype(jnp.float32)
+        for g in range(NY * NC):
+            hits = hits + (own_ref[g, 4 * CAP:4 * CAP + 8, :] == block).astype(jnp.float32)
         times = hits[:, :128] + hits[:, 128:] + (u == 2 * grp + w).astype(jnp.float32)
         times_ref[w] = jnp.concatenate([times, times], axis=1)
 
     def put(s, off):
         g = lax.rem(s + u, 16)
         t = lax.rem(s // 16 + u // 16, 2)
-        y = g // 2
-
-        def copy(ref):
-            for i in range(OCC_DEV):
-                rows = ref[y, pl.ds(pl.multiple_of((t * OCC_DEV + i) * CAP, 8), CAP), :]
-                put_rows(dense, off, slice(i * V, (i + 1) * V), rows)
-
-        @pl.when(lax.rem(g, 2) == core)
-        def _():
-            copy(own_ref)
-
-        @pl.when(lax.rem(g, 2) != core)
-        def _():
-            copy(other_ref)
-
+        for i in range(OCC_DEV):
+            rows = own_ref[g, pl.ds(pl.multiple_of((t * OCC_DEV + i) * CAP, 8), CAP), :]
+            put_rows(dense, off, slice(i * V, (i + 1) * V), rows)
         return off + counts[s]
 
     lax.fori_loop(0, 32, put, jnp.int32(0))
@@ -89,20 +76,33 @@
         turn(n, 0)
 
 
-def pair_kernel(place, counts, occ, own_hi_any, own_lo_any, times, virt, wide_any,
-                theirs_ref, mine_ref, own_hi, own_lo, rows, dense, w_hi, w_lo, x_hi, x_lo, sems):
+def pair_kernel(place, counts, occ, own_hi_any, own_lo_any, times, virt, *refs):
+    parts, refs = refs[:2 * NZ], refs[2 * NZ:]
+    theirs_ref, mine_ref, own_hi, own_lo, rows, dense, w_hi, w_lo, x_hi, x_lo, sems = refs
     core, u, grp = place[0], place[1], place[2]
-    row_copies = [pltpu.make_async_copy(wide_any.at[z], rows.at[z], sems.at[z]) for z in range(NZ)]
+    z_here = place[3]
+
+    def copies_of(refs, d, js, first_sem):
+        at = lax.rem(z_here + d + NZ, NZ)
+        return [
+            pltpu.make_async_copy(ref, rows.at[at, :, pl.ds(2 * j, 2)], sems.at[first_sem + n])
+            for n, (ref, j) in enumerate(zip(refs, js))
+        ]
+
+    row_copies = []
+    for n, d in enumerate((0, -1, -2, -3, 1, 2, 3, 4)):
+        row_copies += copies_of(parts[2 * n:2 * n + 2], d, (0, 1), 2 + 2 * n)
     own_copies = [
-        pltpu.make_async_copy(own_hi_any, own_hi, sems.at[NZ]),
-        pltpu.make_async_copy(own_lo_any, own_lo, sems.at[NZ + 1]),
+        pltpu.make_async_copy(own_hi_any, own_hi, sems.at[0]),
+        pltpu.make_async_copy(own_lo_any, own_lo, sems.at[1]),
     ]
     for copy in row_copies + own_copies:
         copy.start()
 
+    for copy in row_copies:
+        copy.wait()
     off = jnp.int32(0)
     for z in range(NZ):
-        row_copies[z].wait()
         for x in range(NX):
             for j in range(4):
                 put_rows(dense, off, slice(j * V, (j + 1) * V), rows[z, x, j])
@@ -144,25 +144,25 @@
 HBM = pl.BlockSpec(memory_space=pl.ANY)
 
 
-def own_rows(place, counts, own_pay, other_pay):
+def own_rows(place, counts, own_pay):
     return pl.pallas_call(
         own_rows_kernel,
         out_shape=[jax.ShapeDtypeStruct((OCC_DEV * V, NAUX), jnp.bfloat16)] * 2
         + [jax.ShapeDtypeStruct((2, 8, V), jnp.float32)],
-        in_specs=[SMEM, SMEM, VMEM, VMEM],
+        in_specs=[SMEM, SMEM, VMEM],
         out_specs=[VMEM] * 3,
         scratch_shapes=[pltpu.VMEM((NAUX + PAD, OCC_DEV * V), jnp.float32)],
         compiler_params=pltpu.CompilerParams(vmem_limit_bytes=24 * MIB),
         name="own_rows",
-    )(place, counts, own_pay, other_pay)
-
-
-def pairs(place, counts, occ_energy, own_hi, own_lo, times, virt, wide_all):
+    )(place, counts, own_pay)
+
+
+def pairs(place, counts, occ_energy, own_hi, own_lo, times, virt, parts):
     part = jax.ShapeDtypeStruct((NY, OCC_DEV, BLK, V), jnp.float32)
     return pl.pallas_call(
         pair_kernel,
         out_shape=[part, part],
-        in_specs=[SMEM] * 3 + [HBM, HBM, VMEM, VMEM, HBM],
+        in_specs=[SMEM] * 3 + [HBM, HBM, VMEM, VMEM] + [HBM] * (2 * NZ),
         out_specs=[VMEM, VMEM],
         scratch_shapes=[
             pltpu.VMEM((OCC_DEV * V, NAUX), jnp.bfloat16),
@@ -173,23 +173,24 @@
             pltpu.VMEM((NAUX, 4 * V), jnp.bfloat16),
             pltpu.VMEM((4 * V, OCC_DEV * V), jnp.bfloat16),
             pltpu.VMEM((4 * V, OCC_DEV * V), jnp.bfloat16),
-            pltpu.SemaphoreType.DMA((NZ + 2,)),
+            pltpu.SemaphoreType.DMA((2 + 2 * NZ,)),
         ],
-        compiler_params=pltpu.CompilerParams(vmem_limit_bytes=48 * MIB),
+        compiler_params=pltpu.CompilerParams(vmem_limit_bytes=36 * MIB),
         name="pairs",
-    )(place, counts, occ_energy, own_hi, own_lo, times, virt, wide_all)
+    )(place, counts, occ_energy, own_hi, own_lo, times, virt, *parts)
 
 
 def per_device(three_center, counts, occ_energy, virt_energy, match_tables):
     y, c = lax.axis_index("y"), lax.axis_index("c")
     z, x = lax.axis_index("z"), lax.axis_index("x")
     grp, pos = y * NC + c, z * NX + x
-    place = jnp.stack([c, pos, grp]).astype(jnp.int32)
-
-    wide_part = lax.dynamic_slice_in_dim(three_center, 4 * grp, 4, 0)
-    wide_all = lax.all_gather(lax.all_gather(wide_part, "x"), "z")
+    place = jnp.stack([c, pos, grp, z]).astype(jnp.int32)
+
+    wide_part = lax.dynamic_slice_in_dim(three_center, 4 * grp, 4, 0).reshape(2, OCC_DEV, CAP, V)
+    here = lax.all_gather(wide_part, "x", axis=1)
 
     axes = ("y", "c", "z", "x")
+    three_center, here = lax.optimization_barrier((three_center, here))
     got = []
     for t in range(2):
         to = lax.rem(grp - pos + 32, 16) + 16 * lax.rem(pos // 16 + t, 2)
@@ -202,12 +203,20 @@
     partners = lax.dynamic_slice_in_dim(match_tables[:, 0, :], pos, 1, 1).astype(jnp.float32)
     note = jnp.broadcast_to(jnp.repeat(partners.reshape(1, 2), 128, axis=1), (8, V))
     load = jnp.concatenate(got + [note], axis=0)
-    sent = jnp.broadcast_to(load[None], (NY, 4 * CAP + 8, V))
-    own_pay = lax.all_to_all(sent, "y", split_axis=0, concat_axis=0, tiled=True)
-    other_pay = lax.ppermute(own_pay, "c", [(0, 1), (1, 0)])
-
-    own_hi, own_lo, times = own_rows(place, counts, own_pay, other_pay)
-    theirs, mine = pairs(place, counts, occ_energy, own_hi, own_lo, times, virt_energy.reshape(1, V), wide_all)
+    own_pay = lax.all_gather(load, ("y", "c"))
+
+    def along_z(a, d):
+        return lax.ppermute(a, "z", [(k, (k + d) % NZ) for k in range(NZ)])
+
+    up, down = [[here[0], here[1]]], [[here[0], here[1]]]
+    for _ in range(3):
+        up.append([along_z(a, 1) for a in up[-1]])
+        down.append([along_z(a, -1) for a in down[-1]])
+    far = [along_z(up[3][0], 1), along_z(down[3][1], -1)]
+    parts = sum(up + down[1:], []) + far
+
+    own_hi, own_lo, times = own_rows(place, counts, own_pay)
+    theirs, mine = pairs(place, counts, occ_energy, own_hi, own_lo, times, virt_energy.reshape(1, V), parts)
 
     mine = mine + lax.ppermute(theirs, "c", [(0, 1), (1, 0)])
     pieces = lax.all_to_all(mine, "y", split_axis=0, concat_axis=0, tiled=True)

time: 153 us -> 166 us (1.085)
  the two profiles are of different devices: /device:TPU:1 before, /device:TPU:2 now
where the time goes in v5:
time: 166 us
  starting transfers between devices  65.7 us (40%)
  blocking collectives  57.3 us (35%)
  between operations  13.7 us (8%)
  Pallas kernels  12.9 us (8%)
  waiting for transfers between devices  9.77 us (6%)
  local copies, waits for them, and re-layouts  3.81 us (2%)
  other arithmetic  2.51 us (2%)
    ppermute x14, starting transfers between devices, along_z(): return lax.ppermute(a, 'z', [(k, (k + d) % NZ) for k in range(NZ)])  50.2 us
    all_to_all x1, blocking collectives, per_device(): pieces = lax.all_to_all(mine, 'y', split_axis=0, concat_axis=0, tiled=True)  41.3 us
    all_gather x1, blocking collectives, per_device(): here = lax.all_gather(wide_part, 'x', axis=1)  16 us
    ppermute x2, starting transfers between devices, per_device(): got.append(lax.ppermute(piece, axes, perm).reshape(OCC_DEV * CAP, V))  13.6 us
    pallas_call x1, Pallas kernels, pairs(): pl.pallas_call(pair_kernel, out_shape=[part, part], in_specs=[SMEM] * 3 +...  10.5 us
    ppermute x14, waiting for transfers between devices, along_z(): return lax.ppermute(a, 'z', [(k, (k + d) % NZ) for k in range(NZ)])  4.29 us
  transfers between devices with their start and end apart: 18, of which 3 were waited for; matrix products, arithmetic and copies ran while one was open for 1% of the time, Pallas kernels for 1%

profile of v5, /device:TPU:2, one launch (start us, length us, event | category | flops | bytes accessed | tf_op | source)
XLA Modules:
  0.0 165.7 jit_solution(12532920841775238131)
XLA Ops:
  6.5 0.0 copy-start.1
  6.5 0.0 all-gather.3.cloned.1.call-start
  6.5 0.9 constant_dynamic-slice_fusion.2
  7.5 16.0 %all_gather.9 = f32[2,4,2,40,256]{4,3,2,1,0:T(8,128)S(1)} all-gather(f32[2,1,2,40,256]{4,3,2,1,0:T(8,128)S(1)} %bitcast.17), channel_id=1, replica_groups=mesh['y'=8,'c'=2,'z'=8,'x'=4] {'x'}, dimensions={1}, use_global_device_ids=true | all-gather | bytes 819200 | tf_op jit(solution)/shard_map/all_gather | solution.py:190
  23.5 0.0 copy-start.2
  23.5 0.0 copy-start.3
  23.5 1.0 constant_dynamic-slice_fusion.1
  24.4 7.2 %collective-permute-start = (f32[2,40,256]{2,1,0:T(8,128)S(1)}, f32[2,40,256]{2,1,0:T(8,128)S(1)}, u32[]{:S(2)}, u32[]{:S(2)}) collective-permute-start(f32[2,40,256]{2,1,0:T(8,128)S(1)} %get-tuple-element.19), channel_id=1, source_target_pairs={{0,0},{1,15},{2,14},{3,13},{4,12},{5,11},{6,10},{7,9},{8,8},{9,7},... | collective-permute-start | bytes 245768 | tf_op jit(solution)/shard_map/ppermute | solution.py:202
  31.7 6.4 %collective-permute-start.1 = (f32[2,40,256]{2,1,0:T(8,128)S(1)}, f32[2,40,256]{2,1,0:T(8,128)S(1)}, u32[]{:S(2)}, u32[]{:S(2)}) collective-permute-start(f32[2,40,256]{2,1,0:T(8,128)S(1)} %get-tuple-element.20), channel_id=1, source_target_pairs={{0,16},{1,31},{2,30},{3,29},{4,28},{5,27},{6,26},{7,25},{8,24},{9,... | collective-permute-start | bytes 245768 | tf_op jit(solution)/shard_map/ppermute | solution.py:202
  38.1 0.9 convert_reduce_fusion
  38.9 0.1 broadcast_bitcast_fusion
  39.0 0.0 collective-permute-done
  39.0 2.8 %collective-permute-done.1 = f32[2,40,256]{2,1,0:T(8,128)S(1)} collective-permute-done((f32[2,40,256]{2,1,0:T(8,128)S(1)}, f32[2,40,256]{2,1,0:T(8,128)S(1)}, u32[]{:S(2)}, u32[]{:S(2)}) %collective-permute-start.1) | collective-permute-done | bytes 81952 | tf_op jit(solution)/shard_map/ppermute | solution.py:202
  41.8 0.7 pad_maximum_fusion
  42.5 0.0 all-gather.3.cloned.1.call-update
  42.6 5.3 %collective-permute-start.9 = (f32[4,2,40,256]{3,2,1,0:T(8,128)S(1)}, f32[4,2,40,256]{3,2,1,0:T(8,128)S(1)}, u32[]{:S(2)}, u32[]{:S(2)}) collective-permute-start(f32[4,2,40,256]{3,2,1,0:T(8,128)S(1)} %get-tuple-element.21.refs_1_), channel_id=1, source_target_pairs={{0,28},{4,0},{8,4},{12,8},{16,12},{20,16},{24,20},{28,24},{1,29},{... | collective-permute-start | bytes 983048 | tf_op jit(solution)/shard_map/ppermute | solution.py:209
  47.9 1.9 %collective-permute-start.2 = (f32[4,2,40,256]{3,2,1,0:T(8,128)S(1)}, f32[4,2,40,256]{3,2,1,0:T(8,128)S(1)}, u32[]{:S(2)}, u32[]{:S(2)}) collective-permute-start(f32[4,2,40,256]{3,2,1,0:T(8,128)S(1)} %get-tuple-element.22.refs_0_), channel_id=1, source_target_pairs={{0,4},{4,8},{8,12},{12,16},{16,20},{20,24},{24,28},{28,0},{1,5},{5... | collective-permute-start | bytes 983048 | tf_op jit(solution)/shard_map/ppermute | solution.py:209
  49.8 1.9 %collective-permute-start.3 = (f32[4,2,40,256]{3,2,1,0:T(8,128)S(1)}, f32[4,2,40,256]{3,2,1,0:T(8,128)S(1)}, u32[]{:S(2)}, u32[]{:S(2)}) collective-permute-start(f32[4,2,40,256]{3,2,1,0:T(8,128)S(1)} %get-tuple-element.21.refs_1_), channel_id=1, source_target_pairs={{0,4},{4,8},{8,12},{12,16},{16,20},{20,24},{24,28},{28,0},{1,5},{5... | collective-permute-start | bytes 983048 | tf_op jit(solution)/shard_map/ppermute | solution.py:209
  51.8 5.1 %collective-permute-start.8 = (f32[4,2,40,256]{3,2,1,0:T(8,128)S(1)}, f32[4,2,40,256]{3,2,1,0:T(8,128)S(1)}, u32[]{:S(2)}, u32[]{:S(2)}) collective-permute-start(f32[4,2,40,256]{3,2,1,0:T(8,128)S(1)} %get-tuple-element.22.refs_0_), channel_id=1, source_target_pairs={{0,28},{4,0},{8,4},{12,8},{16,12},{20,16},{24,20},{28,24},{1,29},{... | collective-permute-start | bytes 983048 | tf_op jit(solution)/shard_map/ppermute | solution.py:209
  56.9 0.0 collective-permute-done.9.refs_9_
  56.9 3.9 %collective-permute-start.11 = (f32[4,2,40,256]{3,2,1,0:T(8,128)S(1)}, f32[4,2,40,256]{3,2,1,0:T(8,128)S(1)}, u32[]{:S(2)}, u32[]{:S(2)}) collective-permute-start(f32[4,2,40,256]{3,2,1,0:T(8,128)S(1)} %collective-permute-done.9.refs_9_), channel_id=1, source_target_pairs={{0,28},{4,0},{8,4},{12,8},{16,12},{20,16},{24,20},{28,24},{1,29},{... | collective-permute-start | bytes 983048 | tf_op jit(solution)/shard_map/ppermute | solution.py:209
  60.8 0.0 collective-permute-done.2.refs_2_
  60.9 1.9 %collective-permute-start.4 = (f32[4,2,40,256]{3,2,1,0:T(8,128)S(1)}, f32[4,2,40,256]{3,2,1,0:T(8,128)S(1)}, u32[]{:S(2)}, u32[]{:S(2)}) collective-permute-start(f32[4,2,40,256]{3,2,1,0:T(8,128)S(1)} %collective-permute-done.2.refs_2_), channel_id=1, source_target_pairs={{0,4},{4,8},{8,12},{12,16},{16,20},{20,24},{24,28},{28,0},{1,5},{5... | collective-permute-start | bytes 983048 | tf_op jit(solution)/shard_map/ppermute | solution.py:209
  62.8 0.0 collective-permute-done.3.refs_3_
  62.8 2.0 %collective-permute-start.5 = (f32[4,2,40,256]{3,2,1,0:T(8,128)S(1)}, f32[4,2,40,256]{3,2,1,0:T(8,128)S(1)}, u32[]{:S(2)}, u32[]{:S(2)}) collective-permute-start(f32[4,2,40,256]{3,2,1,0:T(8,128)S(1)} %collective-permute-done.3.refs_3_), channel_id=1, source_target_pairs={{0,4},{4,8},{8,12},{12,16},{16,20},{20,24},{24,28},{28,0},{1,5},{5... | collective-permute-start | bytes 983048 | tf_op jit(solution)/shard_map/ppermute | solution.py:209
  64.8 0.0 collective-permute-done.8.refs_8_
  64.8 8.3 %collective-permute-start.10 = (f32[4,2,40,256]{3,2,1,0:T(8,128)S(1)}, f32[4,2,40,256]{3,2,1,0:T(8,128)S(1)}, u32[]{:S(2)}, u32[]{:S(2)}) collective-permute-start(f32[4,2,40,256]{3,2,1,0:T(8,128)S(1)} %collective-permute-done.8.refs_8_), channel_id=1, source_target_pairs={{0,28},{4,0},{8,4},{12,8},{16,12},{20,16},{24,20},{28,24},{1,29},{... | collective-permute-start | bytes 983048 | tf_op jit(solution)/shard_map/ppermute | solution.py:209
  73.1 0.0 collective-permute-done.11.refs_11_
  73.1 3.9 %collective-permute-start.13 = (f32[4,2,40,256]{3,2,1,0:T(8,128)S(1)}, f32[4,2,40,256]{3,2,1,0:T(8,128)}, u32[]{:S(2)}, u32[]{:S(2)}) collective-permute-start(f32[4,2,40,256]{3,2,1,0:T(8,128)S(1)} %collective-permute-done.11.refs_11_), channel_id=1, source_target_pairs={{0,28},{4,0},{8,4},{12,8},{16,12},{20,16},{24,20},{28,24},{1,29},{... | collective-permute-start | bytes 983048 | tf_op jit(solution)/shard_map/ppermute | solution.py:209
  77.0 0.0 collective-permute-done.4.refs_4_
  77.0 1.9 %collective-permute-start.6 = (f32[4,2,40,256]{3,2,1,0:T(8,128)S(1)}, f32[4,2,40,256]{3,2,1,0:T(8,128)}, u32[]{:S(2)}, u32[]{:S(2)}) collective-permute-start(f32[4,2,40,256]{3,2,1,0:T(8,128)S(1)} %collective-permute-done.4.refs_4_), channel_id=1, source_target_pairs={{0,4},{4,8},{8,12},{12,16},{16,20},{20,24},{24,28},{28,0},{1,5},{5... | collective-permute-start | bytes 983048 | tf_op jit(solution)/shard_map/ppermute | solution.py:209
  79.0 0.0 collective-permute-done.5.refs_5_
  79.0 1.9 %collective-permute-start.7 = (f32[4,2,40,256]{3,2,1,0:T(8,128)S(1)}, f32[4,2,40,256]{3,2,1,0:T(8,128)}, u32[]{:S(2)}, u32[]{:S(2)}) collective-permute-start(f32[4,2,40,256]{3,2,1,0:T(8,128)S(1)} %collective-permute-done.5.refs_5_), channel_id=1, source_target_pairs={{0,4},{4,8},{8,12},{12,16},{16,20},{20,24},{24,28},{28,0},{1,5},{5... | collective-permute-start | bytes 983048 | tf_op jit(solution)/shard_map/ppermute | solution.py:209
  80.9 0.0 collective-permute-done.10.refs_10_
  80.9 6.2 %collective-permute-start.12 = (f32[4,2,40,256]{3,2,1,0:T(8,128)S(1)}, f32[4,2,40,256]{3,2,1,0:T(8,128)}, u32[]{:S(2)}, u32[]{:S(2)}) collective-permute-start(f32[4,2,40,256]{3,2,1,0:T(8,128)S(1)} %collective-permute-done.10.refs_10_), channel_id=1, source_target_pairs={{0,28},{4,0},{8,4},{12,8},{16,12},{20,16},{24,20},{28,24},{1,29},{... | collective-permute-start | bytes 983048 | tf_op jit(solution)/shard_map/ppermute | solution.py:209
  87.1 0.0 collective-permute-done.13.refs_13_
  87.1 3.9 %collective-permute-start.15 = (f32[4,2,40,256]{3,2,1,0:T(8,128)}, f32[4,2,40,256]{3,2,1,0:T(8,128)}, u32[]{:S(2)}, u32[]{:S(2)}) collective-permute-start(f32[4,2,40,256]{3,2,1,0:T(8,128)} %collective-permute-done.13.refs_13_), channel_id=1, source_target_pairs={{0,28},{4,0},{8,4},{12,8},{16,12},{20,16},{24,20},{28,24},{1,29},{... | collective-permute-start | bytes 983048 | tf_op jit(solution)/shard_map/ppermute | solution.py:209
  91.1 0.0 collective-permute-done.6.refs_6_
  91.1 1.9 %collective-permute-start.14 = (f32[4,2,40,256]{3,2,1,0:T(8,128)}, f32[4,2,40,256]{3,2,1,0:T(8,128)}, u32[]{:S(2)}, u32[]{:S(2)}) collective-permute-start(f32[4,2,40,256]{3,2,1,0:T(8,128)} %collective-permute-done.6.refs_6_), channel_id=1, source_target_pairs={{0,4},{4,8},{8,12},{12,16},{16,20},{20,24},{24,28},{28,0},{1,5},{5... | collective-permute-start | bytes 983048 | tf_op jit(solution)/shard_map/ppermute | solution.py:209
  93.0 0.1 pad_add_fusion.place
  93.1 0.0 all-gather.3.cloned.1.call-done
  93.1 0.0 copy-done.1
  93.1 0.0 copy-start
  93.1 1.8 %copy-done = f32[2688,256]{1,0:T(8,128)S(1)} copy-done((f32[2688,256]{1,0:T(8,128)S(1)}, f32[2688,256]{1,0:T(8,128)}, u32[]{:S(2)}) %copy-start) | copy-done | bytes 2752536
  94.9 2.4 %own_rows.1 = (bf16[512,1024]{1,0:T(8,128)(2,1)S(1)}, bf16[512,1024]{1,0:T(8,128)(2,1)S(1)}, f32[2,8,256]{2,1,0:T(8,128)S(1)}) custom-call(s32[4]{0:T(128)S(1)} %pad_add_fusion.place, s32[32]{0:T(128)S(1)} %copy-done.1, f32[16,168,256]{2,1,0:T(8,128)S(1)} %bitcast.15), custom_call_target="tpu_custom_call" | custom-call | tf_op jit(solution)/shard_map/own_rows/pallas_call | solution.py:148
  97.3 0.0 collective-permute-done.7.refs_7_
  97.3 0.0 collective-permute-done.12.refs_12_
  97.3 0.0 collective-permute-done.15.refs_15_
  97.3 4.3 %collective-permute-done.14.refs_14_ = f32[4,2,40,256]{3,2,1,0:T(8,128)} collective-permute-done((f32[4,2,40,256]{3,2,1,0:T(8,128)}, f32[4,2,40,256]{3,2,1,0:T(8,128)}, u32[]{:S(2)}, u32[]{:S(2)}) %collective-permute-start.14) | collective-permute-done | bytes 327712 | tf_op jit(solution)/shard_map/ppermute | solution.py:209
  101.6 0.0 copy-done.2
  101.6 0.0 copy-done.3
  101.6 10.5 %pairs.1 = (f32[8,2,64,256]{3,2,1,0:T(8,128)S(1)}, f32[8,2,64,256]{3,2,1,0:T(8,128)S(1)}) custom-call(s32[4]{0:T(128)S(1)} %pad_add_fusion.place, s32[32]{0:T(128)S(1)} %copy-done.1, f32[64]{0:T(128)S(1)} %copy-done.3, bf16[512,1024]{1,0:T(8,128)(2,1)S(1)} %get-tuple-element.13.own_hi_any, bf16[512,1024]{1,0:T(8,128)(2,1)S(1)} %get-tuple-element.14.own_lo_any, ...), custom_call_target="tpu_custom_call" | custom-call | tf_op jit(solution)/shard_map/pairs/pallas_call | solution.py:162
  112.1 1.9 %collective-permute-start.16 = (f32[8,2,64,256]{3,2,1,0:T(8,128)S(1)}, f32[8,2,64,256]{3,2,1,0:T(8,128)S(1)}, u32[]{:S(2)}, u32[]{:S(2)}) collective-permute-start(f32[8,2,64,256]{3,2,1,0:T(8,128)S(1)} %get-tuple-element.18), channel_id=1, source_target_pairs={{0,32},{32,0},{1,33},{33,1},{2,34},{34,2},{3,35},{35,3},{4,36},{36... | collective-permute-start | bytes 3145736 | tf_op jit(solution)/shard_map/ppermute | solution.py:221
  114.0 2.6 %collective-permute-done.16 = f32[8,2,64,256]{3,2,1,0:T(8,128)S(1)} collective-permute-done((f32[8,2,64,256]{3,2,1,0:T(8,128)S(1)}, f32[8,2,64,256]{3,2,1,0:T(8,128)S(1)}, u32[]{:S(2)}, u32[]{:S(2)}) %collective-permute-start.16) | collective-permute-done | bytes 1048608 | tf_op jit(solution)/shard_map/ppermute | solution.py:221
  116.7 0.2 add.45
  116.8 41.3 %all_to_all.5 = f32[8,2,64,256]{3,2,1,0:T(8,128)S(1)} all-to-all(f32[8,2,64,256]{3,2,1,0:T(8,128)S(1)} %add.45), channel_id=1, replica_groups=mesh['y'=8,'c'=2,'z'=8,'x'=4] {'y'}, dimensions={0} | all-to-all | bytes 2097152 | tf_op jit(solution)/shard_map/all_to_all | solution.py:222
  158.1 0.7 reduce_sum.9
  (2 shorter events, 0.0 us)
Async XLA Ops:
  6.5 86.6 %copy-start.1 = (s32[32]{0:T(128)S(1)}, s32[32]{0:T(128)}, u32[]{:S(2)}) copy-start(s32[32]{0:T(128)} %counts.3) | copy-start | bytes 388
  6.5 86.6 %all-gather.3.cloned.1.call-start = ((), (), s32[]{:S(2)}) async-start(), calls=%async_computation.1 | async-start | bytes 2924544 | tf_op jit(solution)/shard_map/all_gather | solution.py:206
  23.5 78.1 %copy-start.2 = (f32[256]{0:T(256)S(1)}, f32[256]{0:T(256)}, u32[]{:S(2)}) copy-start(f32[256]{0:T(256)} %param.8) | copy-start | bytes 3076
  23.5 78.1 %copy-start.3 = (f32[64]{0:T(128)S(1)}, f32[64]{0:T(128)}, u32[]{:S(2)}) copy-start(f32[64]{0:T(128)} %occ.1) | copy-start | bytes 772
  24.4 14.6 %collective-permute-start = (f32[2,40,256]{2,1,0:T(8,128)S(1)}, f32[2,40,256]{2,1,0:T(8,128)S(1)}, u32[]{:S(2)}, u32[]{:S(2)}) collective-permute-start(f32[2,40,256]{2,1,0:T(8,128)S(1)} %get-tuple-element.19), channel_id=1, source_target_pairs={{0,0},{1,15},{2,14},{3,13},{4,12},{5,11},{6,10},{7,9},{8,8},{9,7},... | collective-permute-start | bytes 245768 | tf_op jit(solution)/shard_map/ppermute | solution.py:202
  31.7 10.2 %collective-permute-start.1 = (f32[2,40,256]{2,1,0:T(8,128)S(1)}, f32[2,40,256]{2,1,0:T(8,128)S(1)}, u32[]{:S(2)}, u32[]{:S(2)}) collective-permute-start(f32[2,40,256]{2,1,0:T(8,128)S(1)} %get-tuple-element.20), channel_id=1, source_target_pairs={{0,16},{1,31},{2,30},{3,29},{4,28},{5,27},{6,26},{7,25},{8,24},{9,... | collective-permute-start | bytes 245768 | tf_op jit(solution)/shard_map/ppermute | solution.py:202
  42.6 14.3 %collective-permute-start.9 = (f32[4,2,40,256]{3,2,1,0:T(8,128)S(1)}, f32[4,2,40,256]{3,2,1,0:T(8,128)S(1)}, u32[]{:S(2)}, u32[]{:S(2)}) collective-permute-start(f32[4,2,40,256]{3,2,1,0:T(8,128)S(1)} %get-tuple-element.21.refs_1_), channel_id=1, source_target_pairs={{0,28},{4,0},{8,4},{12,8},{16,12},{20,16},{24,20},{28,24},{1,29},{... | collective-permute-start | bytes 983048 | tf_op jit(solution)/shard_map/ppermute | solution.py:209
  47.9 12.9 %collective-permute-start.2 = (f32[4,2,40,256]{3,2,1,0:T(8,128)S(1)}, f32[4,2,40,256]{3,2,1,0:T(8,128)S(1)}, u32[]{:S(2)}, u32[]{:S(2)}) collective-permute-start(f32[4,2,40,256]{3,2,1,0:T(8,128)S(1)} %get-tuple-element.22.refs_0_), channel_id=1, source_target_pairs={{0,4},{4,8},{8,12},{12,16},{16,20},{20,24},{24,28},{28,0},{1,5},{5... | collective-permute-start | bytes 983048 | tf_op jit(solution)/shard_map/ppermute | solution.py:209
  49.8 13.0 %collective-permute-start.3 = (f32[4,2,40,256]{3,2,1,0:T(8,128)S(1)}, f32[4,2,40,256]{3,2,1,0:T(8,128)S(1)}, u32[]{:S(2)}, u32[]{:S(2)}) collective-permute-start(f32[4,2,40,256]{3,2,1,0:T(8,128)S(1)} %get-tuple-element.21.refs_1_), channel_id=1, source_target_pairs={{0,4},{4,8},{8,12},{12,16},{16,20},{20,24},{24,28},{28,0},{1,5},{5... | collective-permute-start | bytes 983048 | tf_op jit(solution)/shard_map/ppermute | solution.py:209
  51.8 13.0 %collective-permute-start.8 = (f32[4,2,40,256]{3,2,1,0:T(8,128)S(1)}, f32[4,2,40,256]{3,2,1,0:T(8,128)S(1)}, u32[]{:S(2)}, u32[]{:S(2)}) collective-permute-start(f32[4,2,40,256]{3,2,1,0:T(8,128)S(1)} %get-tuple-element.22.refs_0_), channel_id=1, source_target_pairs={{0,28},{4,0},{8,4},{12,8},{16,12},{20,16},{24,20},{28,24},{1,29},{... | collective-permute-start | bytes 983048 | tf_op jit(solution)/shard_map/ppermute | solution.py:209
  56.9 16.2 %collective-permute-start.11 = (f32[4,2,40,256]{3,2,1,0:T(8,128)S(1)}, f32[4,2,40,256]{3,2,1,0:T(8,128)S(1)}, u32[]{:S(2)}, u32[]{:S(2)}) collective-permute-start(f32[4,2,40,256]{3,2,1,0:T(8,128)S(1)} %collective-permute-done.9.refs_9_), channel_id=1, source_target_pairs={{0,28},{4,0},{8,4},{12,8},{16,12},{20,16},{24,20},{28,24},{1,29},{... | collective-permute-start | bytes 983048 | tf_op jit(solution)/shard_map/ppermute | solution.py:209
  60.9 16.2 %collective-permute-start.4 = (f32[4,2,40,256]{3,2,1,0:T(8,128)S(1)}, f32[4,2,40,256]{3,2,1,0:T(8,128)S(1)}, u32[]{:S(2)}, u32[]{:S(2)}) collective-permute-start(f32[4,2,40,256]{3,2,1,0:T(8,128)S(1)} %collective-permute-done.2.refs_2_), channel_id=1, source_target_pairs={{0,4},{4,8},{8,12},{12,16},{16,20},{20,24},{24,28},{28,0},{1,5},{5... | collective-permute-start | bytes 983048 | tf_op jit(solution)/shard_map/ppermute | solution.py:209
  62.8 16.2 %collective-permute-start.5 = (f32[4,2,40,256]{3,2,1,0:T(8,128)S(1)}, f32[4,2,40,256]{3,2,1,0:T(8,128)S(1)}, u32[]{:S(2)}, u32[]{:S(2)}) collective-permute-start(f32[4,2,40,256]{3,2,1,0:T(8,128)S(1)} %collective-permute-done.3.refs_3_), channel_id=1, source_target_pairs={{0,4},{4,8},{8,12},{12,16},{16,20},{20,24},{24,28},{28,0},{1,5},{5... | collective-permute-start | bytes 983048 | tf_op jit(solution)/shard_map/ppermute | solution.py:209
  64.8 16.2 %collective-permute-start.10 = (f32[4,2,40,256]{3,2,1,0:T(8,128)S(1)}, f32[4,2,40,256]{3,2,1,0:T(8,128)S(1)}, u32[]{:S(2)}, u32[]{:S(2)}) collective-permute-start(f32[4,2,40,256]{3,2,1,0:T(8,128)S(1)} %collective-permute-done.8.refs_8_), channel_id=1, source_target_pairs={{0,28},{4,0},{8,4},{12,8},{16,12},{20,16},{24,20},{28,24},{1,29},{... | collective-permute-start | bytes 983048 | tf_op jit(solution)/shard_map/ppermute | solution.py:209
  73.1 14.0 %collective-permute-start.13 = (f32[4,2,40,256]{3,2,1,0:T(8,128)S(1)}, f32[4,2,40,256]{3,2,1,0:T(8,128)}, u32[]{:S(2)}, u32[]{:S(2)}) collective-permute-start(f32[4,2,40,256]{3,2,1,0:T(8,128)S(1)} %collective-permute-done.11.refs_11_), channel_id=1, source_target_pairs={{0,28},{4,0},{8,4},{12,8},{16,12},{20,16},{24,20},{28,24},{1,29},{... | collective-permute-start | bytes 983048 | tf_op jit(solution)/shard_map/ppermute | solution.py:209
  77.0 14.0 %collective-permute-start.6 = (f32[4,2,40,256]{3,2,1,0:T(8,128)S(1)}, f32[4,2,40,256]{3,2,1,0:T(8,128)}, u32[]{:S(2)}, u32[]{:S(2)}) collective-permute-start(f32[4,2,40,256]{3,2,1,0:T(8,128)S(1)} %collective-permute-done.4.refs_4_), channel_id=1, source_target_pairs={{0,4},{4,8},{8,12},{12,16},{16,20},{20,24},{24,28},{28,0},{1,5},{5... | collective-permute-start | bytes 983048 | tf_op jit(solution)/shard_map/ppermute | solution.py:209
  79.0 18.3 %collective-permute-start.7 = (f32[4,2,40,256]{3,2,1,0:T(8,128)S(1)}, f32[4,2,40,256]{3,2,1,0:T(8,128)}, u32[]{:S(2)}, u32[]{:S(2)}) collective-permute-start(f32[4,2,40,256]{3,2,1,0:T(8,128)S(1)} %collective-permute-done.5.refs_5_), channel_id=1, source_target_pairs={{0,4},{4,8},{8,12},{12,16},{16,20},{20,24},{24,28},{28,0},{1,5},{5... | collective-permute-start | bytes 983048 | tf_op jit(solution)/shard_map/ppermute | solution.py:209
  80.9 16.4 %collective-permute-start.12 = (f32[4,2,40,256]{3,2,1,0:T(8,128)S(1)}, f32[4,2,40,256]{3,2,1,0:T(8,128)}, u32[]{:S(2)}, u32[]{:S(2)}) collective-permute-start(f32[4,2,40,256]{3,2,1,0:T(8,128)S(1)} %collective-permute-done.10.refs_10_), channel_id=1, source_target_pairs={{0,28},{4,0},{8,4},{12,8},{16,12},{20,16},{24,20},{28,24},{1,29},{... | collective-permute-start | bytes 983048 | tf_op jit(solution)/shard_map/ppermute | solution.py:209
  87.1 10.2 %collective-permute-start.15 = (f32[4,2,40,256]{3,2,1,0:T(8,128)}, f32[4,2,40,256]{3,2,1,0:T(8,128)}, u32[]{:S(2)}, u32[]{:S(2)}) collective-permute-start(f32[4,2,40,256]{3,2,1,0:T(8,128)} %collective-permute-done.13.refs_13_), channel_id=1, source_target_pairs={{0,28},{4,0},{8,4},{12,8},{16,12},{20,16},{24,20},{28,24},{1,29},{... | collective-permute-start | bytes 983048 | tf_op jit(solution)/shard_map/ppermute | solution.py:209
  91.1 10.5 %collective-permute-start.14 = (f32[4,2,40,256]{3,2,1,0:T(8,128)}, f32[4,2,40,256]{3,2,1,0:T(8,128)}, u32[]{:S(2)}, u32[]{:S(2)}) collective-permute-start(f32[4,2,40,256]{3,2,1,0:T(8,128)} %collective-permute-done.6.refs_6_), channel_id=1, source_target_pairs={{0,4},{4,8},{8,12},{12,16},{16,20},{20,24},{24,28},{28,0},{1,5},{5... | collective-permute-start | bytes 983048 | tf_op jit(solution)/shard_map/ppermute | solution.py:209
  93.1 1.8 %copy-start = (f32[2688,256]{1,0:T(8,128)S(1)}, f32[2688,256]{1,0:T(8,128)}, u32[]{:S(2)}) copy-start(f32[2688,256]{1,0:T(8,128)} %all-gather.3.cloned.1.call-done) | copy-start | bytes 8257540
  112.1 4.6 %collective-permute-start.16 = (f32[8,2,64,256]{3,2,1,0:T(8,128)S(1)}, f32[8,2,64,256]{3,2,1,0:T(8,128)S(1)}, u32[]{:S(2)}, u32[]{:S(2)}) collective-permute-start(f32[8,2,64,256]{3,2,1,0:T(8,128)S(1)} %get-tuple-element.18), channel_id=1, source_target_pairs={{0,32},{32,0},{1,33},{33,1},{2,34},{34,2},{3,35},{35,3},{4,36},{36... | collective-permute-start | bytes 3145736 | tf_op jit(solution)/shard_map/ppermute | solution.py:221
Sparse Core Ops, SparseCore 0:
  42.7 44.6 all-gather.2

commit v6 on v5

--- a/solution.py
+++ b/solution.py
@@ -85,13 +85,16 @@
     def copies_of(refs, d, js, first_sem):
         at = lax.rem(z_here + d + NZ, NZ)
         return [
-            pltpu.make_async_copy(ref, rows.at[at, :, pl.ds(2 * j, 2)], sems.at[first_sem + n])
-            for n, (ref, j) in enumerate(zip(refs, js))
+            pltpu.make_async_copy(
+                ref.at[e], rows.at[at, lax.rem(place[4] - e + NX, NX), pl.ds(2 * j, 2)],
+                sems.at[first_sem + n * NX + e],
+            )
+            for n, (ref, j) in enumerate(zip(refs, js)) for e in range(NX)
         ]
 
     row_copies = []
     for n, d in enumerate((0, -1, -2, -3, 1, 2, 3, 4)):
-        row_copies += copies_of(parts[2 * n:2 * n + 2], d, (0, 1), 2 + 2 * n)
+        row_copies += copies_of(parts[2 * n:2 * n + 2], d, (0, 1), 2 + 2 * NX * n)
     own_copies = [
         pltpu.make_async_copy(own_hi_any, own_hi, sems.at[0]),
         pltpu.make_async_copy(own_lo_any, own_lo, sems.at[1]),
@@ -173,7 +176,7 @@
             pltpu.VMEM((NAUX, 4 * V), jnp.bfloat16),
             pltpu.VMEM((4 * V, OCC_DEV * V), jnp.bfloat16),
             pltpu.VMEM((4 * V, OCC_DEV * V), jnp.bfloat16),
-            pltpu.SemaphoreType.DMA((2 + 2 * NZ,)),
+            pltpu.SemaphoreType.DMA((2 + 2 * NZ * NX,)),
         ],
         compiler_params=pltpu.CompilerParams(vmem_limit_bytes=36 * MIB),
         name="pairs",
@@ -184,13 +187,15 @@
     y, c = lax.axis_index("y"), lax.axis_index("c")
     z, x = lax.axis_index("z"), lax.axis_index("x")
     grp, pos = y * NC + c, z * NX + x
-    place = jnp.stack([c, pos, grp, z]).astype(jnp.int32)
-
-    wide_part = lax.dynamic_slice_in_dim(three_center, 4 * grp, 4, 0).reshape(2, OCC_DEV, CAP, V)
-    here = lax.all_gather(wide_part, "x", axis=1)
-
+    place = jnp.stack([c, pos, grp, z, x]).astype(jnp.int32)
+
+    wide_part = lax.dynamic_slice_in_dim(three_center, 4 * grp, 4, 0)
+
+    def along(a, axis, size, d):
+        return lax.ppermute(a, axis, [(k, (k + d) % size) for k in range(size)])
+
+    beside = [along(wide_part, "x", NX, d) for d in (1, 2, 3)]
     axes = ("y", "c", "z", "x")
-    three_center, here = lax.optimization_barrier((three_center, here))
     got = []
     for t in range(2):
         to = lax.rem(grp - pos + 32, 16) + 16 * lax.rem(pos // 16 + t, 2)
@@ -199,20 +204,21 @@
             (g * 32 + s, g * 32 + (g - s) % 16 + 16 * ((s // 16 + t) % 2))
             for g in range(16) for s in range(32)
         ]
-        got.append(lax.ppermute(piece, axes, perm).reshape(OCC_DEV * CAP, V))
+        got.append(lax.ppermute(piece, axes, perm))
+    got, beside = lax.optimization_barrier((got, beside))
+    got = [a.reshape(OCC_DEV * CAP, V) for a in got]
+    row = jnp.stack([wide_part] + beside)
+
     partners = lax.dynamic_slice_in_dim(match_tables[:, 0, :], pos, 1, 1).astype(jnp.float32)
     note = jnp.broadcast_to(jnp.repeat(partners.reshape(1, 2), 128, axis=1), (8, V))
     load = jnp.concatenate(got + [note], axis=0)
     own_pay = lax.all_gather(load, ("y", "c"))
 
-    def along_z(a, d):
-        return lax.ppermute(a, "z", [(k, (k + d) % NZ) for k in range(NZ)])
-
-    up, down = [[here[0], here[1]]], [[here[0], here[1]]]
+    up, down = [[row[:, :2], row[:, 2:]]], [[row[:, :2], row[:, 2:]]]
     for _ in range(3):
-        up.append([along_z(a, 1) for a in up[-1]])
-        down.append([along_z(a, -1) for a in down[-1]])
-    far = [along_z(up[3][0], 1), along_z(down[3][1], -1)]
+        up.append([along(a, "z", NZ, 1) for a in up[-1]])
+        down.append([along(a, "z", NZ, -1) for a in down[-1]])
+    far = [along(up[3][0], "z", NZ, 1), along(down[3][1], "z", NZ, -1)]
     parts = sum(up + down[1:], []) + far
 
     own_hi, own_lo, times = own_rows(place, counts, own_pay)

time: 166 us -> 162 us (0.976)
  the two profiles are of different devices: /device:TPU:2 before, /device:TPU:1 now
where the time goes in v6:
time: 162 us; the launch traced here: 160 us
  starting transfers between devices  72.7 us (45%)
  blocking collectives  36.2 us (22%)
  Pallas kernels  17.8 us (11%)
  between operations  13.8 us (9%)
  waiting for transfers between devices  12.7 us (8%)
  local copies, waits for them, and re-layouts  4.82 us (3%)
  other arithmetic  2.47 us (2%)
    ppermute x17, starting transfers between devices, along(): return lax.ppermute(a, axis, [(k, (k + d) % size) for k in range(size)])  52.3 us
    all_to_all x1, blocking collectives, per_device(): pieces = lax.all_to_all(mine, 'y', split_axis=0, concat_axis=0, tiled=True)  36.2 us
    pallas_call x1, Pallas kernels, pairs(): pl.pallas_call(pair_kernel, out_shape=[part, part], in_specs=[SMEM] * 3 +...  15.4 us
    ppermute x2, starting transfers between devices, per_device(): got.append(lax.ppermute(piece, axes, perm))  13.8 us
    ppermute x17, waiting for transfers between devices, along(): return lax.ppermute(a, axis, [(k, (k + d) % size) for k in range(size)])  7.48 us
    ppermute x1, starting transfers between devices, per_device(): mine = mine + lax.ppermute(theirs, 'c', [(0, 1), (1, 0)])  6.58 us
  transfers between devices with their start and end apart: 21, of which 8 were waited for; matrix products, arithmetic and copies ran while one was open for 2% of the time, Pallas kernels for 1%

profile of v6, /device:TPU:1, one launch (start us, length us, event | category | flops | bytes accessed | tf_op | source)
XLA Modules:
  0.0 160.3 jit_solution(16829464761939679690)
XLA Ops:
  6.5 0.0 copy-start.1
  6.5 0.0 all-gather.3.cloned.1.call-start
  6.5 0.9 constant_dynamic-slice_fusion
  7.5 5.2 %collective-permute-start.4 = (f32[4,40,256]{2,1,0:T(8,128)S(1)}, f32[4,40,256]{2,1,0:T(8,128)S(1)}, u32[]{:S(2)}, u32[]{:S(2)}) collective-permute-start(f32[4,40,256]{2,1,0:T(8,128)S(1)} %constant_dynamic-slice_fusion), channel_id=1, source_target_pairs={{0,3},{1,0},{2,1},{3,2},{4,7},{5,4},{6,5},{7,6},{8,11},{9,8},{10,9... | collective-permute-start | bytes 491528 | tf_op jit(solution)/shard_map/ppermute | solution.py:195
  12.7 2.4 %collective-permute-start.3 = (f32[4,40,256]{2,1,0:T(8,128)S(1)}, f32[4,40,256]{2,1,0:T(8,128)S(1)}, u32[]{:S(2)}, u32[]{:S(2)}) collective-permute-start(f32[4,40,256]{2,1,0:T(8,128)S(1)} %constant_dynamic-slice_fusion), channel_id=1, source_target_pairs={{0,2},{1,3},{2,0},{3,1},{4,6},{5,7},{6,4},{7,5},{8,10},{9,11},{10,... | collective-permute-start | bytes 491528 | tf_op jit(solution)/shard_map/ppermute | solution.py:195
  15.1 2.5 %collective-permute-start.2 = (f32[4,40,256]{2,1,0:T(8,128)S(1)}, f32[4,40,256]{2,1,0:T(8,128)S(1)}, u32[]{:S(2)}, u32[]{:S(2)}) collective-permute-start(f32[4,40,256]{2,1,0:T(8,128)S(1)} %constant_dynamic-slice_fusion), channel_id=1, source_target_pairs={{0,1},{1,2},{2,3},{3,0},{4,5},{5,6},{6,7},{7,4},{8,9},{9,10},{10,1... | collective-permute-start | bytes 491528 | tf_op jit(solution)/shard_map/ppermute | solution.py:195
  17.7 0.9 constant_dynamic-slice_fusion.1
  18.7 11.9 %collective-permute-start.1 = (f32[2,40,256]{2,1,0:T(8,128)S(1)}, f32[2,40,256]{2,1,0:T(8,128)S(1)}, u32[]{:S(2)}, u32[]{:S(2)}) collective-permute-start(f32[2,40,256]{2,1,0:T(8,128)S(1)} %get-tuple-element.25), channel_id=1, source_target_pairs={{0,16},{1,31},{2,30},{3,29},{4,28},{5,27},{6,26},{7,25},{8,24},{9,... | collective-permute-start | bytes 245768 | tf_op jit(solution)/shard_map/ppermute | solution.py:207
  30.5 1.9 %collective-permute-start = (f32[2,40,256]{2,1,0:T(8,128)S(1)}, f32[2,40,256]{2,1,0:T(8,128)S(1)}, u32[]{:S(2)}, u32[]{:S(2)}) collective-permute-start(f32[2,40,256]{2,1,0:T(8,128)S(1)} %get-tuple-element.26), channel_id=1, source_target_pairs={{0,0},{1,15},{2,14},{3,13},{4,12},{5,11},{6,10},{7,9},{8,8},{9,7},... | collective-permute-start | bytes 245768 | tf_op jit(solution)/shard_map/ppermute | solution.py:207
  32.5 0.9 convert_reduce_fusion
  33.3 0.1 broadcast_bitcast_fusion
  33.4 1.8 %collective-permute-done.1 = f32[2,40,256]{2,1,0:T(8,128)S(1)} collective-permute-done((f32[2,40,256]{2,1,0:T(8,128)S(1)}, f32[2,40,256]{2,1,0:T(8,128)S(1)}, u32[]{:S(2)}, u32[]{:S(2)}) %collective-permute-start.1) | collective-permute-done | bytes 81952 | tf_op jit(solution)/shard_map/ppermute | solution.py:207
  35.2 1.1 collective-permute-done
  36.3 0.0 collective-permute-done.4
  36.3 0.0 collective-permute-done.3
  36.3 0.0 collective-permute-done.2
  36.3 0.7 pad_maximum_fusion.1
  37.0 0.0 all-gather.3.cloned.1.call-update
  37.0 0.9 fusion.1
  38.0 0.0 copy-start.2
  38.0 0.0 copy-start.3
  38.1 2.2 %collective-permute-start.12 = (f32[4,2,40,256]{3,2,1,0:T(8,128)S(1)}, f32[4,2,40,256]{3,2,1,0:T(8,128)S(1)}, u32[]{:S(2)}, u32[]{:S(2)}) collective-permute-start(f32[4,2,40,256]{3,2,1,0:T(8,128)S(1)} %get-tuple-element.27.refs_1_), channel_id=1, source_target_pairs={{0,28},{4,0},{8,4},{12,8},{16,12},{20,16},{24,20},{28,24},{1,29},{... | collective-permute-start | bytes 983048 | tf_op jit(solution)/shard_map/ppermute | solution.py:195
  40.4 4.0 %collective-permute-start.5 = (f32[4,2,40,256]{3,2,1,0:T(8,128)S(1)}, f32[4,2,40,256]{3,2,1,0:T(8,128)S(1)}, u32[]{:S(2)}, u32[]{:S(2)}) collective-permute-start(f32[4,2,40,256]{3,2,1,0:T(8,128)S(1)} %get-tuple-element.28.refs_0_), channel_id=1, source_target_pairs={{0,4},{4,8},{8,12},{12,16},{16,20},{20,24},{24,28},{28,0},{1,5},{5... | collective-permute-start | bytes 983048 | tf_op jit(solution)/shard_map/ppermute | solution.py:195
  44.4 3.4 %collective-permute-start.6 = (f32[4,2,40,256]{3,2,1,0:T(8,128)S(1)}, f32[4,2,40,256]{3,2,1,0:T(8,128)S(1)}, u32[]{:S(2)}, u32[]{:S(2)}) collective-permute-start(f32[4,2,40,256]{3,2,1,0:T(8,128)S(1)} %get-tuple-element.27.refs_1_), channel_id=1, source_target_pairs={{0,4},{4,8},{8,12},{12,16},{16,20},{20,24},{24,28},{28,0},{1,5},{5... | collective-permute-start | bytes 983048 | tf_op jit(solution)/shard_map/ppermute | solution.py:195
  47.8 3.1 %collective-permute-start.11 = (f32[4,2,40,256]{3,2,1,0:T(8,128)S(1)}, f32[4,2,40,256]{3,2,1,0:T(8,128)S(1)}, u32[]{:S(2)}, u32[]{:S(2)}) collective-permute-start(f32[4,2,40,256]{3,2,1,0:T(8,128)S(1)} %get-tuple-element.28.refs_0_), channel_id=1, source_target_pairs={{0,28},{4,0},{8,4},{12,8},{16,12},{20,16},{24,20},{28,24},{1,29},{... | collective-permute-start | bytes 983048 | tf_op jit(solution)/shard_map/ppermute | solution.py:195
  50.9 0.0 collective-permute-done.12.refs_9_
  50.9 1.9 %collective-permute-start.14 = (f32[4,2,40,256]{3,2,1,0:T(8,128)S(1)}, f32[4,2,40,256]{3,2,1,0:T(8,128)S(1)}, u32[]{:S(2)}, u32[]{:S(2)}) collective-permute-start(f32[4,2,40,256]{3,2,1,0:T(8,128)S(1)} %collective-permute-done.12.refs_9_), channel_id=1, source_target_pairs={{0,28},{4,0},{8,4},{12,8},{16,12},{20,16},{24,20},{28,24},{1,29},{... | collective-permute-start | bytes 983048 | tf_op jit(solution)/shard_map/ppermute | solution.py:195
  52.9 0.0 collective-permute-done.5.refs_2_
  52.9 3.4 %collective-permute-start.7 = (f32[4,2,40,256]{3,2,1,0:T(8,128)S(1)}, f32[4,2,40,256]{3,2,1,0:T(8,128)S(1)}, u32[]{:S(2)}, u32[]{:S(2)}) collective-permute-start(f32[4,2,40,256]{3,2,1,0:T(8,128)S(1)} %collective-permute-done.5.refs_2_), channel_id=1, source_target_pairs={{0,4},{4,8},{8,12},{12,16},{16,20},{20,24},{24,28},{28,0},{1,5},{5... | collective-permute-start | bytes 983048 | tf_op jit(solution)/shard_map/ppermute | solution.py:195
  56.2 1.4 collective-permute-done.6.refs_3_
  57.6 4.1 %collective-permute-start.8 = (f32[4,2,40,256]{3,2,1,0:T(8,128)S(1)}, f32[4,2,40,256]{3,2,1,0:T(8,128)S(1)}, u32[]{:S(2)}, u32[]{:S(2)}) collective-permute-start(f32[4,2,40,256]{3,2,1,0:T(8,128)S(1)} %collective-permute-done.6.refs_3_), channel_id=1, source_target_pairs={{0,4},{4,8},{8,12},{12,16},{16,20},{20,24},{24,28},{28,0},{1,5},{5... | collective-permute-start | bytes 983048 | tf_op jit(solution)/shard_map/ppermute | solution.py:195
  61.7 0.0 collective-permute-done.11.refs_8_
  61.8 2.4 %collective-permute-start.13 = (f32[4,2,40,256]{3,2,1,0:T(8,128)S(1)}, f32[4,2,40,256]{3,2,1,0:T(8,128)S(1)}, u32[]{:S(2)}, u32[]{:S(2)}) collective-permute-start(f32[4,2,40,256]{3,2,1,0:T(8,128)S(1)} %collective-permute-done.11.refs_8_), channel_id=1, source_target_pairs={{0,28},{4,0},{8,4},{12,8},{16,12},{20,16},{24,20},{28,24},{1,29},{... | collective-permute-start | bytes 983048 | tf_op jit(solution)/shard_map/ppermute | solution.py:195
  64.1 0.2 collective-permute-done.14.refs_11_
  64.4 3.9 %collective-permute-start.16 = (f32[4,2,40,256]{3,2,1,0:T(8,128)S(1)}, f32[4,2,40,256]{3,2,1,0:T(8,128)}, u32[]{:S(2)}, u32[]{:S(2)}) collective-permute-start(f32[4,2,40,256]{3,2,1,0:T(8,128)S(1)} %collective-permute-done.14.refs_11_), channel_id=1, source_target_pairs={{0,28},{4,0},{8,4},{12,8},{16,12},{20,16},{24,20},{28,24},{1,29},{... | collective-permute-start | bytes 983048 | tf_op jit(solution)/shard_map/ppermute | solution.py:195
  68.2 0.0 collective-permute-done.7.refs_4_
  68.3 1.9 %collective-permute-start.9 = (f32[4,2,40,256]{3,2,1,0:T(8,128)S(1)}, f32[4,2,40,256]{3,2,1,0:T(8,128)}, u32[]{:S(2)}, u32[]{:S(2)}) collective-permute-start(f32[4,2,40,256]{3,2,1,0:T(8,128)S(1)} %collective-permute-done.7.refs_4_), channel_id=1, source_target_pairs={{0,4},{4,8},{8,12},{12,16},{16,20},{20,24},{24,28},{28,0},{1,5},{5... | collective-permute-start | bytes 983048 | tf_op jit(solution)/shard_map/ppermute | solution.py:195
  70.2 1.5 collective-permute-done.8.refs_5_
  71.7 4.2 %collective-permute-start.10 = (f32[4,2,40,256]{3,2,1,0:T(8,128)S(1)}, f32[4,2,40,256]{3,2,1,0:T(8,128)}, u32[]{:S(2)}, u32[]{:S(2)}) collective-permute-start(f32[4,2,40,256]{3,2,1,0:T(8,128)S(1)} %collective-permute-done.8.refs_5_), channel_id=1, source_target_pairs={{0,4},{4,8},{8,12},{12,16},{16,20},{20,24},{24,28},{28,0},{1,5},{5... | collective-permute-start | bytes 983048 | tf_op jit(solution)/shard_map/ppermute | solution.py:195
  75.9 0.0 collective-permute-done.13.refs_10_
  75.9 2.3 %collective-permute-start.15 = (f32[4,2,40,256]{3,2,1,0:T(8,128)S(1)}, f32[4,2,40,256]{3,2,1,0:T(8,128)}, u32[]{:S(2)}, u32[]{:S(2)}) collective-permute-start(f32[4,2,40,256]{3,2,1,0:T(8,128)S(1)} %collective-permute-done.13.refs_10_), channel_id=1, source_target_pairs={{0,28},{4,0},{8,4},{12,8},{16,12},{20,16},{24,20},{28,24},{1,29},{... | collective-permute-start | bytes 983048 | tf_op jit(solution)/shard_map/ppermute | solution.py:195
  78.2 0.0 collective-permute-done.16.refs_13_
  78.2 1.9 %collective-permute-start.18 = (f32[4,2,40,256]{3,2,1,0:T(8,128)}, f32[4,2,40,256]{3,2,1,0:T(8,128)}, u32[]{:S(2)}, u32[]{:S(2)}) collective-permute-start(f32[4,2,40,256]{3,2,1,0:T(8,128)} %collective-permute-done.16.refs_13_), channel_id=1, source_target_pairs={{0,28},{4,0},{8,4},{12,8},{16,12},{20,16},{24,20},{28,24},{1,29},{... | collective-permute-start | bytes 983048 | tf_op jit(solution)/shard_map/ppermute | solution.py:195
  80.1 0.0 collective-permute-done.9.refs_6_
  80.1 3.4 %collective-permute-start.17 = (f32[4,2,40,256]{3,2,1,0:T(8,128)}, f32[4,2,40,256]{3,2,1,0:T(8,128)}, u32[]{:S(2)}, u32[]{:S(2)}) collective-permute-start(f32[4,2,40,256]{3,2,1,0:T(8,128)} %collective-permute-done.9.refs_6_), channel_id=1, source_target_pairs={{0,4},{4,8},{8,12},{12,16},{16,20},{20,24},{24,28},{28,0},{1,5},{5... | collective-permute-start | bytes 983048 | tf_op jit(solution)/shard_map/ppermute | solution.py:195
  83.5 0.1 stack.38.place
  83.6 0.0 all-gather.3.cloned.1.call-done
  83.6 0.0 copy-done.1
  83.6 0.0 copy-start
  83.6 1.8 %copy-done = f32[2688,256]{1,0:T(8,128)S(1)} copy-done((f32[2688,256]{1,0:T(8,128)S(1)}, f32[2688,256]{1,0:T(8,128)}, u32[]{:S(2)}) %copy-start) | copy-done | bytes 2752536
  85.4 2.4 %own_rows.1 = (bf16[512,1024]{1,0:T(8,128)(2,1)S(1)}, bf16[512,1024]{1,0:T(8,128)(2,1)S(1)}, f32[2,8,256]{2,1,0:T(8,128)S(1)}) custom-call(s32[5]{0:T(128)S(1)} %stack.38.place, s32[32]{0:T(128)S(1)} %copy-done.1, f32[16,168,256]{2,1,0:T(8,128)S(1)} %bitcast.16), custom_call_target="tpu_custom_call" | custom-call | tf_op jit(solution)/shard_map/own_rows/pallas_call | solution.py:151
  87.8 0.0 collective-permute-done.10.refs_7_
  87.8 0.0 collective-permute-done.15.refs_12_
  87.8 3.1 %collective-permute-done.18.refs_15_ = f32[4,2,40,256]{3,2,1,0:T(8,128)} collective-permute-done((f32[4,2,40,256]{3,2,1,0:T(8,128)}, f32[4,2,40,256]{3,2,1,0:T(8,128)}, u32[]{:S(2)}, u32[]{:S(2)}) %collective-permute-start.18) | collective-permute-done | bytes 327712 | tf_op jit(solution)/shard_map/ppermute | solution.py:195
  90.9 1.2 collective-permute-done.17.refs_14_
  92.2 0.0 copy-done.2
  92.2 0.0 copy-done.3
  92.2 15.4 %pairs.1 = (f32[8,2,64,256]{3,2,1,0:T(8,128)S(1)}, f32[8,2,64,256]{3,2,1,0:T(8,128)S(1)}) custom-call(s32[5]{0:T(128)S(1)} %stack.38.place, s32[32]{0:T(128)S(1)} %copy-done.1, f32[64]{0:T(128)S(1)} %copy-done.3, bf16[512,1024]{1,0:T(8,128)(2,1)S(1)} %get-tuple-element.17.own_hi_any, bf16[512,1024]{1,0:T(8,128)(2,1)S(1)} %get-tuple-element.18.own_lo_any, ...), custom_call_target="tpu_custom_call" | custom-call | tf_op jit(solution)/shard_map/pairs/pallas_call | solution.py:165
  107.5 6.6 %collective-permute-start.19 = (f32[8,2,64,256]{3,2,1,0:T(8,128)S(1)}, f32[8,2,64,256]{3,2,1,0:T(8,128)S(1)}, u32[]{:S(2)}, u32[]{:S(2)}) collective-permute-start(f32[8,2,64,256]{3,2,1,0:T(8,128)S(1)} %get-tuple-element.24), channel_id=1, source_target_pairs={{0,32},{32,0},{1,33},{33,1},{2,34},{34,2},{3,35},{35,3},{4,36},{36... | collective-permute-start | bytes 3145736 | tf_op jit(solution)/shard_map/ppermute | solution.py:227
  114.1 2.3 %collective-permute-done.19 = f32[8,2,64,256]{3,2,1,0:T(8,128)S(1)} collective-permute-done((f32[8,2,64,256]{3,2,1,0:T(8,128)S(1)}, f32[8,2,64,256]{3,2,1,0:T(8,128)S(1)}, u32[]{:S(2)}, u32[]{:S(2)}) %collective-permute-start.19) | collective-permute-done | bytes 1048608 | tf_op jit(solution)/shard_map/ppermute | solution.py:227
  116.4 0.1 add.45
  116.5 36.2 %all_to_all.5 = f32[8,2,64,256]{3,2,1,0:T(8,128)S(1)} all-to-all(f32[8,2,64,256]{3,2,1,0:T(8,128)S(1)} %add.45), channel_id=1, replica_groups=mesh['y'=8,'c'=2,'z'=8,'x'=4] {'y'}, dimensions={0} | all-to-all | bytes 2097152 | tf_op jit(solution)/shard_map/all_to_all | solution.py:228
  152.7 0.7 reduce_sum.9
  (3 shorter events, 0.1 us)
Async XLA Ops:
  6.5 77.1 %copy-start.1 = (s32[32]{0:T(128)S(1)}, s32[32]{0:T(128)}, u32[]{:S(2)}) copy-start(s32[32]{0:T(128)} %counts.3) | copy-start | bytes 388
  6.5 77.1 %all-gather.3.cloned.1.call-start = ((), (), s32[]{:S(2)}) async-start(), calls=%async_computation.1 | async-start | bytes 2924544 | tf_op jit(solution)/shard_map/all_gather | solution.py:215
  7.5 28.8 %collective-permute-start.4 = (f32[4,40,256]{2,1,0:T(8,128)S(1)}, f32[4,40,256]{2,1,0:T(8,128)S(1)}, u32[]{:S(2)}, u32[]{:S(2)}) collective-permute-start(f32[4,40,256]{2,1,0:T(8,128)S(1)} %constant_dynamic-slice_fusion), channel_id=1, source_target_pairs={{0,3},{1,0},{2,1},{3,2},{4,7},{5,4},{6,5},{7,6},{8,11},{9,8},{10,9... | collective-permute-start | bytes 491528 | tf_op jit(solution)/shard_map/ppermute | solution.py:195
  12.7 23.6 %collective-permute-start.3 = (f32[4,40,256]{2,1,0:T(8,128)S(1)}, f32[4,40,256]{2,1,0:T(8,128)S(1)}, u32[]{:S(2)}, u32[]{:S(2)}) collective-permute-start(f32[4,40,256]{2,1,0:T(8,128)S(1)} %constant_dynamic-slice_fusion), channel_id=1, source_target_pairs={{0,2},{1,3},{2,0},{3,1},{4,6},{5,7},{6,4},{7,5},{8,10},{9,11},{10,... | collective-permute-start | bytes 491528 | tf_op jit(solution)/shard_map/ppermute | solution.py:195
  15.1 21.2 %collective-permute-start.2 = (f32[4,40,256]{2,1,0:T(8,128)S(1)}, f32[4,40,256]{2,1,0:T(8,128)S(1)}, u32[]{:S(2)}, u32[]{:S(2)}) collective-permute-start(f32[4,40,256]{2,1,0:T(8,128)S(1)} %constant_dynamic-slice_fusion), channel_id=1, source_target_pairs={{0,1},{1,2},{2,3},{3,0},{4,5},{5,6},{6,7},{7,4},{8,9},{9,10},{10,1... | collective-permute-start | bytes 491528 | tf_op jit(solution)/shard_map/ppermute | solution.py:195
  18.7 16.5 %collective-permute-start.1 = (f32[2,40,256]{2,1,0:T(8,128)S(1)}, f32[2,40,256]{2,1,0:T(8,128)S(1)}, u32[]{:S(2)}, u32[]{:S(2)}) collective-permute-start(f32[2,40,256]{2,1,0:T(8,128)S(1)} %get-tuple-element.25), channel_id=1, source_target_pairs={{0,16},{1,31},{2,30},{3,29},{4,28},{5,27},{6,26},{7,25},{8,24},{9,... | collective-permute-start | bytes 245768 | tf_op jit(solution)/shard_map/ppermute | solution.py:207
  30.5 5.7 %collective-permute-start = (f32[2,40,256]{2,1,0:T(8,128)S(1)}, f32[2,40,256]{2,1,0:T(8,128)S(1)}, u32[]{:S(2)}, u32[]{:S(2)}) collective-permute-start(f32[2,40,256]{2,1,0:T(8,128)S(1)} %get-tuple-element.26), channel_id=1, source_target_pairs={{0,0},{1,15},{2,14},{3,13},{4,12},{5,11},{6,10},{7,9},{8,8},{9,7},... | collective-permute-start | bytes 245768 | tf_op jit(solution)/shard_map/ppermute | solution.py:207
  38.0 54.2 %copy-start.2 = (f32[256]{0:T(256)S(1)}, f32[256]{0:T(256)}, u32[]{:S(2)}) copy-start(f32[256]{0:T(256)} %param.8) | copy-start | bytes 3076
  38.0 54.2 %copy-start.3 = (f32[64]{0:T(128)S(1)}, f32[64]{0:T(128)}, u32[]{:S(2)}) copy-start(f32[64]{0:T(128)} %occ.1) | copy-start | bytes 772
  38.1 12.8 %collective-permute-start.12 = (f32[4,2,40,256]{3,2,1,0:T(8,128)S(1)}, f32[4,2,40,256]{3,2,1,0:T(8,128)S(1)}, u32[]{:S(2)}, u32[]{:S(2)}) collective-permute-start(f32[4,2,40,256]{3,2,1,0:T(8,128)S(1)} %get-tuple-element.27.refs_1_), channel_id=1, source_target_pairs={{0,28},{4,0},{8,4},{12,8},{16,12},{20,16},{24,20},{28,24},{1,29},{... | collective-permute-start | bytes 983048 | tf_op jit(solution)/shard_map/ppermute | solution.py:195
  40.4 12.5 %collective-permute-start.5 = (f32[4,2,40,256]{3,2,1,0:T(8,128)S(1)}, f32[4,2,40,256]{3,2,1,0:T(8,128)S(1)}, u32[]{:S(2)}, u32[]{:S(2)}) collective-permute-start(f32[4,2,40,256]{3,2,1,0:T(8,128)S(1)} %get-tuple-element.28.refs_0_), channel_id=1, source_target_pairs={{0,4},{4,8},{8,12},{12,16},{16,20},{20,24},{24,28},{28,0},{1,5},{5... | collective-permute-start | bytes 983048 | tf_op jit(solution)/shard_map/ppermute | solution.py:195
  44.4 13.2 %collective-permute-start.6 = (f32[4,2,40,256]{3,2,1,0:T(8,128)S(1)}, f32[4,2,40,256]{3,2,1,0:T(8,128)S(1)}, u32[]{:S(2)}, u32[]{:S(2)}) collective-permute-start(f32[4,2,40,256]{3,2,1,0:T(8,128)S(1)} %get-tuple-element.27.refs_1_), channel_id=1, source_target_pairs={{0,4},{4,8},{8,12},{12,16},{16,20},{20,24},{24,28},{28,0},{1,5},{5... | collective-permute-start | bytes 983048 | tf_op jit(solution)/shard_map/ppermute | solution.py:195
  47.8 14.0 %collective-permute-start.11 = (f32[4,2,40,256]{3,2,1,0:T(8,128)S(1)}, f32[4,2,40,256]{3,2,1,0:T(8,128)S(1)}, u32[]{:S(2)}, u32[]{:S(2)}) collective-permute-start(f32[4,2,40,256]{3,2,1,0:T(8,128)S(1)} %get-tuple-element.28.refs_0_), channel_id=1, source_target_pairs={{0,28},{4,0},{8,4},{12,8},{16,12},{20,16},{24,20},{28,24},{1,29},{... | collective-permute-start | bytes 983048 | tf_op jit(solution)/shard_map/ppermute | solution.py:195
  50.9 13.4 %collective-permute-start.14 = (f32[4,2,40,256]{3,2,1,0:T(8,128)S(1)}, f32[4,2,40,256]{3,2,1,0:T(8,128)S(1)}, u32[]{:S(2)}, u32[]{:S(2)}) collective-permute-start(f32[4,2,40,256]{3,2,1,0:T(8,128)S(1)} %collective-permute-done.12.refs_9_), channel_id=1, source_target_pairs={{0,28},{4,0},{8,4},{12,8},{16,12},{20,16},{24,20},{28,24},{1,29},{... | collective-permute-start | bytes 983048 | tf_op jit(solution)/shard_map/ppermute | solution.py:195
  52.9 15.4 %collective-permute-start.7 = (f32[4,2,40,256]{3,2,1,0:T(8,128)S(1)}, f32[4,2,40,256]{3,2,1,0:T(8,128)S(1)}, u32[]{:S(2)}, u32[]{:S(2)}) collective-permute-start(f32[4,2,40,256]{3,2,1,0:T(8,128)S(1)} %collective-permute-done.5.refs_2_), channel_id=1, source_target_pairs={{0,4},{4,8},{8,12},{12,16},{16,20},{20,24},{24,28},{28,0},{1,5},{5... | collective-permute-start | bytes 983048 | tf_op jit(solution)/shard_map/ppermute | solution.py:195
  57.6 14.0 %collective-permute-start.8 = (f32[4,2,40,256]{3,2,1,0:T(8,128)S(1)}, f32[4,2,40,256]{3,2,1,0:T(8,128)S(1)}, u32[]{:S(2)}, u32[]{:S(2)}) collective-permute-start(f32[4,2,40,256]{3,2,1,0:T(8,128)S(1)} %collective-permute-done.6.refs_3_), channel_id=1, source_target_pairs={{0,4},{4,8},{8,12},{12,16},{16,20},{20,24},{24,28},{28,0},{1,5},{5... | collective-permute-start | bytes 983048 | tf_op jit(solution)/shard_map/ppermute | solution.py:195
  61.8 14.1 %collective-permute-start.13 = (f32[4,2,40,256]{3,2,1,0:T(8,128)S(1)}, f32[4,2,40,256]{3,2,1,0:T(8,128)S(1)}, u32[]{:S(2)}, u32[]{:S(2)}) collective-permute-start(f32[4,2,40,256]{3,2,1,0:T(8,128)S(1)} %collective-permute-done.11.refs_8_), channel_id=1, source_target_pairs={{0,28},{4,0},{8,4},{12,8},{16,12},{20,16},{24,20},{28,24},{1,29},{... | collective-permute-start | bytes 983048 | tf_op jit(solution)/shard_map/ppermute | solution.py:195
  64.4 13.8 %collective-permute-start.16 = (f32[4,2,40,256]{3,2,1,0:T(8,128)S(1)}, f32[4,2,40,256]{3,2,1,0:T(8,128)}, u32[]{:S(2)}, u32[]{:S(2)}) collective-permute-start(f32[4,2,40,256]{3,2,1,0:T(8,128)S(1)} %collective-permute-done.14.refs_11_), channel_id=1, source_target_pairs={{0,28},{4,0},{8,4},{12,8},{16,12},{20,16},{24,20},{28,24},{1,29},{... | collective-permute-start | bytes 983048 | tf_op jit(solution)/shard_map/ppermute | solution.py:195
  68.3 11.9 %collective-permute-start.9 = (f32[4,2,40,256]{3,2,1,0:T(8,128)S(1)}, f32[4,2,40,256]{3,2,1,0:T(8,128)}, u32[]{:S(2)}, u32[]{:S(2)}) collective-permute-start(f32[4,2,40,256]{3,2,1,0:T(8,128)S(1)} %collective-permute-done.7.refs_4_), channel_id=1, source_target_pairs={{0,4},{4,8},{8,12},{12,16},{16,20},{20,24},{24,28},{28,0},{1,5},{5... | collective-permute-start | bytes 983048 | tf_op jit(solution)/shard_map/ppermute | solution.py:195
  71.7 16.1 %collective-permute-start.10 = (f32[4,2,40,256]{3,2,1,0:T(8,128)S(1)}, f32[4,2,40,256]{3,2,1,0:T(8,128)}, u32[]{:S(2)}, u32[]{:S(2)}) collective-permute-start(f32[4,2,40,256]{3,2,1,0:T(8,128)S(1)} %collective-permute-done.8.refs_5_), channel_id=1, source_target_pairs={{0,4},{4,8},{8,12},{12,16},{16,20},{20,24},{24,28},{28,0},{1,5},{5... | collective-permute-start | bytes 983048 | tf_op jit(solution)/shard_map/ppermute | solution.py:195
  75.9 11.9 %collective-permute-start.15 = (f32[4,2,40,256]{3,2,1,0:T(8,128)S(1)}, f32[4,2,40,256]{3,2,1,0:T(8,128)}, u32[]{:S(2)}, u32[]{:S(2)}) collective-permute-start(f32[4,2,40,256]{3,2,1,0:T(8,128)S(1)} %collective-permute-done.13.refs_10_), channel_id=1, source_target_pairs={{0,28},{4,0},{8,4},{12,8},{16,12},{20,16},{24,20},{28,24},{1,29},{... | collective-permute-start | bytes 983048 | tf_op jit(solution)/shard_map/ppermute | solution.py:195
  78.2 12.7 %collective-permute-start.18 = (f32[4,2,40,256]{3,2,1,0:T(8,128)}, f32[4,2,40,256]{3,2,1,0:T(8,128)}, u32[]{:S(2)}, u32[]{:S(2)}) collective-permute-start(f32[4,2,40,256]{3,2,1,0:T(8,128)} %collective-permute-done.16.refs_13_), channel_id=1, source_target_pairs={{0,28},{4,0},{8,4},{12,8},{16,12},{20,16},{24,20},{28,24},{1,29},{... | collective-permute-start | bytes 983048 | tf_op jit(solution)/shard_map/ppermute | solution.py:195
  80.1 12.0 %collective-permute-start.17 = (f32[4,2,40,256]{3,2,1,0:T(8,128)}, f32[4,2,40,256]{3,2,1,0:T(8,128)}, u32[]{:S(2)}, u32[]{:S(2)}) collective-permute-start(f32[4,2,40,256]{3,2,1,0:T(8,128)} %collective-permute-done.9.refs_6_), channel_id=1, source_target_pairs={{0,4},{4,8},{8,12},{12,16},{16,20},{20,24},{24,28},{28,0},{1,5},{5... | collective-permute-start | bytes 983048 | tf_op jit(solution)/shard_map/ppermute | solution.py:195
  83.6 1.8 %copy-start = (f32[2688,256]{1,0:T(8,128)S(1)}, f32[2688,256]{1,0:T(8,128)}, u32[]{:S(2)}) copy-start(f32[2688,256]{1,0:T(8,128)} %all-gather.3.cloned.1.call-done) | copy-start | bytes 8257540
  107.5 8.9 %collective-permute-start.19 = (f32[8,2,64,256]{3,2,1,0:T(8,128)S(1)}, f32[8,2,64,256]{3,2,1,0:T(8,128)S(1)}, u32[]{:S(2)}, u32[]{:S(2)}) collective-permute-start(f32[8,2,64,256]{3,2,1,0:T(8,128)S(1)} %get-tuple-element.24), channel_id=1, source_target_pairs={{0,32},{32,0},{1,33},{33,1},{2,34},{34,2},{3,35},{35,3},{4,36},{36... | collective-permute-start | bytes 3145736 | tf_op jit(solution)/shard_map/ppermute | solution.py:227
Sparse Core Ops, SparseCore 0:
  37.2 45.1 all-gather.2

commit v7 on v4

--- a/solution.py
+++ b/solution.py
@@ -89,16 +89,27 @@
         turn(n, 0)
 
 
-def pair_kernel(place, counts, occ, own_hi_any, own_lo_any, times, virt, wide_any,
-                theirs_ref, mine_ref, own_hi, own_lo, rows, dense, w_hi, w_lo, x_hi, x_lo, sems):
+def pair_kernel(place, counts, occ, own_hi_any, own_lo_any, times, virt, most_any, *refs):
+    rest, refs = refs[:NZ], refs[NZ:]
+    theirs_ref, mine_ref, own_hi, own_lo, rows, dense, w_hi, w_lo, x_hi, x_lo, sems = refs
     core, u, grp = place[0], place[1], place[2]
-    row_copies = [pltpu.make_async_copy(wide_any.at[z], rows.at[z], sems.at[z]) for z in range(NZ)]
+    row_copies = [
+        pltpu.make_async_copy(most_any.at[z], rows.at[z, :, pl.ds(0, 3)], sems.at[z]) for z in range(NZ)
+    ]
+    rest_copies = [
+        pltpu.make_async_copy(
+            rest[n], rows.at[lax.rem(place[3] + d + NZ, NZ), :, pl.ds(3, 1)], sems.at[NZ + 2 + n]
+        )
+        for n, d in enumerate((0, -1, -2, -3, -4, 1, 2, 3))
+    ]
     own_copies = [
         pltpu.make_async_copy(own_hi_any, own_hi, sems.at[NZ]),
         pltpu.make_async_copy(own_lo_any, own_lo, sems.at[NZ + 1]),
     ]
-    for copy in row_copies + own_copies:
+    for copy in rest_copies + row_copies + own_copies:
         copy.start()
+    for copy in rest_copies:
+        copy.wait()
 
     off = jnp.int32(0)
     for z in range(NZ):
@@ -157,12 +168,12 @@
     )(place, counts, own_pay, other_pay)
 
 
-def pairs(place, counts, occ_energy, own_hi, own_lo, times, virt, wide_all):
+def pairs(place, counts, occ_energy, own_hi, own_lo, times, virt, most, rest):
     part = jax.ShapeDtypeStruct((NY, OCC_DEV, BLK, V), jnp.float32)
     return pl.pallas_call(
         pair_kernel,
         out_shape=[part, part],
-        in_specs=[SMEM] * 3 + [HBM, HBM, VMEM, VMEM, HBM],
+        in_specs=[SMEM] * 3 + [HBM, HBM, VMEM, VMEM] + [HBM] * (1 + NZ),
         out_specs=[VMEM, VMEM],
         scratch_shapes=[
             pltpu.VMEM((OCC_DEV * V, NAUX), jnp.bfloat16),
@@ -173,21 +184,22 @@
             pltpu.VMEM((NAUX, 4 * V), jnp.bfloat16),
             pltpu.VMEM((4 * V, OCC_DEV * V), jnp.bfloat16),
             pltpu.VMEM((4 * V, OCC_DEV * V), jnp.bfloat16),
-            pltpu.SemaphoreType.DMA((NZ + 2,)),
+            pltpu.SemaphoreType.DMA((2 * NZ + 2,)),
         ],
-        compiler_params=pltpu.CompilerParams(vmem_limit_bytes=48 * MIB),
+        compiler_params=pltpu.CompilerParams(vmem_limit_bytes=50 * MIB),
         name="pairs",
-    )(place, counts, occ_energy, own_hi, own_lo, times, virt, wide_all)
+    )(place, counts, occ_energy, own_hi, own_lo, times, virt, most, *rest)
 
 
 def per_device(three_center, counts, occ_energy, virt_energy, match_tables):
     y, c = lax.axis_index("y"), lax.axis_index("c")
     z, x = lax.axis_index("z"), lax.axis_index("x")
     grp, pos = y * NC + c, z * NX + x
-    place = jnp.stack([c, pos, grp]).astype(jnp.int32)
+    place = jnp.stack([c, pos, grp, z]).astype(jnp.int32)
 
     wide_part = lax.dynamic_slice_in_dim(three_center, 4 * grp, 4, 0)
-    wide_all = lax.all_gather(lax.all_gather(wide_part, "x"), "z")
+    row = lax.all_gather(wide_part, "x")
+    most = lax.all_gather(row[:, :3], "z")
 
     axes = ("y", "c", "z", "x")
     got = []
@@ -204,10 +216,23 @@
     load = jnp.concatenate(got + [note], axis=0)
     sent = jnp.broadcast_to(load[None], (NY, 4 * CAP + 8, V))
     own_pay = lax.all_to_all(sent, "y", split_axis=0, concat_axis=0, tiled=True)
+
+    def along_z(a, d):
+        return lax.ppermute(a, "z", [(k, (k + d) % NZ) for k in range(NZ)])
+
+    up, down = [row[:, 3:]], [row[:, 3:]]
+    for step in range(3):
+        up.append(along_z(up[-1], 1))
+        down.append(along_z(down[-1], -1))
+        if step == 1:
+            own_pay, up[2], down[2] = lax.optimization_barrier((own_pay, up[2], down[2]))
+    up.append(along_z(up[-1], 1))
+    rest = (*up, *down[1:])
+
     other_pay = lax.ppermute(own_pay, "c", [(0, 1), (1, 0)])
 
     own_hi, own_lo, times = own_rows(place, counts, own_pay, other_pay)
-    theirs, mine = pairs(place, counts, occ_energy, own_hi, own_lo, times, virt_energy.reshape(1, V), wide_all)
+    theirs, mine = pairs(place, counts, occ_energy, own_hi, own_lo, times, virt_energy.reshape(1, V), most, rest)
 
     mine = mine + lax.ppermute(theirs, "c", [(0, 1), (1, 0)])
     pieces = lax.all_to_all(mine, "y", split_axis=0, concat_axis=0, tiled=True)

time: 153 us -> 162 us (1.059)
  blocking collectives: 81.5 us -> 43 us
  starting transfers between devices: 24.5 us -> 59.1 us
  waiting for transfers between devices: 15.9 us -> 25.5 us
  local copies, waits for them, and re-layouts: 2.05 us -> 5.94 us
    all_to_all x1 -> x0, blocking collectives: 34.6 us -> none  [per_device(): own_pay = lax.all_to_all(sent, 'y', split_axis=0, concat_axis=0, tiled=True)]
    ppermute x0 -> x7, starting transfers between devices: none -> 29.6 us  [along_z(): return lax.ppermute(a, 'z', [(k, (k + d) % NZ) for k in range(NZ)])]
    ppermute x0 -> x7, waiting for transfers between devices: none -> 14.6 us  [along_z(): return lax.ppermute(a, 'z', [(k, (k + d) % NZ) for k in range(NZ)])]
    all_gather x1, waiting for transfers between devices: 6.83 us -> 0.01 us  [per_device(): most = lax.all_gather(row[:, :3], 'z')]
    all_to_all x0 -> x1, starting transfers between devices: none -> 4.07 us  [per_device(): own_pay = lax.all_to_all(sent, 'y', split_axis=0, concat_axis=0, tiled=True)]
    all_to_all x0 -> x1, waiting for transfers between devices: none -> 3.78 us  [per_device(): own_pay = lax.all_to_all(sent, 'y', split_axis=0, concat_axis=0, tiled=True)]
    ppermute x1, waiting for transfers between devices: 2.65 us -> 0.01 us  [per_device(): other_pay = lax.ppermute(own_pay, 'c', [(0, 1), (1, 0)])]
    all_to_all x1, blocking collectives: 34.2 us -> 31.6 us  [per_device(): pieces = lax.all_to_all(mine, 'y', split_axis=0, concat_axis=0, tiled=True)]
  transfers between devices with their start and end apart: 5 -> 13, of which waited for: 4 -> 8; matrix products, arithmetic and copies ran while one was open for 1% -> 2% of each run, Pallas kernels for 2% -> 2%
where the time goes in v7:
time: 162 us
  starting transfers between devices  59.1 us (36%)
  blocking collectives  43 us (27%)
  waiting for transfers between devices  25.5 us (16%)
  between operations  13.6 us (8%)
  Pallas kernels  13.5 us (8%)
  local copies, waits for them, and re-layouts  5.94 us (4%)
    all_to_all x1, blocking collectives, per_device(): pieces = lax.all_to_all(mine, 'y', split_axis=0, concat_axis=0, tiled=True)  31.6 us
    ppermute x7, starting transfers between devices, along_z(): return lax.ppermute(a, 'z', [(k, (k + d) % NZ) for k in range(NZ)])  29.6 us
    ppermute x2, starting transfers between devices, per_device(): got.append(lax.ppermute(piece, axes, perm).reshape(OCC_DEV * CAP, V))  15 us
    ppermute x7, waiting for transfers between devices, along_z(): return lax.ppermute(a, 'z', [(k, (k + d) % NZ) for k in range(NZ)])  14.6 us
    all_gather x1, blocking collectives, per_device(): row = lax.all_gather(wide_part, 'x')  11.3 us
    pallas_call x1, Pallas kernels, pairs(): pl.pallas_call(pair_kernel, out_shape=[part, part], in_specs=[SMEM] * 3 +...  10.6 us
    ppermute x1, starting transfers between devices, per_device(): other_pay = lax.ppermute(own_pay, 'c', [(0, 1), (1, 0)])  6.99 us
    ppermute x2, waiting for transfers between devices, per_device(): got.append(lax.ppermute(piece, axes, perm).reshape(OCC_DEV * CAP, V))  4.86 us
  transfers between devices with their start and end apart: 13, of which 8 were waited for; matrix products, arithmetic and copies ran while one was open for 2% of the time, Pallas kernels for 2%

profile of v7, /device:TPU:1, one launch (start us, length us, event | category | flops | bytes accessed | tf_op | source)
XLA Modules:
  0.0 161.8 jit_solution(14046781671094634338)
XLA Ops:
  6.5 0.0 copy-start.5
  6.5 0.0 all-gather.4.cloned.1.call-start
  6.5 0.9 constant_dynamic-slice_fusion
  7.5 11.3 %all-gather = f32[16,40,256]{2,1,0:T(8,128)S(1)} all-gather(f32[4,40,256]{2,1,0:T(8,128)S(1)} %constant_dynamic-slice_fusion), channel_id=2, replica_groups=mesh['y'=8,'c'=2,'z'=8,'x'=4] {'x'}, dimensions={0}, use_global_device_ids=true | all-gather | bytes 819200 | tf_op jit(solution)/shard_map/all_gather | solution.py:201
  18.8 0.8 slice.10
  19.6 0.0 all-gather.4.cloned.1.call-update
  19.7 0.0 copy-start.2
  19.7 0.9 constant_dynamic-slice_fusion.2
  20.7 2.8 %collective-permute-start = (f32[2,40,256]{2,1,0:T(8,128)S(1)}, f32[2,40,256]{2,1,0:T(8,128)S(1)}, u32[]{:S(2)}, u32[]{:S(2)}) collective-permute-start(f32[2,40,256]{2,1,0:T(8,128)S(1)} %get-tuple-element.21), channel_id=1, source_target_pairs={{0,0},{1,15},{2,14},{3,13},{4,12},{5,11},{6,10},{7,9},{8,8},{9,7},... | collective-permute-start | bytes 245768 | tf_op jit(solution)/shard_map/ppermute | solution.py:213
  23.5 12.2 %collective-permute-start.1 = (f32[2,40,256]{2,1,0:T(8,128)S(1)}, f32[2,40,256]{2,1,0:T(8,128)S(1)}, u32[]{:S(2)}, u32[]{:S(2)}) collective-permute-start(f32[2,40,256]{2,1,0:T(8,128)S(1)} %get-tuple-element.22), channel_id=1, source_target_pairs={{0,16},{1,31},{2,30},{3,29},{4,28},{5,27},{6,26},{7,25},{8,24},{9,... | collective-permute-start | bytes 245768 | tf_op jit(solution)/shard_map/ppermute | solution.py:213
  35.7 0.0 copy-done.5
  35.7 0.2 convert_reduce_fusion
  35.9 0.1 broadcast_bitcast_fusion
  36.0 0.0 collective-permute-done
  36.0 4.9 %collective-permute-done.1 = f32[2,40,256]{2,1,0:T(8,128)S(1)} collective-permute-done((f32[2,40,256]{2,1,0:T(8,128)S(1)}, f32[2,40,256]{2,1,0:T(8,128)S(1)}, u32[]{:S(2)}, u32[]{:S(2)}) %collective-permute-start.1) | collective-permute-done | bytes 81952 | tf_op jit(solution)/shard_map/ppermute | solution.py:213
  40.9 1.2 broadcast_in_dim.19
  42.0 0.0 copy-start.3
  42.0 0.0 copy-start.4
  42.0 4.1 %all-to-all-start = ((f32[8,168,256]{2,1,0:T(8,128)}), f32[8,168,256]{2,1,0:T(8,128)S(1)}, u32[]{:S(2)}, u32[]{:S(2)}) async-start(f32[8,168,256]{2,1,0:T(8,128)} %broadcast_in_dim.19), calls=%async_computation | async-start | bytes 2752512 | tf_op jit(solution)/shard_map/all_to_all | solution.py:218
  46.1 3.1 %collective-permute-start.2 = (f32[4,1,40,256]{3,2,1,0:T(8,128)S(1)}, f32[4,1,40,256]{3,2,1,0:T(8,128)S(1)}, u32[]{:S(2)}, u32[]{:S(2)}) collective-permute-start(f32[4,1,40,256]{3,2,1,0:T(8,128)S(1)} %slice.9.refs_0_), channel_id=1, source_target_pairs={{0,4},{4,8},{8,12},{12,16},{16,20},{20,24},{24,28},{28,0},{1,5},{5... | collective-permute-start | bytes 491528 | tf_op jit(solution)/shard_map/ppermute | solution.py:221
  49.2 7.5 %collective-permute-start.4 = (f32[4,1,40,256]{3,2,1,0:T(8,128)S(1)}, f32[4,1,40,256]{3,2,1,0:T(8,128)S(1)}, u32[]{:S(2)}, u32[]{:S(2)}) collective-permute-start(f32[4,1,40,256]{3,2,1,0:T(8,128)S(1)} %slice.9.refs_0_), channel_id=1, source_target_pairs={{0,28},{4,0},{8,4},{12,8},{16,12},{20,16},{24,20},{28,24},{1,29},{... | collective-permute-start | bytes 491528 | tf_op jit(solution)/shard_map/ppermute | solution.py:221
  56.8 5.1 %collective-permute-done.2.refs_1_ = f32[4,1,40,256]{3,2,1,0:T(8,128)S(1)} collective-permute-done((f32[4,1,40,256]{3,2,1,0:T(8,128)S(1)}, f32[4,1,40,256]{3,2,1,0:T(8,128)S(1)}, u32[]{:S(2)}, u32[]{:S(2)}) %collective-permute-start.2) | collective-permute-done | bytes 163872 | tf_op jit(solution)/shard_map/ppermute | solution.py:221
  61.8 1.9 %collective-permute-start.3 = (f32[4,1,40,256]{3,2,1,0:T(8,128)S(1)}, f32[4,1,40,256]{3,2,1,0:T(8,128)S(1)}, u32[]{:S(2)}, u32[]{:S(2)}) collective-permute-start(f32[4,1,40,256]{3,2,1,0:T(8,128)S(1)} %collective-permute-done.2.refs_1_), channel_id=1, source_target_pairs={{0,4},{4,8},{8,12},{12,16},{16,20},{20,24},{24,28},{28,0},{1,5},{5... | collective-permute-start | bytes 491528 | tf_op jit(solution)/shard_map/ppermute | solution.py:221
  63.8 0.0 collective-permute-done.4.refs_5_
  63.8 4.6 %collective-permute-start.5 = (f32[4,1,40,256]{3,2,1,0:T(8,128)S(1)}, f32[4,1,40,256]{3,2,1,0:T(8,128)S(1)}, u32[]{:S(2)}, u32[]{:S(2)}) collective-permute-start(f32[4,1,40,256]{3,2,1,0:T(8,128)S(1)} %collective-permute-done.4.refs_5_), channel_id=1, source_target_pairs={{0,28},{4,0},{8,4},{12,8},{16,12},{20,16},{24,20},{28,24},{1,29},{... | collective-permute-start | bytes 491528 | tf_op jit(solution)/shard_map/ppermute | solution.py:221
  68.4 4.8 %collective-permute-done.3.refs_2_ = f32[4,1,40,256]{3,2,1,0:T(8,128)S(1)} collective-permute-done((f32[4,1,40,256]{3,2,1,0:T(8,128)S(1)}, f32[4,1,40,256]{3,2,1,0:T(8,128)S(1)}, u32[]{:S(2)}, u32[]{:S(2)}) %collective-permute-start.3) | collective-permute-done | bytes 163872 | tf_op jit(solution)/shard_map/ppermute | solution.py:221
  73.2 0.8 collective-permute-done.5.refs_6_
  74.0 3.8 %all-to-all-done.own_ref = f32[8,168,256]{2,1,0:T(8,128)S(1)} async-done(((f32[8,168,256]{2,1,0:T(8,128)}), f32[8,168,256]{2,1,0:T(8,128)S(1)}, u32[]{:S(2)}, u32[]{:S(2)}) %all-to-all-start) | async-done | bytes 1376288 | tf_op jit(solution)/shard_map/all_to_all | solution.py:218
  77.8 7.0 %collective-permute-start.6 = (f32[8,168,256]{2,1,0:T(8,128)S(1)}, f32[8,168,256]{2,1,0:T(8,128)S(1)}, u32[]{:S(2)}, u32[]{:S(2)}) collective-permute-start(f32[8,168,256]{2,1,0:T(8,128)S(1)} %all-to-all-done.own_ref), channel_id=1, source_target_pairs={{0,32},{32,0},{1,33},{33,1},{2,34},{34,2},{3,35},{35,3},{4,36},{36... | collective-permute-start | bytes 4128776 | tf_op jit(solution)/shard_map/ppermute | solution.py:232
  84.8 3.1 %collective-permute-start.7 = (f32[4,1,40,256]{3,2,1,0:T(8,128)S(1)}, f32[4,1,40,256]{3,2,1,0:T(8,128)S(1)}, u32[]{:S(2)}, u32[]{:S(2)}) collective-permute-start(f32[4,1,40,256]{3,2,1,0:T(8,128)S(1)} %collective-permute-done.3.refs_2_), channel_id=1, source_target_pairs={{0,4},{4,8},{8,12},{12,16},{16,20},{20,24},{24,28},{28,0},{1,5},{5... | collective-permute-start | bytes 491528 | tf_op jit(solution)/shard_map/ppermute | solution.py:221
  87.8 7.5 %collective-permute-start.9 = (f32[4,1,40,256]{3,2,1,0:T(8,128)S(1)}, f32[4,1,40,256]{3,2,1,0:T(8,128)S(1)}, u32[]{:S(2)}, u32[]{:S(2)}) collective-permute-start(f32[4,1,40,256]{3,2,1,0:T(8,128)S(1)} %collective-permute-done.5.refs_6_), channel_id=1, source_target_pairs={{0,28},{4,0},{8,4},{12,8},{16,12},{20,16},{24,20},{28,24},{1,29},{... | collective-permute-start | bytes 491528 | tf_op jit(solution)/shard_map/ppermute | solution.py:221
  95.4 2.6 %collective-permute-done.7.refs_3_ = f32[4,1,40,256]{3,2,1,0:T(8,128)S(1)} collective-permute-done((f32[4,1,40,256]{3,2,1,0:T(8,128)S(1)}, f32[4,1,40,256]{3,2,1,0:T(8,128)S(1)}, u32[]{:S(2)}, u32[]{:S(2)}) %collective-permute-start.7) | collective-permute-done | bytes 163872 | tf_op jit(solution)/shard_map/ppermute | solution.py:221
  98.0 1.9 %collective-permute-start.8 = (f32[4,1,40,256]{3,2,1,0:T(8,128)S(1)}, f32[4,1,40,256]{3,2,1,0:T(8,128)S(1)}, u32[]{:S(2)}, u32[]{:S(2)}) collective-permute-start(f32[4,1,40,256]{3,2,1,0:T(8,128)S(1)} %collective-permute-done.7.refs_3_), channel_id=1, source_target_pairs={{0,4},{4,8},{8,12},{12,16},{16,20},{20,24},{24,28},{28,0},{1,5},{5... | collective-permute-start | bytes 491528 | tf_op jit(solution)/shard_map/ppermute | solution.py:221
  99.9 0.1 pad_add_fusion.place
  100.0 0.0 collective-permute-done.6.other_ref
  100.0 0.0 copy-done.2
  100.0 3.0 %own_rows.1 = (bf16[512,1024]{1,0:T(8,128)(2,1)S(1)}, bf16[512,1024]{1,0:T(8,128)(2,1)S(1)}, f32[2,8,256]{2,1,0:T(8,128)S(1)}) custom-call(s32[4]{0:T(128)S(1)} %pad_add_fusion.place, s32[32]{0:T(128)S(1)} %copy-done.2, f32[8,168,256]{2,1,0:T(8,128)S(1)} %all-to-all-done.own_ref, f32[8,168,256]{2,1,0:T(8,128)S(1)} %collective-permute-done.6.other_ref), custom_call_target="tpu_custom_call" | custom-call | tf_op jit(solution)/shard_map/own_rows/pallas_call | solution.py:159
  103.0 0.0 copy-start
  103.0 1.0 copy-done
  103.9 0.0 copy-start.1
  103.9 1.0 copy-done.1
  104.9 0.0 collective-permute-done.9.refs_7_
  104.9 1.3 collective-permute-done.8.refs_4_
  106.3 0.0 all-gather.4.cloned.1.call-done
  106.3 0.0 copy-done.3
  106.3 0.0 copy-done.4
  106.3 10.6 %pairs.1 = (f32[8,2,64,256]{3,2,1,0:T(8,128)S(1)}, f32[8,2,64,256]{3,2,1,0:T(8,128)S(1)}) custom-call(s32[4]{0:T(128)S(1)} %pad_add_fusion.place, s32[32]{0:T(128)S(1)} %copy-done.2, f32[64]{0:T(128)S(1)} %copy-done.4, bf16[512,1024]{1,0:T(8,128)(2,1)} %copy-done, bf16[512,1024]{1,0:T(8,128)(2,1)} %copy-done.1, f32[2,8,256]{2,1,0:T(8,128)S(1)} %get-tuple-element.16.times, ...), custom_call_target="tpu_custom_call" | custom-call | tf_op jit(solution)/shard_map/pairs/pallas_call | solution.py:173
  116.8 3.4 %collective-permute-start.10 = (f32[8,2,64,256]{3,2,1,0:T(8,128)S(1)}, f32[8,2,64,256]{3,2,1,0:T(8,128)S(1)}, u32[]{:S(2)}, u32[]{:S(2)}) collective-permute-start(f32[8,2,64,256]{3,2,1,0:T(8,128)S(1)} %get-tuple-element.20), channel_id=1, source_target_pairs={{0,32},{32,0},{1,33},{33,1},{2,34},{34,2},{3,35},{35,3},{4,36},{36... | collective-permute-start | bytes 3145736 | tf_op jit(solution)/shard_map/ppermute | solution.py:237
  120.2 2.3 %collective-permute-done.10 = f32[8,2,64,256]{3,2,1,0:T(8,128)S(1)} collective-permute-done((f32[8,2,64,256]{3,2,1,0:T(8,128)S(1)}, f32[8,2,64,256]{3,2,1,0:T(8,128)S(1)}, u32[]{:S(2)}, u32[]{:S(2)}) %collective-permute-start.10) | collective-permute-done | bytes 1048608 | tf_op jit(solution)/shard_map/ppermute | solution.py:237
  122.5 0.1 add.45
  122.6 31.6 %all_to_all.10 = f32[8,2,64,256]{3,2,1,0:T(8,128)S(1)} all-to-all(f32[8,2,64,256]{3,2,1,0:T(8,128)S(1)} %add.45), channel_id=1, replica_groups=mesh['y'=8,'c'=2,'z'=8,'x'=4] {'y'}, dimensions={0} | all-to-all | bytes 2097152 | tf_op jit(solution)/shard_map/all_to_all | solution.py:238
  154.3 0.7 reduce_sum.9
  (3 shorter events, 0.0 us)
Async XLA Ops:
  6.5 29.2 %copy-start.5 = (s32[2,1,32]{2,1,0:T(1,128)S(1)}, s32[2,1,32]{2,1,0:T(1,128)}, u32[]{:S(2)}) copy-start(s32[2,1,32]{2,1,0:T(1,128)} %param.9) | copy-start | bytes 772
  6.5 99.7 %all-gather.4.cloned.1.call-start = ((), (), s32[]{:S(2)}) async-start(), calls=%async_computation.2 | async-start | bytes 4423680 | tf_op jit(solution)/shard_map/all_gather | solution.py:202
  19.7 80.3 %copy-start.2 = (s32[32]{0:T(128)S(1)}, s32[32]{0:T(128)}, u32[]{:S(2)}) copy-start(s32[32]{0:T(128)} %counts.3) | copy-start | bytes 388
  20.7 15.3 %collective-permute-start = (f32[2,40,256]{2,1,0:T(8,128)S(1)}, f32[2,40,256]{2,1,0:T(8,128)S(1)}, u32[]{:S(2)}, u32[]{:S(2)}) collective-permute-start(f32[2,40,256]{2,1,0:T(8,128)S(1)} %get-tuple-element.21), channel_id=1, source_target_pairs={{0,0},{1,15},{2,14},{3,13},{4,12},{5,11},{6,10},{7,9},{8,8},{9,7},... | collective-permute-start | bytes 245768 | tf_op jit(solution)/shard_map/ppermute | solution.py:213
  23.5 17.3 %collective-permute-start.1 = (f32[2,40,256]{2,1,0:T(8,128)S(1)}, f32[2,40,256]{2,1,0:T(8,128)S(1)}, u32[]{:S(2)}, u32[]{:S(2)}) collective-permute-start(f32[2,40,256]{2,1,0:T(8,128)S(1)} %get-tuple-element.22), channel_id=1, source_target_pairs={{0,16},{1,31},{2,30},{3,29},{4,28},{5,27},{6,26},{7,25},{8,24},{9,... | collective-permute-start | bytes 245768 | tf_op jit(solution)/shard_map/ppermute | solution.py:213
  42.0 64.2 %copy-start.3 = (f32[256]{0:T(256)S(1)}, f32[256]{0:T(256)}, u32[]{:S(2)}) copy-start(f32[256]{0:T(256)} %param.8) | copy-start | bytes 3076
  42.0 64.2 %copy-start.4 = (f32[64]{0:T(128)S(1)}, f32[64]{0:T(128)}, u32[]{:S(2)}) copy-start(f32[64]{0:T(128)} %occ.1) | copy-start | bytes 772
  42.0 35.7 %all-to-all-start = ((f32[8,168,256]{2,1,0:T(8,128)}), f32[8,168,256]{2,1,0:T(8,128)S(1)}, u32[]{:S(2)}, u32[]{:S(2)}) async-start(f32[8,168,256]{2,1,0:T(8,128)} %broadcast_in_dim.19), calls=%async_computation | async-start | bytes 2752512 | tf_op jit(solution)/shard_map/all_to_all | solution.py:218
  46.1 15.7 %collective-permute-start.2 = (f32[4,1,40,256]{3,2,1,0:T(8,128)S(1)}, f32[4,1,40,256]{3,2,1,0:T(8,128)S(1)}, u32[]{:S(2)}, u32[]{:S(2)}) collective-permute-start(f32[4,1,40,256]{3,2,1,0:T(8,128)S(1)} %slice.9.refs_0_), channel_id=1, source_target_pairs={{0,4},{4,8},{8,12},{12,16},{16,20},{20,24},{24,28},{28,0},{1,5},{5... | collective-permute-start | bytes 491528 | tf_op jit(solution)/shard_map/ppermute | solution.py:221
  49.2 14.5 %collective-permute-start.4 = (f32[4,1,40,256]{3,2,1,0:T(8,128)S(1)}, f32[4,1,40,256]{3,2,1,0:T(8,128)S(1)}, u32[]{:S(2)}, u32[]{:S(2)}) collective-permute-start(f32[4,1,40,256]{3,2,1,0:T(8,128)S(1)} %slice.9.refs_0_), channel_id=1, source_target_pairs={{0,28},{4,0},{8,4},{12,8},{16,12},{20,16},{24,20},{28,24},{1,29},{... | collective-permute-start | bytes 491528 | tf_op jit(solution)/shard_map/ppermute | solution.py:221
  61.8 11.3 %collective-permute-start.3 = (f32[4,1,40,256]{3,2,1,0:T(8,128)S(1)}, f32[4,1,40,256]{3,2,1,0:T(8,128)S(1)}, u32[]{:S(2)}, u32[]{:S(2)}) collective-permute-start(f32[4,1,40,256]{3,2,1,0:T(8,128)S(1)} %collective-permute-done.2.refs_1_), channel_id=1, source_target_pairs={{0,4},{4,8},{8,12},{12,16},{16,20},{20,24},{24,28},{28,0},{1,5},{5... | collective-permute-start | bytes 491528 | tf_op jit(solution)/shard_map/ppermute | solution.py:221
  63.8 10.2 %collective-permute-start.5 = (f32[4,1,40,256]{3,2,1,0:T(8,128)S(1)}, f32[4,1,40,256]{3,2,1,0:T(8,128)S(1)}, u32[]{:S(2)}, u32[]{:S(2)}) collective-permute-start(f32[4,1,40,256]{3,2,1,0:T(8,128)S(1)} %collective-permute-done.4.refs_5_), channel_id=1, source_target_pairs={{0,28},{4,0},{8,4},{12,8},{16,12},{20,16},{24,20},{28,24},{1,29},{... | collective-permute-start | bytes 491528 | tf_op jit(solution)/shard_map/ppermute | solution.py:221
  77.8 22.2 %collective-permute-start.6 = (f32[8,168,256]{2,1,0:T(8,128)S(1)}, f32[8,168,256]{2,1,0:T(8,128)S(1)}, u32[]{:S(2)}, u32[]{:S(2)}) collective-permute-start(f32[8,168,256]{2,1,0:T(8,128)S(1)} %all-to-all-done.own_ref), channel_id=1, source_target_pairs={{0,32},{32,0},{1,33},{33,1},{2,34},{34,2},{3,35},{35,3},{4,36},{36... | collective-permute-start | bytes 4128776 | tf_op jit(solution)/shard_map/ppermute | solution.py:232
  84.8 13.2 %collective-permute-start.7 = (f32[4,1,40,256]{3,2,1,0:T(8,128)S(1)}, f32[4,1,40,256]{3,2,1,0:T(8,128)S(1)}, u32[]{:S(2)}, u32[]{:S(2)}) collective-permute-start(f32[4,1,40,256]{3,2,1,0:T(8,128)S(1)} %collective-permute-done.3.refs_2_), channel_id=1, source_target_pairs={{0,4},{4,8},{8,12},{12,16},{16,20},{20,24},{24,28},{28,0},{1,5},{5... | collective-permute-start | bytes 491528 | tf_op jit(solution)/shard_map/ppermute | solution.py:221
  87.8 17.1 %collective-permute-start.9 = (f32[4,1,40,256]{3,2,1,0:T(8,128)S(1)}, f32[4,1,40,256]{3,2,1,0:T(8,128)S(1)}, u32[]{:S(2)}, u32[]{:S(2)}) collective-permute-start(f32[4,1,40,256]{3,2,1,0:T(8,128)S(1)} %collective-permute-done.5.refs_6_), channel_id=1, source_target_pairs={{0,28},{4,0},{8,4},{12,8},{16,12},{20,16},{24,20},{28,24},{1,29},{... | collective-permute-start | bytes 491528 | tf_op jit(solution)/shard_map/ppermute | solution.py:221
  98.0 8.3 %collective-permute-start.8 = (f32[4,1,40,256]{3,2,1,0:T(8,128)S(1)}, f32[4,1,40,256]{3,2,1,0:T(8,128)S(1)}, u32[]{:S(2)}, u32[]{:S(2)}) collective-permute-start(f32[4,1,40,256]{3,2,1,0:T(8,128)S(1)} %collective-permute-done.7.refs_3_), channel_id=1, source_target_pairs={{0,4},{4,8},{8,12},{12,16},{16,20},{20,24},{24,28},{28,0},{1,5},{5... | collective-permute-start | bytes 491528 | tf_op jit(solution)/shard_map/ppermute | solution.py:221
  103.0 1.0 copy-start
  103.9 1.0 copy-start.1
  116.8 5.6 %collective-permute-start.10 = (f32[8,2,64,256]{3,2,1,0:T(8,128)S(1)}, f32[8,2,64,256]{3,2,1,0:T(8,128)S(1)}, u32[]{:S(2)}, u32[]{:S(2)}) collective-permute-start(f32[8,2,64,256]{3,2,1,0:T(8,128)S(1)} %get-tuple-element.20), channel_id=1, source_target_pairs={{0,32},{32,0},{1,33},{33,1},{2,34},{34,2},{3,35},{35,3},{4,36},{36... | collective-permute-start | bytes 3145736 | tf_op jit(solution)/shard_map/ppermute | solution.py:237
Sparse Core Ops, SparseCore 0:
  19.8 70.4 all-gather.3

commit v8 on v4

--- a/solution.py
+++ b/solution.py
@@ -90,7 +90,7 @@
 
 
 def pair_kernel(place, counts, occ, own_hi_any, own_lo_any, times, virt, wide_any,
-                theirs_ref, mine_ref, own_hi, own_lo, rows, dense, w_hi, w_lo, x_hi, x_lo, sems):
+                theirs_ref, w_hi, w_lo, x_hi, x_lo, own_hi, own_lo, rows, dense, sems):
     core, u, grp = place[0], place[1], place[2]
     row_copies = [pltpu.make_async_copy(wide_any.at[z], rows.at[z], sems.at[z]) for z in range(NZ)]
     own_copies = [
@@ -130,13 +130,19 @@
             x_hi[cols, i * V:(i + 1) * V] = hi
             x_lo[cols, i * V:(i + 1) * V] = lo
 
-    for k, out in enumerate((theirs_ref, mine_ref)):
-        part = slice(k * 512, (k + 1) * 512)
-        for i in range(OCC_DEV):
-            cols = slice(i * V, (i + 1) * V)
-            term = dot3(w_hi[part, :], w_lo[part, :], x_hi[:, cols], x_lo[:, cols])
-            for q in range(NY):
-                out[q, i] = term[q * BLK:(q + 1) * BLK, :]
+    put_terms(theirs_ref, slice(0, 512), w_hi, w_lo, x_hi, x_lo)
+
+
+def put_terms(out, part, w_hi, w_lo, x_hi, x_lo):
+    for i in range(OCC_DEV):
+        cols = slice(i * V, (i + 1) * V)
+        term = dot3(w_hi[part, :], w_lo[part, :], x_hi[:, cols], x_lo[:, cols])
+        for q in range(NY):
+            out[q, i] = term[q * BLK:(q + 1) * BLK, :]
+
+
+def mine_kernel(w_hi, w_lo, x_hi, x_lo, mine_ref):
+    put_terms(mine_ref, slice(512, 1024), w_hi, w_lo, x_hi, x_lo)
 
 
 SMEM = pl.BlockSpec(memory_space=pltpu.SMEM)
@@ -159,25 +165,35 @@
 
 def pairs(place, counts, occ_energy, own_hi, own_lo, times, virt, wide_all):
     part = jax.ShapeDtypeStruct((NY, OCC_DEV, BLK, V), jnp.float32)
+    wide_split = jax.ShapeDtypeStruct((NAUX, 4 * V), jnp.bfloat16)
+    weights = jax.ShapeDtypeStruct((4 * V, OCC_DEV * V), jnp.bfloat16)
     return pl.pallas_call(
         pair_kernel,
-        out_shape=[part, part],
+        out_shape=[part] + [wide_split] * 2 + [weights] * 2,
         in_specs=[SMEM] * 3 + [HBM, HBM, VMEM, VMEM, HBM],
-        out_specs=[VMEM, VMEM],
+        out_specs=[VMEM] * 5,
         scratch_shapes=[
             pltpu.VMEM((OCC_DEV * V, NAUX), jnp.bfloat16),
             pltpu.VMEM((OCC_DEV * V, NAUX), jnp.bfloat16),
             pltpu.VMEM((NZ, NX, 4, CAP, V), jnp.float32),
             pltpu.VMEM((NAUX + PAD, 4 * V), jnp.float32),
-            pltpu.VMEM((NAUX, 4 * V), jnp.bfloat16),
-            pltpu.VMEM((NAUX, 4 * V), jnp.bfloat16),
-            pltpu.VMEM((4 * V, OCC_DEV * V), jnp.bfloat16),
-            pltpu.VMEM((4 * V, OCC_DEV * V), jnp.bfloat16),
             pltpu.SemaphoreType.DMA((NZ + 2,)),
         ],
-        compiler_params=pltpu.CompilerParams(vmem_limit_bytes=48 * MIB),
+        compiler_params=pltpu.CompilerParams(vmem_limit_bytes=40 * MIB),
         name="pairs",
     )(place, counts, occ_energy, own_hi, own_lo, times, virt, wide_all)
+
+
+def own_core_rows(*operands):
+    return pl.pallas_call(
+        mine_kernel,
+        out_shape=jax.ShapeDtypeStruct((NY, OCC_DEV, BLK, V), jnp.float32),
+        in_specs=[VMEM] * 4,
+        out_specs=VMEM,
+        compiler_params=pltpu.CompilerParams(vmem_limit_bytes=32 * MIB),
+        cost_estimate=pl.CostEstimate(flops=6 * 512 * 512 * 1024, bytes_accessed=8 * MIB, transcendentals=0),
+        name="own_core_rows",
+    )(*operands)
 
 
 def per_device(three_center, counts, occ_energy, virt_energy, match_tables):
@@ -207,9 +223,10 @@
     other_pay = lax.ppermute(own_pay, "c", [(0, 1), (1, 0)])
 
     own_hi, own_lo, times = own_rows(place, counts, own_pay, other_pay)
-    theirs, mine = pairs(place, counts, occ_energy, own_hi, own_lo, times, virt_energy.reshape(1, V), wide_all)
-
-    mine = mine + lax.ppermute(theirs, "c", [(0, 1), (1, 0)])
+    theirs, *split = pairs(place, counts, occ_energy, own_hi, own_lo, times, virt_energy.reshape(1, V), wide_all)
+
+    sums = lax.ppermute(theirs, "c", [(0, 1), (1, 0)])
+    mine = own_core_rows(*split) + sums
     pieces = lax.all_to_all(mine, "y", split_axis=0, concat_axis=0, tiled=True)
     return jnp.sum(pieces, axis=0)
 

time: 153 us -> 152 us (level)
    ppermute x1, waiting for transfers between devices: 2.26 us -> 0.48 us  [per_device(): sums = lax.ppermute(theirs, 'c', [(0, 1), (1, 0)])]
    pallas_call x1 -> x2, Pallas kernels: 10.4 us -> 11.1 us  [the longest x1 9.29 us: pairs(): pl.pallas_call(pair_kernel, out_shape=[part] + [wide_split] * 2 + [weight...]
  transfers between devices with their start and end apart: 5 -> 5, of which waited for: 4 -> 4; matrix products, arithmetic and copies ran while one was open for 1% -> 1% of each run, Pallas kernels for 2% -> 3%
where the time goes in v8:
time: 152 us
  blocking collectives  81.5 us (54%)
  starting transfers between devices  24.5 us (16%)
  waiting for transfers between devices  14.8 us (10%)
  Pallas kernels  14 us (9%)
  between operations  13.6 us (9%)
  local copies, waits for them, and re-layouts  2.07 us (1%)
    all_to_all x1, blocking collectives, per_device(): own_pay = lax.all_to_all(sent, 'y', split_axis=0, concat_axis=0, tiled=True)  34.6 us
    all_to_all x1, blocking collectives, per_device(): pieces = lax.all_to_all(mine, 'y', split_axis=0, concat_axis=0, tiled=True)  34.2 us
    ppermute x2, starting transfers between devices, per_device(): got.append(lax.ppermute(piece, axes, perm).reshape(OCC_DEV * CAP, V))  14.1 us
    all_gather x1, blocking collectives, per_device(): wide_all = lax.all_gather(lax.all_gather(wide_part, 'x'), 'z')  12.7 us
    pallas_call x1, Pallas kernels, pairs(): pl.pallas_call(pair_kernel, out_shape=[part] + [wide_split] * 2 + [weight...  9.29 us
    ppermute x1, starting transfers between devices, per_device(): other_pay = lax.ppermute(own_pay, 'c', [(0, 1), (1, 0)])  7.78 us
    all_gather x1, waiting for transfers between devices, per_device(): wide_all = lax.all_gather(lax.all_gather(wide_part, 'x'), 'z')  6.82 us
    ppermute x2, waiting for transfers between devices, per_device(): got.append(lax.ppermute(piece, axes, perm).reshape(OCC_DEV * CAP, V))  4.84 us
  transfers between devices with their start and end apart: 5, of which 4 were waited for; matrix products, arithmetic and copies ran while one was open for 1% of the time, Pallas kernels for 3%

profile of v8, /device:TPU:1, one launch (start us, length us, event | category | flops | bytes accessed | tf_op | source)
XLA Modules:
  0.0 151.6 jit_solution(761298045519560346)
XLA Ops:
  6.5 0.0 copy-start.3
  6.5 0.0 all-gather.4.cloned.1.call-start
  6.5 0.9 constant_dynamic-slice_fusion
  7.5 12.7 %all-gather = f32[16,40,256]{2,1,0:T(8,128)} all-gather(f32[4,40,256]{2,1,0:T(8,128)S(1)} %constant_dynamic-slice_fusion), channel_id=2, replica_groups=mesh['y'=8,'c'=2,'z'=8,'x'=4] {'x'}, dimensions={0}, use_global_device_ids=true | all-gather | bytes 819200 | tf_op jit(solution)/shard_map/all_gather | solution.py:206
  20.2 0.0 all-gather.4.cloned.1.call-update
  20.3 0.9 constant_dynamic-slice_fusion.2
  21.2 2.2 %collective-permute-start = (f32[2,40,256]{2,1,0:T(8,128)S(1)}, f32[2,40,256]{2,1,0:T(8,128)S(1)}, u32[]{:S(2)}, u32[]{:S(2)}) collective-permute-start(f32[2,40,256]{2,1,0:T(8,128)S(1)} %get-tuple-element.21), channel_id=1, source_target_pairs={{0,0},{1,15},{2,14},{3,13},{4,12},{5,11},{6,10},{7,9},{8,8},{9,7},... | collective-permute-start | bytes 245768 | tf_op jit(solution)/shard_map/ppermute | solution.py:217
  23.4 12.0 %collective-permute-start.1 = (f32[2,40,256]{2,1,0:T(8,128)S(1)}, f32[2,40,256]{2,1,0:T(8,128)S(1)}, u32[]{:S(2)}, u32[]{:S(2)}) collective-permute-start(f32[2,40,256]{2,1,0:T(8,128)S(1)} %get-tuple-element.22), channel_id=1, source_target_pairs={{0,16},{1,31},{2,30},{3,29},{4,28},{5,27},{6,26},{7,25},{8,24},{9,... | collective-permute-start | bytes 245768 | tf_op jit(solution)/shard_map/ppermute | solution.py:217
  35.4 0.0 copy-done.3
  35.4 0.2 convert_reduce_fusion
  35.6 0.1 broadcast_bitcast_fusion
  35.6 0.0 collective-permute-done
  35.6 4.8 %collective-permute-done.1 = f32[2,40,256]{2,1,0:T(8,128)S(1)} collective-permute-done((f32[2,40,256]{2,1,0:T(8,128)S(1)}, f32[2,40,256]{2,1,0:T(8,128)S(1)}, u32[]{:S(2)}, u32[]{:S(2)}) %collective-permute-start.1) | collective-permute-done | bytes 81952 | tf_op jit(solution)/shard_map/ppermute | solution.py:217
  40.5 0.0 copy-start
  40.5 0.1 broadcast_in_dim.19
  40.6 0.0 copy-start.1
  40.6 0.0 copy-start.2
  40.6 34.6 %all_to_all.10.own_ref = f32[8,168,256]{2,1,0:T(8,128)S(1)} all-to-all(f32[8,168,256]{2,1,0:T(8,128)S(1)} %broadcast_in_dim.19), channel_id=1, replica_groups=mesh['y'=8,'c'=2,'z'=8,'x'=4] {'y'}, dimensions={0} | all-to-all | bytes 2752512 | tf_op jit(solution)/shard_map/all_to_all | solution.py:222
  75.2 7.8 %collective-permute-start.2 = (f32[8,168,256]{2,1,0:T(8,128)S(1)}, f32[8,168,256]{2,1,0:T(8,128)S(1)}, u32[]{:S(2)}, u32[]{:S(2)}) collective-permute-start(f32[8,168,256]{2,1,0:T(8,128)S(1)} %all_to_all.10.own_ref), channel_id=1, source_target_pairs={{0,32},{32,0},{1,33},{33,1},{2,34},{34,2},{3,35},{35,3},{4,36},{36... | collective-permute-start | bytes 4128776 | tf_op jit(solution)/shard_map/ppermute | solution.py:223
  83.0 0.1 pad_add_fusion.place
  83.1 2.7 %collective-permute-done.2.other_ref = f32[8,168,256]{2,1,0:T(8,128)S(1)} collective-permute-done((f32[8,168,256]{2,1,0:T(8,128)S(1)}, f32[8,168,256]{2,1,0:T(8,128)S(1)}, u32[]{:S(2)}, u32[]{:S(2)}) %collective-permute-start.2) | collective-permute-done | bytes 1376288 | tf_op jit(solution)/shard_map/ppermute | solution.py:223
  85.7 0.0 copy-done
  85.7 3.0 %own_rows.1 = (bf16[512,1024]{1,0:T(8,128)(2,1)S(1)}, bf16[512,1024]{1,0:T(8,128)(2,1)S(1)}, f32[2,8,256]{2,1,0:T(8,128)S(1)}) custom-call(s32[3]{0:T(128)S(1)} %pad_add_fusion.place, s32[32]{0:T(128)S(1)} %copy-done, f32[8,168,256]{2,1,0:T(8,128)S(1)} %all_to_all.10.own_ref, f32[8,168,256]{2,1,0:T(8,128)S(1)} %collective-permute-done.2.other_ref), custom_call_target="tpu_custom_call" | custom-call | tf_op jit(solution)/shard_map/own_rows/pallas_call | solution.py:154
  88.7 6.8 %all-gather.4.cloned.1.call-done = f32[32,4,40,256]{3,2,1,0:T(8,128)} async-done(((f32[4,4,40,256]{3,2,1,0:T(8,128)}), f32[32,4,40,256]{3,2,1,0:T(8,128)}) %all-gather.4.cloned.1.call-update) | async-done | bytes 5242896 | tf_op jit(solution)/shard_map/all_gather | solution.py:206
  95.5 0.0 copy-done.1
  95.5 0.0 copy-done.2
  95.5 9.3 %pairs.1 = (f32[8,2,64,256]{3,2,1,0:T(8,128)S(1)}, bf16[1024,1024]{1,0:T(8,128)(2,1)S(1)}, bf16[1024,1024]{1,0:T(8,128)(2,1)S(1)}, bf16[1024,512]{1,0:T(8,128)(2,1)S(1)}, bf16[1024,512]{1,0:T(8,128)(2,1)S(1)}) custom-call(s32[3]{0:T(128)S(1)} %pad_add_fusion.place, s32[32]{0:T(128)S(1)} %copy-done, f32[64]{0:T(128)S(1)} %copy-done.2, ...), custom_call_target="tpu_custom_call" | custom-call | tf_op jit(solution)/shard_map/pairs/pallas_call | solution.py:170
  104.8 2.6 %collective-permute-start.3 = (f32[8,2,64,256]{3,2,1,0:T(8,128)S(1)}, f32[8,2,64,256]{3,2,1,0:T(8,128)S(1)}, u32[]{:S(2)}, u32[]{:S(2)}) collective-permute-start(f32[8,2,64,256]{3,2,1,0:T(8,128)S(1)} %get-tuple-element.20), channel_id=1, source_target_pairs={{0,32},{32,0},{1,33},{33,1},{2,34},{34,2},{3,35},{35,3},{4,36},{36... | collective-permute-start | bytes 3145736 | tf_op jit(solution)/shard_map/ppermute | solution.py:228
  107.4 1.8 %own_core_rows.1 = f32[8,2,64,256]{3,2,1,0:T(8,128)S(1)} custom-call(bf16[1024,1024]{1,0:T(8,128)(2,1)S(1)} %get-tuple-element.16.w_hi, bf16[1024,1024]{1,0:T(8,128)(2,1)S(1)} %get-tuple-element.17.w_lo, bf16[1024,512]{1,0:T(8,128)(2,1)S(1)} %get-tuple-element.18.x_hi, bf16[1024,512]{1,0:T(8,128)(2,1)S(1)} %get-tuple-element.19.x_lo), custom_call_target="tpu_custom_call" | custom-call | flops 1610612736 | bytes 8388608 | tf_op jit(solution)/shard_map/own_core_rows/pallas_call | solution.py:188
  109.2 0.5 collective-permute-done.3
  109.7 0.1 add.45
  109.9 34.2 %all_to_all.11 = f32[8,2,64,256]{3,2,1,0:T(8,128)S(1)} all-to-all(f32[8,2,64,256]{3,2,1,0:T(8,128)S(1)} %add.45), channel_id=1, replica_groups=mesh['y'=8,'c'=2,'z'=8,'x'=4] {'y'}, dimensions={0} | all-to-all | bytes 2097152 | tf_op jit(solution)/shard_map/all_to_all | solution.py:230
  144.1 0.7 reduce_sum.9
  (2 shorter events, 0.0 us)
Async XLA Ops:
  6.5 28.8 %copy-start.3 = (s32[2,1,32]{2,1,0:T(1,128)S(1)}, s32[2,1,32]{2,1,0:T(1,128)}, u32[]{:S(2)}) copy-start(s32[2,1,32]{2,1,0:T(1,128)} %param.9) | copy-start | bytes 772
  6.5 89.0 %all-gather.4.cloned.1.call-start = ((), (), s32[]{:S(2)}) async-start(), calls=%async_computation.2 | async-start | bytes 5898240 | tf_op jit(solution)/shard_map/all_gather | solution.py:206
  21.2 14.4 %collective-permute-start = (f32[2,40,256]{2,1,0:T(8,128)S(1)}, f32[2,40,256]{2,1,0:T(8,128)S(1)}, u32[]{:S(2)}, u32[]{:S(2)}) collective-permute-start(f32[2,40,256]{2,1,0:T(8,128)S(1)} %get-tuple-element.21), channel_id=1, source_target_pairs={{0,0},{1,15},{2,14},{3,13},{4,12},{5,11},{6,10},{7,9},{8,8},{9,7},... | collective-permute-start | bytes 245768 | tf_op jit(solution)/shard_map/ppermute | solution.py:217
  23.4 17.1 %collective-permute-start.1 = (f32[2,40,256]{2,1,0:T(8,128)S(1)}, f32[2,40,256]{2,1,0:T(8,128)S(1)}, u32[]{:S(2)}, u32[]{:S(2)}) collective-permute-start(f32[2,40,256]{2,1,0:T(8,128)S(1)} %get-tuple-element.22), channel_id=1, source_target_pairs={{0,16},{1,31},{2,30},{3,29},{4,28},{5,27},{6,26},{7,25},{8,24},{9,... | collective-permute-start | bytes 245768 | tf_op jit(solution)/shard_map/ppermute | solution.py:217
  40.5 45.2 %copy-start = (s32[32]{0:T(128)S(1)}, s32[32]{0:T(128)}, u32[]{:S(2)}) copy-start(s32[32]{0:T(128)} %counts.3) | copy-start | bytes 388
  40.6 54.9 %copy-start.1 = (f32[256]{0:T(256)S(1)}, f32[256]{0:T(256)}, u32[]{:S(2)}) copy-start(f32[256]{0:T(256)} %param.8) | copy-start | bytes 3076
  40.6 54.9 %copy-start.2 = (f32[64]{0:T(128)S(1)}, f32[64]{0:T(128)}, u32[]{:S(2)}) copy-start(f32[64]{0:T(128)} %occ.1) | copy-start | bytes 772
  75.2 10.5 %collective-permute-start.2 = (f32[8,168,256]{2,1,0:T(8,128)S(1)}, f32[8,168,256]{2,1,0:T(8,128)S(1)}, u32[]{:S(2)}, u32[]{:S(2)}) collective-permute-start(f32[8,168,256]{2,1,0:T(8,128)S(1)} %all_to_all.10.own_ref), channel_id=1, source_target_pairs={{0,32},{32,0},{1,33},{33,1},{2,34},{34,2},{3,35},{35,3},{4,36},{36... | collective-permute-start | bytes 4128776 | tf_op jit(solution)/shard_map/ppermute | solution.py:223
  104.8 4.9 %collective-permute-start.3 = (f32[8,2,64,256]{3,2,1,0:T(8,128)S(1)}, f32[8,2,64,256]{3,2,1,0:T(8,128)S(1)}, u32[]{:S(2)}, u32[]{:S(2)}) collective-permute-start(f32[8,2,64,256]{3,2,1,0:T(8,128)S(1)} %get-tuple-element.20), channel_id=1, source_target_pairs={{0,32},{32,0},{1,33},{33,1},{2,34},{34,2},{3,35},{35,3},{4,36},{36... | collective-permute-start | bytes 3145736 | tf_op jit(solution)/shard_map/ppermute | solution.py:228
Sparse Core Ops, SparseCore 0:
  20.4 75.1 all-gather.3

commit v9 on v8

--- a/solution.py
+++ b/solution.py
@@ -89,15 +89,11 @@
         turn(n, 0)
 
 
-def pair_kernel(place, counts, occ, own_hi_any, own_lo_any, times, virt, wide_any,
-                theirs_ref, w_hi, w_lo, x_hi, x_lo, own_hi, own_lo, rows, dense, sems):
+def pair_kernel(place, counts, occ, own_hi, own_lo, times, virt, wide_any,
+                theirs_ref, w_hi, w_lo, x_hi, x_lo, rows, dense, sems):
     core, u, grp = place[0], place[1], place[2]
     row_copies = [pltpu.make_async_copy(wide_any.at[z], rows.at[z], sems.at[z]) for z in range(NZ)]
-    own_copies = [
-        pltpu.make_async_copy(own_hi_any, own_hi, sems.at[NZ]),
-        pltpu.make_async_copy(own_lo_any, own_lo, sems.at[NZ + 1]),
-    ]
-    for copy in row_copies + own_copies:
+    for copy in row_copies:
         copy.start()
 
     off = jnp.int32(0)
@@ -118,8 +114,6 @@
 
     virt_row = jnp.broadcast_to(virt[...], (V, V))
     virt_sum = virt_row + virt_row.T
-    for copy in own_copies:
-        copy.wait()
     for j in range(4):
         cols = slice(j * V, (j + 1) * V)
         coulomb = dot3(own_hi[...], own_lo[...], w_hi[:, cols], w_lo[:, cols])
@@ -170,14 +164,12 @@
     return pl.pallas_call(
         pair_kernel,
         out_shape=[part] + [wide_split] * 2 + [weights] * 2,
-        in_specs=[SMEM] * 3 + [HBM, HBM, VMEM, VMEM, HBM],
+        in_specs=[SMEM] * 3 + [VMEM] * 4 + [HBM],
         out_specs=[VMEM] * 5,
         scratch_shapes=[
-            pltpu.VMEM((OCC_DEV * V, NAUX), jnp.bfloat16),
-            pltpu.VMEM((OCC_DEV * V, NAUX), jnp.bfloat16),
             pltpu.VMEM((NZ, NX, 4, CAP, V), jnp.float32),
             pltpu.VMEM((NAUX + PAD, 4 * V), jnp.float32),
-            pltpu.SemaphoreType.DMA((NZ + 2,)),
+            pltpu.SemaphoreType.DMA((NZ,)),
         ],
         compiler_params=pltpu.CompilerParams(vmem_limit_bytes=40 * MIB),
         name="pairs",

time: 152 us -> 151 us (level)
  no operation moved by 1% of the time
where the time goes in v9:
time: 151 us
  blocking collectives  81.5 us (54%)
  starting transfers between devices  24.5 us (16%)
  waiting for transfers between devices  14.8 us (10%)
  between operations  13.6 us (9%)
  Pallas kernels  13.3 us (9%)
  local copies, waits for them, and re-layouts  2.07 us (1%)
    all_to_all x1, blocking collectives, per_device(): own_pay = lax.all_to_all(sent, 'y', split_axis=0, concat_axis=0, tiled=True)  34.6 us
    all_to_all x1, blocking collectives, per_device(): pieces = lax.all_to_all(mine, 'y', split_axis=0, concat_axis=0, tiled=True)  34.2 us
    ppermute x2, starting transfers between devices, per_device(): got.append(lax.ppermute(piece, axes, perm).reshape(OCC_DEV * CAP, V))  14.1 us
    all_gather x1, blocking collectives, per_device(): wide_all = lax.all_gather(lax.all_gather(wide_part, 'x'), 'z')  12.7 us
    pallas_call x1, Pallas kernels, pairs(): pl.pallas_call(pair_kernel, out_shape=[part] + [wide_split] * 2 + [weight...  8.53 us
    ppermute x1, starting transfers between devices, per_device(): other_pay = lax.ppermute(own_pay, 'c', [(0, 1), (1, 0)])  7.78 us
    all_gather x1, waiting for transfers between devices, per_device(): wide_all = lax.all_gather(lax.all_gather(wide_part, 'x'), 'z')  6.82 us
    ppermute x2, waiting for transfers between devices, per_device(): got.append(lax.ppermute(piece, axes, perm).reshape(OCC_DEV * CAP, V))  4.84 us
  transfers between devices with their start and end apart: 5, of which 4 were waited for; matrix products, arithmetic and copies ran while one was open for 1% of the time, Pallas kernels for 3%

profile of v9, /device:TPU:1, one launch (start us, length us, event | category | flops | bytes accessed | tf_op | source)
XLA Modules:
  0.0 150.9 jit_solution(18322013560888127336)
XLA Ops:
  6.5 0.0 copy-start.3
  6.5 0.0 all-gather.4.cloned.1.call-start
  6.5 0.9 constant_dynamic-slice_fusion
  7.5 12.7 %all-gather = f32[16,40,256]{2,1,0:T(8,128)} all-gather(f32[4,40,256]{2,1,0:T(8,128)S(1)} %constant_dynamic-slice_fusion), channel_id=2, replica_groups=mesh['y'=8,'c'=2,'z'=8,'x'=4] {'x'}, dimensions={0}, use_global_device_ids=true | all-gather | bytes 819200 | tf_op jit(solution)/shard_map/all_gather | solution.py:198
  20.2 0.0 all-gather.4.cloned.1.call-update
  20.3 0.9 constant_dynamic-slice_fusion.2
  21.2 2.2 %collective-permute-start = (f32[2,40,256]{2,1,0:T(8,128)S(1)}, f32[2,40,256]{2,1,0:T(8,128)S(1)}, u32[]{:S(2)}, u32[]{:S(2)}) collective-permute-start(f32[2,40,256]{2,1,0:T(8,128)S(1)} %get-tuple-element.21), channel_id=1, source_target_pairs={{0,0},{1,15},{2,14},{3,13},{4,12},{5,11},{6,10},{7,9},{8,8},{9,7},... | collective-permute-start | bytes 245768 | tf_op jit(solution)/shard_map/ppermute | solution.py:209
  23.4 12.0 %collective-permute-start.1 = (f32[2,40,256]{2,1,0:T(8,128)S(1)}, f32[2,40,256]{2,1,0:T(8,128)S(1)}, u32[]{:S(2)}, u32[]{:S(2)}) collective-permute-start(f32[2,40,256]{2,1,0:T(8,128)S(1)} %get-tuple-element.22), channel_id=1, source_target_pairs={{0,16},{1,31},{2,30},{3,29},{4,28},{5,27},{6,26},{7,25},{8,24},{9,... | collective-permute-start | bytes 245768 | tf_op jit(solution)/shard_map/ppermute | solution.py:209
  35.4 0.0 copy-done.3
  35.4 0.2 convert_reduce_fusion
  35.6 0.1 broadcast_bitcast_fusion
  35.6 0.0 collective-permute-done
  35.6 4.8 %collective-permute-done.1 = f32[2,40,256]{2,1,0:T(8,128)S(1)} collective-permute-done((f32[2,40,256]{2,1,0:T(8,128)S(1)}, f32[2,40,256]{2,1,0:T(8,128)S(1)}, u32[]{:S(2)}, u32[]{:S(2)}) %collective-permute-start.1) | collective-permute-done | bytes 81952 | tf_op jit(solution)/shard_map/ppermute | solution.py:209
  40.5 0.0 copy-start
  40.5 0.1 broadcast_in_dim.19
  40.6 0.0 copy-start.1
  40.6 0.0 copy-start.2
  40.6 34.6 %all_to_all.10.own_ref = f32[8,168,256]{2,1,0:T(8,128)S(1)} all-to-all(f32[8,168,256]{2,1,0:T(8,128)S(1)} %broadcast_in_dim.19), channel_id=1, replica_groups=mesh['y'=8,'c'=2,'z'=8,'x'=4] {'y'}, dimensions={0} | all-to-all | bytes 2752512 | tf_op jit(solution)/shard_map/all_to_all | solution.py:214
  75.2 7.8 %collective-permute-start.2 = (f32[8,168,256]{2,1,0:T(8,128)S(1)}, f32[8,168,256]{2,1,0:T(8,128)S(1)}, u32[]{:S(2)}, u32[]{:S(2)}) collective-permute-start(f32[8,168,256]{2,1,0:T(8,128)S(1)} %all_to_all.10.own_ref), channel_id=1, source_target_pairs={{0,32},{32,0},{1,33},{33,1},{2,34},{34,2},{3,35},{35,3},{4,36},{36... | collective-permute-start | bytes 4128776 | tf_op jit(solution)/shard_map/ppermute | solution.py:215
  83.0 0.1 pad_add_fusion.place
  83.1 2.7 %collective-permute-done.2.other_ref = f32[8,168,256]{2,1,0:T(8,128)S(1)} collective-permute-done((f32[8,168,256]{2,1,0:T(8,128)S(1)}, f32[8,168,256]{2,1,0:T(8,128)S(1)}, u32[]{:S(2)}, u32[]{:S(2)}) %collective-permute-start.2) | collective-permute-done | bytes 1376288 | tf_op jit(solution)/shard_map/ppermute | solution.py:215
  85.7 0.0 copy-done
  85.7 3.0 %own_rows.1 = (bf16[512,1024]{1,0:T(8,128)(2,1)S(1)}, bf16[512,1024]{1,0:T(8,128)(2,1)S(1)}, f32[2,8,256]{2,1,0:T(8,128)S(1)}) custom-call(s32[3]{0:T(128)S(1)} %pad_add_fusion.place, s32[32]{0:T(128)S(1)} %copy-done, f32[8,168,256]{2,1,0:T(8,128)S(1)} %all_to_all.10.own_ref, f32[8,168,256]{2,1,0:T(8,128)S(1)} %collective-permute-done.2.other_ref), custom_call_target="tpu_custom_call" | custom-call | tf_op jit(solution)/shard_map/own_rows/pallas_call | solution.py:148
  88.7 6.8 %all-gather.4.cloned.1.call-done = f32[32,4,40,256]{3,2,1,0:T(8,128)} async-done(((f32[4,4,40,256]{3,2,1,0:T(8,128)}), f32[32,4,40,256]{3,2,1,0:T(8,128)}) %all-gather.4.cloned.1.call-update) | async-done | bytes 5242896 | tf_op jit(solution)/shard_map/all_gather | solution.py:198
  95.5 0.0 copy-done.1
  95.5 0.0 copy-done.2
  95.5 8.5 %pairs.1 = (f32[8,2,64,256]{3,2,1,0:T(8,128)S(1)}, bf16[1024,1024]{1,0:T(8,128)(2,1)S(1)}, bf16[1024,1024]{1,0:T(8,128)(2,1)S(1)}, bf16[1024,512]{1,0:T(8,128)(2,1)S(1)}, bf16[1024,512]{1,0:T(8,128)(2,1)S(1)}) custom-call(s32[3]{0:T(128)S(1)} %pad_add_fusion.place, s32[32]{0:T(128)S(1)} %copy-done, f32[64]{0:T(128)S(1)} %copy-done.2, ...), custom_call_target="tpu_custom_call" | custom-call | tf_op jit(solution)/shard_map/pairs/pallas_call | solution.py:164
  104.1 2.6 %collective-permute-start.3 = (f32[8,2,64,256]{3,2,1,0:T(8,128)S(1)}, f32[8,2,64,256]{3,2,1,0:T(8,128)S(1)}, u32[]{:S(2)}, u32[]{:S(2)}) collective-permute-start(f32[8,2,64,256]{3,2,1,0:T(8,128)S(1)} %get-tuple-element.20), channel_id=1, source_target_pairs={{0,32},{32,0},{1,33},{33,1},{2,34},{34,2},{3,35},{35,3},{4,36},{36... | collective-permute-start | bytes 3145736 | tf_op jit(solution)/shard_map/ppermute | solution.py:220
  106.7 1.8 %own_core_rows.1 = f32[8,2,64,256]{3,2,1,0:T(8,128)S(1)} custom-call(bf16[1024,1024]{1,0:T(8,128)(2,1)S(1)} %get-tuple-element.16.w_hi, bf16[1024,1024]{1,0:T(8,128)(2,1)S(1)} %get-tuple-element.17.w_lo, bf16[1024,512]{1,0:T(8,128)(2,1)S(1)} %get-tuple-element.18.x_hi, bf16[1024,512]{1,0:T(8,128)(2,1)S(1)} %get-tuple-element.19.x_lo), custom_call_target="tpu_custom_call" | custom-call | flops 1610612736 | bytes 8388608 | tf_op jit(solution)/shard_map/own_core_rows/pallas_call | solution.py:180
  108.5 0.5 collective-permute-done.3
  108.9 0.1 add.45
  109.1 34.2 %all_to_all.11 = f32[8,2,64,256]{3,2,1,0:T(8,128)S(1)} all-to-all(f32[8,2,64,256]{3,2,1,0:T(8,128)S(1)} %add.45), channel_id=1, replica_groups=mesh['y'=8,'c'=2,'z'=8,'x'=4] {'y'}, dimensions={0} | all-to-all | bytes 2097152 | tf_op jit(solution)/shard_map/all_to_all | solution.py:222
  143.3 0.7 reduce_sum.9
  (2 shorter events, 0.0 us)
Async XLA Ops:
  6.5 28.8 %copy-start.3 = (s32[2,1,32]{2,1,0:T(1,128)S(1)}, s32[2,1,32]{2,1,0:T(1,128)}, u32[]{:S(2)}) copy-start(s32[2,1,32]{2,1,0:T(1,128)} %param.9) | copy-start | bytes 772
  6.5 89.0 %all-gather.4.cloned.1.call-start = ((), (), s32[]{:S(2)}) async-start(), calls=%async_computation.2 | async-start | bytes 5898240 | tf_op jit(solution)/shard_map/all_gather | solution.py:198
  21.2 14.4 %collective-permute-start = (f32[2,40,256]{2,1,0:T(8,128)S(1)}, f32[2,40,256]{2,1,0:T(8,128)S(1)}, u32[]{:S(2)}, u32[]{:S(2)}) collective-permute-start(f32[2,40,256]{2,1,0:T(8,128)S(1)} %get-tuple-element.21), channel_id=1, source_target_pairs={{0,0},{1,15},{2,14},{3,13},{4,12},{5,11},{6,10},{7,9},{8,8},{9,7},... | collective-permute-start | bytes 245768 | tf_op jit(solution)/shard_map/ppermute | solution.py:209
  23.4 17.1 %collective-permute-start.1 = (f32[2,40,256]{2,1,0:T(8,128)S(1)}, f32[2,40,256]{2,1,0:T(8,128)S(1)}, u32[]{:S(2)}, u32[]{:S(2)}) collective-permute-start(f32[2,40,256]{2,1,0:T(8,128)S(1)} %get-tuple-element.22), channel_id=1, source_target_pairs={{0,16},{1,31},{2,30},{3,29},{4,28},{5,27},{6,26},{7,25},{8,24},{9,... | collective-permute-start | bytes 245768 | tf_op jit(solution)/shard_map/ppermute | solution.py:209
  40.5 45.2 %copy-start = (s32[32]{0:T(128)S(1)}, s32[32]{0:T(128)}, u32[]{:S(2)}) copy-start(s32[32]{0:T(128)} %counts.3) | copy-start | bytes 388
  40.6 54.9 %copy-start.1 = (f32[256]{0:T(256)S(1)}, f32[256]{0:T(256)}, u32[]{:S(2)}) copy-start(f32[256]{0:T(256)} %param.8) | copy-start | bytes 3076
  40.6 54.9 %copy-start.2 = (f32[64]{0:T(128)S(1)}, f32[64]{0:T(128)}, u32[]{:S(2)}) copy-start(f32[64]{0:T(128)} %occ.1) | copy-start | bytes 772
  75.2 10.5 %collective-permute-start.2 = (f32[8,168,256]{2,1,0:T(8,128)S(1)}, f32[8,168,256]{2,1,0:T(8,128)S(1)}, u32[]{:S(2)}, u32[]{:S(2)}) collective-permute-start(f32[8,168,256]{2,1,0:T(8,128)S(1)} %all_to_all.10.own_ref), channel_id=1, source_target_pairs={{0,32},{32,0},{1,33},{33,1},{2,34},{34,2},{3,35},{35,3},{4,36},{36... | collective-permute-start | bytes 4128776 | tf_op jit(solution)/shard_map/ppermute | solution.py:215
  104.1 4.9 %collective-permute-start.3 = (f32[8,2,64,256]{3,2,1,0:T(8,128)S(1)}, f32[8,2,64,256]{3,2,1,0:T(8,128)S(1)}, u32[]{:S(2)}, u32[]{:S(2)}) collective-permute-start(f32[8,2,64,256]{3,2,1,0:T(8,128)S(1)} %get-tuple-element.20), channel_id=1, source_target_pairs={{0,32},{32,0},{1,33},{33,1},{2,34},{34,2},{3,35},{35,3},{4,36},{36... | collective-permute-start | bytes 3145736 | tf_op jit(solution)/shard_map/ppermute | solution.py:220
Sparse Core Ops, SparseCore 0:
  20.4 75.1 all-gather.3

commit v10 on v9

--- a/solution.py
+++ b/solution.py
@@ -92,14 +92,18 @@
 def pair_kernel(place, counts, occ, own_hi, own_lo, times, virt, wide_any,
                 theirs_ref, w_hi, w_lo, x_hi, x_lo, rows, dense, sems):
     core, u, grp = place[0], place[1], place[2]
-    row_copies = [pltpu.make_async_copy(wide_any.at[z], rows.at[z], sems.at[z]) for z in range(NZ)]
+    row_copies = [
+        pltpu.make_async_copy(wide_any.at[n // 2, pl.ds(n % 2 * 2, 2)], rows.at[n // 2, pl.ds(n % 2 * 2, 2)], sems.at[n])
+        for n in range(2 * NZ)
+    ]
     for copy in row_copies:
         copy.start()
 
     off = jnp.int32(0)
     for z in range(NZ):
-        row_copies[z].wait()
         for x in range(NX):
+            if x % 2 == 0:
+                row_copies[2 * z + x // 2].wait()
             for j in range(4):
                 put_rows(dense, off, slice(j * V, (j + 1) * V), rows[z, x, j])
             off = off + counts[z * NX + x]
@@ -169,7 +173,7 @@
         scratch_shapes=[
             pltpu.VMEM((NZ, NX, 4, CAP, V), jnp.float32),
             pltpu.VMEM((NAUX + PAD, 4 * V), jnp.float32),
-            pltpu.SemaphoreType.DMA((NZ,)),
+            pltpu.SemaphoreType.DMA((2 * NZ,)),
         ],
         compiler_params=pltpu.CompilerParams(vmem_limit_bytes=40 * MIB),
         name="pairs",

time: 151 us -> 151 us (level)
  no operation moved by 1% of the time
where the time goes in v10:
time: 151 us
  blocking collectives  81.5 us (54%)
  starting transfers between devices  24.5 us (16%)
  waiting for transfers between devices  14.8 us (10%)
  between operations  13.6 us (9%)
  Pallas kernels  13.3 us (9%)
  local copies, waits for them, and re-layouts  2.07 us (1%)
    all_to_all x1, blocking collectives, per_device(): own_pay = lax.all_to_all(sent, 'y', split_axis=0, concat_axis=0, tiled=True)  34.6 us
    all_to_all x1, blocking collectives, per_device(): pieces = lax.all_to_all(mine, 'y', split_axis=0, concat_axis=0, tiled=True)  34.2 us
    ppermute x2, starting transfers between devices, per_device(): got.append(lax.ppermute(piece, axes, perm).reshape(OCC_DEV * CAP, V))  14.1 us
    all_gather x1, blocking collectives, per_device(): wide_all = lax.all_gather(lax.all_gather(wide_part, 'x'), 'z')  12.7 us
    pallas_call x1, Pallas kernels, pairs(): pl.pallas_call(pair_kernel, out_shape=[part] + [wide_split] * 2 + [weight...  8.54 us
    ppermute x1, starting transfers between devices, per_device(): other_pay = lax.ppermute(own_pay, 'c', [(0, 1), (1, 0)])  7.78 us
    all_gather x1, waiting for transfers between devices, per_device(): wide_all = lax.all_gather(lax.all_gather(wide_part, 'x'), 'z')  6.82 us
    ppermute x2, waiting for transfers between devices, per_device(): got.append(lax.ppermute(piece, axes, perm).reshape(OCC_DEV * CAP, V))  4.84 us
  transfers between devices with their start and end apart: 5, of which 4 were waited for; matrix products, arithmetic and copies ran while one was open for 1% of the time, Pallas kernels for 3%

profile of v10, /device:TPU:1, one launch (start us, length us, event | category | flops | bytes accessed | tf_op | source)
XLA Modules:
  0.0 150.9 jit_solution(10396961526896594936)
XLA Ops:
  6.5 0.0 copy-start.3
  6.5 0.0 all-gather.4.cloned.1.call-start
  6.5 0.9 constant_dynamic-slice_fusion
  7.5 12.7 %all-gather = f32[16,40,256]{2,1,0:T(8,128)} all-gather(f32[4,40,256]{2,1,0:T(8,128)S(1)} %constant_dynamic-slice_fusion), channel_id=2, replica_groups=mesh['y'=8,'c'=2,'z'=8,'x'=4] {'x'}, dimensions={0}, use_global_device_ids=true | all-gather | bytes 819200 | tf_op jit(solution)/shard_map/all_gather | solution.py:202
  20.2 0.0 all-gather.4.cloned.1.call-update
  20.3 0.9 constant_dynamic-slice_fusion.2
  21.2 2.2 %collective-permute-start = (f32[2,40,256]{2,1,0:T(8,128)S(1)}, f32[2,40,256]{2,1,0:T(8,128)S(1)}, u32[]{:S(2)}, u32[]{:S(2)}) collective-permute-start(f32[2,40,256]{2,1,0:T(8,128)S(1)} %get-tuple-element.21), channel_id=1, source_target_pairs={{0,0},{1,15},{2,14},{3,13},{4,12},{5,11},{6,10},{7,9},{8,8},{9,7},... | collective-permute-start | bytes 245768 | tf_op jit(solution)/shard_map/ppermute | solution.py:213
  23.4 12.0 %collective-permute-start.1 = (f32[2,40,256]{2,1,0:T(8,128)S(1)}, f32[2,40,256]{2,1,0:T(8,128)S(1)}, u32[]{:S(2)}, u32[]{:S(2)}) collective-permute-start(f32[2,40,256]{2,1,0:T(8,128)S(1)} %get-tuple-element.22), channel_id=1, source_target_pairs={{0,16},{1,31},{2,30},{3,29},{4,28},{5,27},{6,26},{7,25},{8,24},{9,... | collective-permute-start | bytes 245768 | tf_op jit(solution)/shard_map/ppermute | solution.py:213
  35.4 0.0 copy-done.3
  35.4 0.2 convert_reduce_fusion
  35.6 0.1 broadcast_bitcast_fusion
  35.6 0.0 collective-permute-done
  35.6 4.8 %collective-permute-done.1 = f32[2,40,256]{2,1,0:T(8,128)S(1)} collective-permute-done((f32[2,40,256]{2,1,0:T(8,128)S(1)}, f32[2,40,256]{2,1,0:T(8,128)S(1)}, u32[]{:S(2)}, u32[]{:S(2)}) %collective-permute-start.1) | collective-permute-done | bytes 81952 | tf_op jit(solution)/shard_map/ppermute | solution.py:213
  40.5 0.0 copy-start
  40.5 0.1 broadcast_in_dim.19
  40.6 0.0 copy-start.1
  40.6 0.0 copy-start.2
  40.6 34.6 %all_to_all.10.own_ref = f32[8,168,256]{2,1,0:T(8,128)S(1)} all-to-all(f32[8,168,256]{2,1,0:T(8,128)S(1)} %broadcast_in_dim.19), channel_id=1, replica_groups=mesh['y'=8,'c'=2,'z'=8,'x'=4] {'y'}, dimensions={0} | all-to-all | bytes 2752512 | tf_op jit(solution)/shard_map/all_to_all | solution.py:218
  75.2 7.8 %collective-permute-start.2 = (f32[8,168,256]{2,1,0:T(8,128)S(1)}, f32[8,168,256]{2,1,0:T(8,128)S(1)}, u32[]{:S(2)}, u32[]{:S(2)}) collective-permute-start(f32[8,168,256]{2,1,0:T(8,128)S(1)} %all_to_all.10.own_ref), channel_id=1, source_target_pairs={{0,32},{32,0},{1,33},{33,1},{2,34},{34,2},{3,35},{35,3},{4,36},{36... | collective-permute-start | bytes 4128776 | tf_op jit(solution)/shard_map/ppermute | solution.py:219
  83.0 0.1 pad_add_fusion.place
  83.1 2.7 %collective-permute-done.2.other_ref = f32[8,168,256]{2,1,0:T(8,128)S(1)} collective-permute-done((f32[8,168,256]{2,1,0:T(8,128)S(1)}, f32[8,168,256]{2,1,0:T(8,128)S(1)}, u32[]{:S(2)}, u32[]{:S(2)}) %collective-permute-start.2) | collective-permute-done | bytes 1376288 | tf_op jit(solution)/shard_map/ppermute | solution.py:219
  85.7 0.0 copy-done
  85.7 3.0 %own_rows.1 = (bf16[512,1024]{1,0:T(8,128)(2,1)S(1)}, bf16[512,1024]{1,0:T(8,128)(2,1)S(1)}, f32[2,8,256]{2,1,0:T(8,128)S(1)}) custom-call(s32[3]{0:T(128)S(1)} %pad_add_fusion.place, s32[32]{0:T(128)S(1)} %copy-done, f32[8,168,256]{2,1,0:T(8,128)S(1)} %all_to_all.10.own_ref, f32[8,168,256]{2,1,0:T(8,128)S(1)} %collective-permute-done.2.other_ref), custom_call_target="tpu_custom_call" | custom-call | tf_op jit(solution)/shard_map/own_rows/pallas_call | solution.py:152
  88.7 6.8 %all-gather.4.cloned.1.call-done = f32[32,4,40,256]{3,2,1,0:T(8,128)} async-done(((f32[4,4,40,256]{3,2,1,0:T(8,128)}), f32[32,4,40,256]{3,2,1,0:T(8,128)}) %all-gather.4.cloned.1.call-update) | async-done | bytes 5242896 | tf_op jit(solution)/shard_map/all_gather | solution.py:202
  95.5 0.0 copy-done.1
  95.5 0.0 copy-done.2
  95.5 8.5 %pairs.1 = (f32[8,2,64,256]{3,2,1,0:T(8,128)S(1)}, bf16[1024,1024]{1,0:T(8,128)(2,1)S(1)}, bf16[1024,1024]{1,0:T(8,128)(2,1)S(1)}, bf16[1024,512]{1,0:T(8,128)(2,1)S(1)}, bf16[1024,512]{1,0:T(8,128)(2,1)S(1)}) custom-call(s32[3]{0:T(128)S(1)} %pad_add_fusion.place, s32[32]{0:T(128)S(1)} %copy-done, f32[64]{0:T(128)S(1)} %copy-done.2, ...), custom_call_target="tpu_custom_call" | custom-call | tf_op jit(solution)/shard_map/pairs/pallas_call | solution.py:168
  104.1 2.6 %collective-permute-start.3 = (f32[8,2,64,256]{3,2,1,0:T(8,128)S(1)}, f32[8,2,64,256]{3,2,1,0:T(8,128)S(1)}, u32[]{:S(2)}, u32[]{:S(2)}) collective-permute-start(f32[8,2,64,256]{3,2,1,0:T(8,128)S(1)} %get-tuple-element.20), channel_id=1, source_target_pairs={{0,32},{32,0},{1,33},{33,1},{2,34},{34,2},{3,35},{35,3},{4,36},{36... | collective-permute-start | bytes 3145736 | tf_op jit(solution)/shard_map/ppermute | solution.py:224
  106.7 1.8 %own_core_rows.1 = f32[8,2,64,256]{3,2,1,0:T(8,128)S(1)} custom-call(bf16[1024,1024]{1,0:T(8,128)(2,1)S(1)} %get-tuple-element.16.w_hi, bf16[1024,1024]{1,0:T(8,128)(2,1)S(1)} %get-tuple-element.17.w_lo, bf16[1024,512]{1,0:T(8,128)(2,1)S(1)} %get-tuple-element.18.x_hi, bf16[1024,512]{1,0:T(8,128)(2,1)S(1)} %get-tuple-element.19.x_lo), custom_call_target="tpu_custom_call" | custom-call | flops 1610612736 | bytes 8388608 | tf_op jit(solution)/shard_map/own_core_rows/pallas_call | solution.py:184
  108.5 0.5 collective-permute-done.3
  108.9 0.1 add.45
  109.1 34.2 %all_to_all.11 = f32[8,2,64,256]{3,2,1,0:T(8,128)S(1)} all-to-all(f32[8,2,64,256]{3,2,1,0:T(8,128)S(1)} %add.45), channel_id=1, replica_groups=mesh['y'=8,'c'=2,'z'=8,'x'=4] {'y'}, dimensions={0} | all-to-all | bytes 2097152 | tf_op jit(solution)/shard_map/all_to_all | solution.py:226
  143.3 0.7 reduce_sum.9
  (2 shorter events, 0.0 us)
Async XLA Ops:
  6.5 28.8 %copy-start.3 = (s32[2,1,32]{2,1,0:T(1,128)S(1)}, s32[2,1,32]{2,1,0:T(1,128)}, u32[]{:S(2)}) copy-start(s32[2,1,32]{2,1,0:T(1,128)} %param.9) | copy-start | bytes 772
  6.5 89.0 %all-gather.4.cloned.1.call-start = ((), (), s32[]{:S(2)}) async-start(), calls=%async_computation.2 | async-start | bytes 5898240 | tf_op jit(solution)/shard_map/all_gather | solution.py:202
  21.2 14.4 %collective-permute-start = (f32[2,40,256]{2,1,0:T(8,128)S(1)}, f32[2,40,256]{2,1,0:T(8,128)S(1)}, u32[]{:S(2)}, u32[]{:S(2)}) collective-permute-start(f32[2,40,256]{2,1,0:T(8,128)S(1)} %get-tuple-element.21), channel_id=1, source_target_pairs={{0,0},{1,15},{2,14},{3,13},{4,12},{5,11},{6,10},{7,9},{8,8},{9,7},... | collective-permute-start | bytes 245768 | tf_op jit(solution)/shard_map/ppermute | solution.py:213
  23.4 17.1 %collective-permute-start.1 = (f32[2,40,256]{2,1,0:T(8,128)S(1)}, f32[2,40,256]{2,1,0:T(8,128)S(1)}, u32[]{:S(2)}, u32[]{:S(2)}) collective-permute-start(f32[2,40,256]{2,1,0:T(8,128)S(1)} %get-tuple-element.22), channel_id=1, source_target_pairs={{0,16},{1,31},{2,30},{3,29},{4,28},{5,27},{6,26},{7,25},{8,24},{9,... | collective-permute-start | bytes 245768 | tf_op jit(solution)/shard_map/ppermute | solution.py:213
  40.5 45.2 %copy-start = (s32[32]{0:T(128)S(1)}, s32[32]{0:T(128)}, u32[]{:S(2)}) copy-start(s32[32]{0:T(128)} %counts.3) | copy-start | bytes 388
  40.6 54.9 %copy-start.1 = (f32[256]{0:T(256)S(1)}, f32[256]{0:T(256)}, u32[]{:S(2)}) copy-start(f32[256]{0:T(256)} %param.8) | copy-start | bytes 3076
  40.6 54.9 %copy-start.2 = (f32[64]{0:T(128)S(1)}, f32[64]{0:T(128)}, u32[]{:S(2)}) copy-start(f32[64]{0:T(128)} %occ.1) | copy-start | bytes 772
  75.2 10.5 %collective-permute-start.2 = (f32[8,168,256]{2,1,0:T(8,128)S(1)}, f32[8,168,256]{2,1,0:T(8,128)S(1)}, u32[]{:S(2)}, u32[]{:S(2)}) collective-permute-start(f32[8,168,256]{2,1,0:T(8,128)S(1)} %all_to_all.10.own_ref), channel_id=1, source_target_pairs={{0,32},{32,0},{1,33},{33,1},{2,34},{34,2},{3,35},{35,3},{4,36},{36... | collective-permute-start | bytes 4128776 | tf_op jit(solution)/shard_map/ppermute | solution.py:219
  104.1 4.9 %collective-permute-start.3 = (f32[8,2,64,256]{3,2,1,0:T(8,128)S(1)}, f32[8,2,64,256]{3,2,1,0:T(8,128)S(1)}, u32[]{:S(2)}, u32[]{:S(2)}) collective-permute-start(f32[8,2,64,256]{3,2,1,0:T(8,128)S(1)} %get-tuple-element.20), channel_id=1, source_target_pairs={{0,32},{32,0},{1,33},{33,1},{2,34},{34,2},{3,35},{35,3},{4,36},{36... | collective-permute-start | bytes 3145736 | tf_op jit(solution)/shard_map/ppermute | solution.py:224
Sparse Core Ops, SparseCore 0:
  20.4 75.1 all-gather.3
